TPU v7x, 256 devices: a whole 4x4x8 slice. The times are simulated.
256 devices in a mesh: gx: 32 (over z, x_lo, core), gy: 8 (over y, x_hi).
Axes of the slice: x: 4 (x_hi: 2, x_lo: 2; x = x_hi * 2 + x_lo), y: 4, z: 8, core: 2. Of those that a mesh axis runs over, the one named last changes fastest.
Arguments:
- density: float32 [256, 512, 256], P('gx', 'gy'), may hold values from 0 to 1
- sensitivity: float32 [256, 512, 256], P('gx', 'gy'), may hold values from -24 to 24
Outputs:
- projected: float32 [256, 512, 256], P('gx', 'gy')
- gradient: float32 [256, 512, 256], P('gx', 'gy')
All inputs are finite; a program needn't handle non-finite values.
Results may differ from a plain program's by a relative error of at most 0.000021.
Values sent between devices are 32-bit elements; how exact they have to be, the bound alone decides.
No kernel may reach another device: no remote copies, remote signals or barrier semaphores. Data moves between devices by JAX's collectives and lax.ppermute only.
A program may use at most 64 MiB of HBM per device.

v0:
```python
import jax
import jax.numpy as jnp
from jax import lax
from jax.sharding import PartitionSpec as P

RADIUS = 8


sharpness = 8.0
threshold = 0.5


def with_halo(cells, sides, width):
    for axis, dim in sides:
        count = lax.axis_size(axis)
        head = lax.slice_in_dim(cells, 0, width, axis=dim)
        tail = lax.slice_in_dim(cells, cells.shape[dim] - width, cells.shape[dim], axis=dim)
        cells = jnp.concatenate(
            [
                lax.ppermute(tail, axis, [(i, (i + 1) % count) for i in range(count)]),
                cells,
                lax.ppermute(head, axis, [((i + 1) % count, i) for i in range(count)]),
            ],
            axis=dim,
        )
    return cells


def tap_weight(offset):
    return (RADIUS + 1 - abs(offset)) / float((RADIUS + 1) ** 2)


def roll_pass(field, axis):
    total = jnp.zeros_like(field)
    for offset in range(-RADIUS, RADIUS + 1):
        total = total + tap_weight(offset) * jnp.roll(field, offset, axis)
    return total


def padded_pass(padded, axis, length):
    total = None
    for offset in range(-RADIUS, RADIUS + 1):
        start = RADIUS - offset
        piece = tap_weight(offset) * lax.slice_in_dim(padded, start, start + length, axis=axis)
        total = piece if total is None else total + piece
    return total


def smooth_field(field):
    first_len = field.shape[0]
    second_len = field.shape[1]
    along_z = roll_pass(field, 2)
    padded = with_halo(along_z, (("gx", 0),), RADIUS)
    along_x = padded_pass(padded, 0, first_len)
    padded_y = with_halo(along_x, (("gy", 1),), RADIUS)
    return padded_pass(padded_y, 1, second_len)


def flip_first(field):
    lines = lax.all_to_all(field, "gx", split_axis=1, concat_axis=0, tiled=True)
    averaged = 0.5 * (lines + lines[::-1, :, :])
    return lax.all_to_all(averaged, "gx", split_axis=0, concat_axis=1, tiled=True)


def flip_second(field):
    lines = lax.all_to_all(field, "gy", split_axis=0, concat_axis=1, tiled=True)
    averaged = 0.5 * (lines + lines[:, ::-1, :])
    return lax.all_to_all(averaged, "gy", split_axis=1, concat_axis=0, tiled=True)


def local(density, sensitivity):
    filtered = smooth_field(density)
    tilted = jnp.tanh(sharpness * (filtered - threshold))
    scale_sum = jnp.tanh(sharpness * threshold) + jnp.tanh(sharpness * (1.0 - threshold))
    projected = (jnp.tanh(sharpness * threshold) + tilted) / scale_sum
    chain = sensitivity * (sharpness * (1.0 - tilted * tilted) / scale_sum)
    partial_grad = smooth_field(chain)
    half_sym = flip_first(partial_grad)
    gradient = flip_second(half_sym)
    return (projected, gradient)


def solution(mesh):
    placed = (P("gx", "gy", None), P("gx", "gy", None))
    return jax.shard_map(
        local,
        mesh=mesh,
        in_specs=placed,
        out_specs=(P("gx", "gy", None), P("gx", "gy", None)),
        check_vma=False,
    )
```

profile of v0, /device:TPU:1, one launch (start us, length us, event | category | flops | bytes accessed | tf_op | source)
XLA Modules:
  0.0 152.5 jit_solution(1106039317893547408)
XLA Ops:
  0.6 1.2 fusion.234
  7.2 0.3 copy.157
  7.5 0.3 copy.128
  7.8 0.3 copy.155
  8.1 0.3 copy.130
  8.4 0.3 copy.153
  8.7 0.3 copy.132
  9.0 0.3 copy.151
  9.4 0.3 copy.134
  9.7 0.3 copy.149
  10.0 0.3 copy.136
  10.3 0.3 copy.147
  10.6 0.3 copy.138
  10.9 0.3 copy.145
  11.2 0.3 copy.140
  11.6 0.3 copy.143
  11.9 0.3 copy.142
  12.2 2.4 %fusion.194 = f32[8,64,256]{2,0,1:T(8,128)S(1)} fusion(f32[8,64,8]{2,0,1:T(8,128)S(1)} %copy.127, f32[8,64,248]{2,0,1:T(8,128)S(1)} %copy.128, f32[8,64,7]{2,0,1:T(8,128)S(1)} %copy.129, f32[8,64,249]{2,0,1:T(8,128)S(1)} %copy.130, f32[8,64,6]{2,0,1:T(8,128)S(1)} %copy.131, f32[8,64,250]{2,0,1:T(8,128)S(1)} %copy.132, f32[8,64,5]{2,0,1:T(8,128)S(1)} %copy.133, ...), kind=kLoop, calls=%fused_computation.307 | loop fusion | flops 6422528 | bytes 9437184 | tf_op jit(solution)/shard_map/add | solution.py:36
  14.6 2.7 %collective-permute-start.1 = (f32[8,64,256]{2,0,1:T(8,128)S(1)}, f32[8,64,256]{2,0,1:T(8,128)S(1)}, u32[]{:S(2)}, u32[]{:S(2)}) collective-permute-start(f32[8,64,256]{2,0,1:T(8,128)S(1)} %fusion.194), channel_id=1, source_target_pairs={{0,8},{8,16},{16,24},{24,32},{32,40},{40,48},{48,56},{56,64},{64,7... | collective-permute-start | bytes 1572872 | tf_op jit(solution)/shard_map/ppermute | solution.py:20
  17.2 0.9 collective-permute-start
  18.1 10.8 %collective-permute-done.1 = f32[8,64,256]{2,0,1:T(8,128)S(1)} collective-permute-done((f32[8,64,256]{2,0,1:T(8,128)S(1)}, f32[8,64,256]{2,0,1:T(8,128)S(1)}, u32[]{:S(2)}, u32[]{:S(2)}) %collective-permute-start.1) | collective-permute-done | bytes 524320 | tf_op jit(solution)/shard_map/ppermute | solution.py:20
  29.0 2.5 %collective-permute-done = f32[8,64,256]{2,0,1:T(8,128)S(1)} collective-permute-done((f32[8,64,256]{2,0,1:T(8,128)S(1)}, f32[8,64,256]{2,0,1:T(8,128)S(1)}, u32[]{:S(2)}, u32[]{:S(2)}) %collective-permute-start) | collective-permute-done | bytes 524320 | tf_op jit(solution)/shard_map/ppermute | solution.py:22
  31.5 1.8 %fusion.135 = f32[8,64,256]{2,0,1:T(8,128)S(1)} fusion(f32[8,64,256]{2,0,1:T(8,128)S(1)} %collective-permute-done.1, f32[8,64,256]{2,0,1:T(8,128)S(1)} %fusion.194, f32[8,64,256]{2,0,1:T(8,128)S(1)} %collective-permute-done), kind=kLoop, calls=%fused_computation.239 | loop fusion | flops 6160384 | bytes 2097152 | tf_op jit(solution)/shard_map/add | solution.py:45
  33.2 5.0 %collective-permute-start.2 = (f32[8,8,256]{2,0,1:T(8,128)S(1)}, f32[8,8,256]{2,0,1:T(8,128)S(1)}, u32[]{:S(2)}, u32[]{:S(2)}) collective-permute-start(f32[8,8,256]{2,0,1:T(8,128)S(1)} %get-tuple-element.44), channel_id=1, source_target_pairs={{1,0},{2,1},{3,2},{4,3},{5,4},{6,5},{7,6},{0,7},{9,8},{10,9},{11,1... | collective-permute-start | bytes 196616 | tf_op jit(solution)/shard_map/ppermute | solution.py:22
  38.2 1.3 collective-permute-done.2
  39.6 5.4 %collective-permute-done.3 = f32[8,8,256]{2,0,1:T(8,128)S(1)} collective-permute-done((f32[8,8,256]{2,0,1:T(8,128)S(1)}, f32[8,8,256]{2,0,1:T(8,128)S(1)}, u32[]{:S(2)}, u32[]{:S(2)}) %collective-permute-start.3) | collective-permute-done | bytes 65568 | tf_op jit(solution)/shard_map/ppermute | solution.py:20
  45.0 1.3 copy_multiply_fusion
  49.0 1.7 %fusion.210 = f32[8,64,256]{2,0,1:T(8,128)S(1)} fusion(f32[8,64,8]{2,0,1:T(8,128)S(1)} %get-tuple-element.13, f32[8,64,248]{2,0,1:T(8,128)S(1)} %get-tuple-element.15, f32[8,64,7]{2,0,1:T(8,128)S(1)} %get-tuple-element.17, f32[8,64,249]{2,0,1:T(8,128)S(1)} %get-tuple-element.19, f32[8,64,6]{2,0,1:T(8,128)S(1)} %get-tuple-element.21, ...), kind=kLoop, calls=%fused_computation.339 | loop fusion | flops 6422528 | bytes 9437184 | tf_op jit(solution)/shard_map/add | solution.py:36
  50.7 0.9 collective-permute-start.5
  51.6 11.7 %collective-permute-done.5 = f32[8,64,256]{2,0,1:T(8,128)S(1)} collective-permute-done((f32[8,64,256]{2,0,1:T(8,128)S(1)}, f32[8,64,256]{2,0,1:T(8,128)S(1)}, u32[]{:S(2)}, u32[]{:S(2)}) %collective-permute-start.5) | collective-permute-done | bytes 524320 | tf_op jit(solution)/shard_map/ppermute | solution.py:20
  63.3 3.2 %collective-permute-done.4 = f32[8,64,256]{2,0,1:T(8,128)S(1)} collective-permute-done((f32[8,64,256]{2,0,1:T(8,128)S(1)}, f32[8,64,256]{2,0,1:T(8,128)S(1)}, u32[]{:S(2)}, u32[]{:S(2)}) %collective-permute-start.4) | collective-permute-done | bytes 524320 | tf_op jit(solution)/shard_map/ppermute | solution.py:22
  66.5 1.8 %fusion.95 = f32[8,64,256]{2,0,1:T(8,128)S(1)} fusion(f32[8,64,256]{2,0,1:T(8,128)S(1)} %collective-permute-done.5, f32[8,64,256]{2,0,1:T(8,128)S(1)} %fusion.210, f32[8,64,256]{2,0,1:T(8,128)S(1)} %collective-permute-done.4), kind=kLoop, calls=%fused_computation.199 | loop fusion | flops 6160384 | bytes 2097152 | tf_op jit(solution)/shard_map/add | solution.py:45
  68.3 0.3 collective-permute-start.6
  68.6 3.0 %collective-permute-start.7 = (f32[8,8,256]{2,0,1:T(8,128)S(1)}, f32[8,8,256]{2,0,1:T(8,128)S(1)}, u32[]{:S(2)}, u32[]{:S(2)}) collective-permute-start(f32[8,8,256]{2,0,1:T(8,128)S(1)} %get-tuple-element.11), channel_id=1, source_target_pairs={{0,1},{1,2},{2,3},{3,4},{4,5},{5,6},{6,7},{7,0},{8,9},{9,10},{10,1... | collective-permute-start | bytes 196616 | tf_op jit(solution)/shard_map/ppermute | solution.py:20
  71.5 1.6 %collective-permute-done.6 = f32[8,8,256]{2,0,1:T(8,128)S(1)} collective-permute-done((f32[8,8,256]{2,0,1:T(8,128)S(1)}, f32[8,8,256]{2,0,1:T(8,128)S(1)}, u32[]{:S(2)}, u32[]{:S(2)}) %collective-permute-start.6) | collective-permute-done | bytes 65568 | tf_op jit(solution)/shard_map/ppermute | solution.py:22
  73.2 2.2 %collective-permute-done.7 = f32[8,8,256]{2,0,1:T(8,128)S(1)} collective-permute-done((f32[8,8,256]{2,0,1:T(8,128)S(1)}, f32[8,8,256]{2,0,1:T(8,128)S(1)}, u32[]{:S(2)}, u32[]{:S(2)}) %collective-permute-start.7) | collective-permute-done | bytes 65568 | tf_op jit(solution)/shard_map/ppermute | solution.py:20
  75.4 0.9 fusion.3
  76.3 25.9 %all_to_all.60 = f32[8,64,256]{2,0,1:T(8,128)S(1)} all-to-all(f32[8,64,256]{2,0,1:T(8,128)S(1)} %fusion.3), channel_id=1, replica_groups=mesh['gx'=32,'gy'=8] {'gx'}, dimensions={1} | all-to-all | bytes 1048576 | tf_op jit(solution)/shard_map/all_to_all | solution.py:60
  102.2 0.3 rev.6
  102.6 0.4 copy.114
  103.0 21.2 %all_to_all.61 = f32[256,2,256]{2,1,0:T(2,128)S(1)} all-to-all(f32[256,2,256]{2,1,0:T(2,128)S(1)} %copy.114), channel_id=1, replica_groups=mesh['gx'=32,'gy'=8] {'gx'}, dimensions={0} | all-to-all | bytes 1048576 | tf_op jit(solution)/shard_map/all_to_all | solution.py:62
  124.5 12.7 %all_to_all.62 = f32[8,64,256]{2,1,0:T(8,128)S(1)} all-to-all(f32[8,64,256]{2,1,0:T(8,128)S(1)} %copy.117), channel_id=1, replica_groups=mesh['gx'=32,'gy'=8] {'gy'}, dimensions={0} | all-to-all | bytes 1048576 | tf_op jit(solution)/shard_map/all_to_all | solution.py:66
  137.3 0.2 rev.7
  137.6 1.3 copy.118
  138.9 3.5 %all-to-all-start.3 = ((f32[1,512,256]{2,0,1:T(1,128)}), f32[1,512,256]{2,0,1:T(1,128)S(1)}, u32[]{:S(2)}, u32[]{:S(2)}) async-start(f32[1,512,256]{2,0,1:T(1,128)} %copy.118), calls=%async_computation.3 | async-start | bytes 1048576 | tf_op jit(solution)/shard_map/all_to_all | solution.py:68
  142.5 1.0 copy.119
  143.5 8.2 %all-to-all-done.3 = f32[1,512,256]{2,0,1:T(1,128)S(1)} async-done(((f32[1,512,256]{2,0,1:T(1,128)}), f32[1,512,256]{2,0,1:T(1,128)S(1)}, u32[]{:S(2)}, u32[]{:S(2)}) %all-to-all-start.3) | async-done | bytes 524320 | tf_op jit(solution)/shard_map/all_to_all | solution.py:68
  151.6 0.8 copy.120
  (62 shorter events, 8.4 us)
Async XLA Ops:
  0.6 1.2 copy-start
  14.6 14.4 %collective-permute-start.1 = (f32[8,64,256]{2,0,1:T(8,128)S(1)}, f32[8,64,256]{2,0,1:T(8,128)S(1)}, u32[]{:S(2)}, u32[]{:S(2)}) collective-permute-start(f32[8,64,256]{2,0,1:T(8,128)S(1)} %fusion.194), channel_id=1, source_target_pairs={{0,8},{8,16},{16,24},{24,32},{32,40},{40,48},{48,56},{56,64},{64,7... | collective-permute-start | bytes 1572872 | tf_op jit(solution)/shard_map/ppermute | solution.py:20
  17.2 14.2 %collective-permute-start = (f32[8,64,256]{2,0,1:T(8,128)S(1)}, f32[8,64,256]{2,0,1:T(8,128)S(1)}, u32[]{:S(2)}, u32[]{:S(2)}) collective-permute-start(f32[8,64,256]{2,0,1:T(8,128)S(1)} %fusion.194), channel_id=1, source_target_pairs={{8,0},{16,8},{24,16},{32,24},{40,32},{48,40},{56,48},{64,56},{72,6... | collective-permute-start | bytes 1572872 | tf_op jit(solution)/shard_map/ppermute | solution.py:22
  31.5 13.5 %copy-start.1 = (f32[8,64,256]{2,1,0:T(8,128)S(1)}, f32[8,64,256]{2,1,0:T(8,128)}, u32[]{:S(2)}) copy-start(f32[8,64,256]{2,1,0:T(8,128)} %param.3) | copy-start | bytes 1572868
  33.2 6.3 %collective-permute-start.2 = (f32[8,8,256]{2,0,1:T(8,128)S(1)}, f32[8,8,256]{2,0,1:T(8,128)S(1)}, u32[]{:S(2)}, u32[]{:S(2)}) collective-permute-start(f32[8,8,256]{2,0,1:T(8,128)S(1)} %get-tuple-element.44), channel_id=1, source_target_pairs={{1,0},{2,1},{3,2},{4,3},{5,4},{6,5},{7,6},{0,7},{9,8},{10,9},{11,1... | collective-permute-start | bytes 196616 | tf_op jit(solution)/shard_map/ppermute | solution.py:22
  38.2 6.7 %collective-permute-start.3 = (f32[8,8,256]{2,0,1:T(8,128)S(1)}, f32[8,8,256]{2,0,1:T(8,128)S(1)}, u32[]{:S(2)}, u32[]{:S(2)}) collective-permute-start(f32[8,8,256]{2,0,1:T(8,128)S(1)} %get-tuple-element.45), channel_id=1, source_target_pairs={{0,1},{1,2},{2,3},{3,4},{4,5},{5,6},{6,7},{7,0},{8,9},{9,10},{10,1... | collective-permute-start | bytes 196616 | tf_op jit(solution)/shard_map/ppermute | solution.py:20
  50.7 12.6 %collective-permute-start.5 = (f32[8,64,256]{2,0,1:T(8,128)S(1)}, f32[8,64,256]{2,0,1:T(8,128)S(1)}, u32[]{:S(2)}, u32[]{:S(2)}) collective-permute-start(f32[8,64,256]{2,0,1:T(8,128)S(1)} %fusion.210), channel_id=1, source_target_pairs={{0,8},{8,16},{16,24},{24,32},{32,40},{40,48},{48,56},{56,64},{64,7... | collective-permute-start | bytes 1572872 | tf_op jit(solution)/shard_map/ppermute | solution.py:20
  51.6 14.9 %collective-permute-start.4 = (f32[8,64,256]{2,0,1:T(8,128)S(1)}, f32[8,64,256]{2,0,1:T(8,128)S(1)}, u32[]{:S(2)}, u32[]{:S(2)}) collective-permute-start(f32[8,64,256]{2,0,1:T(8,128)S(1)} %fusion.210), channel_id=1, source_target_pairs={{8,0},{16,8},{24,16},{32,24},{40,32},{48,40},{56,48},{64,56},{72,6... | collective-permute-start | bytes 1572872 | tf_op jit(solution)/shard_map/ppermute | solution.py:22
  68.3 4.9 %collective-permute-start.6 = (f32[8,8,256]{2,0,1:T(8,128)S(1)}, f32[8,8,256]{2,0,1:T(8,128)S(1)}, u32[]{:S(2)}, u32[]{:S(2)}) collective-permute-start(f32[8,8,256]{2,0,1:T(8,128)S(1)} %get-tuple-element.10), channel_id=1, source_target_pairs={{1,0},{2,1},{3,2},{4,3},{5,4},{6,5},{7,6},{0,7},{9,8},{10,9},{11,1... | collective-permute-start | bytes 196616 | tf_op jit(solution)/shard_map/ppermute | solution.py:22
  68.6 6.8 %collective-permute-start.7 = (f32[8,8,256]{2,0,1:T(8,128)S(1)}, f32[8,8,256]{2,0,1:T(8,128)S(1)}, u32[]{:S(2)}, u32[]{:S(2)}) collective-permute-start(f32[8,8,256]{2,0,1:T(8,128)S(1)} %get-tuple-element.11), channel_id=1, source_target_pairs={{0,1},{1,2},{2,3},{3,4},{4,5},{5,6},{6,7},{7,0},{8,9},{9,10},{10,1... | collective-permute-start | bytes 196616 | tf_op jit(solution)/shard_map/ppermute | solution.py:20
  138.9 12.7 %all-to-all-start.3 = ((f32[1,512,256]{2,0,1:T(1,128)}), f32[1,512,256]{2,0,1:T(1,128)S(1)}, u32[]{:S(2)}, u32[]{:S(2)}) async-start(f32[1,512,256]{2,0,1:T(1,128)} %copy.118), calls=%async_computation.3 | async-start | bytes 1048576 | tf_op jit(solution)/shard_map/all_to_all | solution.py:68
where the time goes:
time: 154 us; the launch traced here: 152 us
  blocking collectives  59.9 us (39%)
  waiting for transfers between devices  46.9 us (30%)
  local copies, waits for them, and re-layouts  18.3 us (12%)
  starting transfers between devices  16.2 us (11%)
  other arithmetic  10 us (6%)
    ppermute x4, waiting for transfers between devices, with_halo(): lax.ppermute(tail, axis, [(i, (i + 1) % count) for i in range(count)])  30.2 us
    all_to_all x1, blocking collectives, flip_first(): lines = lax.all_to_all(field, 'gx', split_axis=1, concat_axis=0, tiled=True)  25.9 us
    all_to_all x1, blocking collectives, flip_first(): lax.all_to_all(averaged, 'gx', split_axis=0, concat_axis=1, tiled=True)  21.2 us
    all_to_all x1, blocking collectives, flip_second(): lines = lax.all_to_all(field, 'gy', split_axis=0, concat_axis=1, tiled=True)  12.7 us
    unnamed x38, local copies, waits for them, and re-layouts  9.25 us
    ppermute x4, waiting for transfers between devices, with_halo(): lax.ppermute(head, axis, [((i + 1) % count, i) for i in range(count)])  8.61 us
    all_to_all x1, waiting for transfers between devices, flip_second(): lax.all_to_all(averaged, 'gy', split_axis=1, concat_axis=0, tiled=True)  8.17 us
    ppermute x4, starting transfers between devices, with_halo(): lax.ppermute(tail, axis, [(i, (i + 1) % count) for i in range(count)])  6.54 us
  transfers between devices with their start and end apart: 9, of which 9 were waited for; matrix products, arithmetic and copies ran while one was open for 1% of the time, Pallas kernels for 0%

commit v1 on v0

v1 whole, which is shorter than its diff:
```python
import math

import jax
import jax.numpy as jnp
from jax import lax
from jax.experimental import pallas as pl
from jax.experimental.pallas import tpu as pltpu
from jax.sharding import PartitionSpec as P

RADIUS = 8
WIDTH = RADIUS + 1
SHARPNESS = 8.0
THRESHOLD = 0.5
TANH_LOW = math.tanh(SHARPNESS * THRESHOLD)
SCALE_SUM = TANH_LOW + math.tanh(SHARPNESS * (1.0 - THRESHOLD))
WEIGHT = 1.0 / float(WIDTH**6)
HALF = 64
F32 = jnp.float32


def run(body, outs, args, scratch=()):
    return pl.pallas_call(
        body,
        out_shape=[jax.ShapeDtypeStruct(shape, F32) for shape in outs],
        in_specs=[pl.BlockSpec(memory_space=pltpu.VMEM)] * len(args),
        out_specs=[pl.BlockSpec(memory_space=pltpu.VMEM)] * len(outs),
        scratch_shapes=list(scratch),
        compiler_params=pltpu.CompilerParams(vmem_limit_bytes=24 * 1024 * 1024),
    )(*args)


def box_list(items):
    pairs = [a + b for a, b in zip(items, items[1:])]
    fours = [a + b for a, b in zip(pairs, pairs[2:])]
    eights = [a + b for a, b in zip(fours, fours[4:])]
    return [a + b for a, b in zip(eights, items[8:])]


def cone_list(items):
    return box_list(box_list(items))


def ahead(field, step, axis):
    return pltpu.roll(field, field.shape[axis] - step, axis)


def box_rows(field, axis):
    pairs = field + ahead(field, 1, axis)
    fours = pairs + ahead(pairs, 2, axis)
    eights = fours + ahead(fours, 4, axis)
    return eights + ahead(field, 8, axis)


def cone_rows(field, axis):
    return box_rows(box_rows(field, axis), axis)


def reverse_eights(field, axis):
    size = field.shape[axis]
    row = lax.broadcasted_iota(jnp.int32, field.shape, axis)
    for bit in (1, 2, 4):
        field = jnp.where(
            (row & bit) == 0, pltpu.roll(field, size - bit, axis), pltpu.roll(field, bit, axis)
        )
    return field


def swap_halves(field):
    return pltpu.roll(field, HALF, field.ndim - 1)


def flip_planes(field):
    return jnp.stack([field[p] for p in reversed(range(field.shape[0]))])


def flip_rows(field):
    field = reverse_eights(field, 1)
    rows = field.shape[1]
    groups = [field[:, r : r + 8] for r in range(0, rows, 8)]
    return swap_halves(jnp.concatenate(groups[::-1], axis=1))


def first_lanes(shape):
    return lax.broadcasted_iota(jnp.int32, shape, len(shape) - 1) < HALF


def z_pass(field):
    count = field.shape[-1]
    row = lax.broadcasted_iota(jnp.int32, (count, count), 0)
    col = lax.broadcasted_iota(jnp.int32, (count, count), 1)
    gap = jnp.abs(row - col)
    taps = jnp.maximum(WIDTH - jnp.minimum(gap, count - gap), 0).astype(F32).astype(jnp.bfloat16)
    high = field.astype(jnp.bfloat16)
    rest = field - high.astype(F32)
    middle = rest.astype(jnp.bfloat16)
    low = (rest - middle.astype(F32)).astype(jnp.bfloat16)
    total = jnp.dot(low, taps, preferred_element_type=F32)
    total = total + jnp.dot(middle, taps, preferred_element_type=F32)
    return total + jnp.dot(high, taps, preferred_element_type=F32)


def solution(mesh):
    nx, ny = mesh.shape["gx"], mesh.shape["gy"]
    hx, hy = nx // 2, ny // 2

    def project_kernel(
        own, left, right, low, high, corner_l, corner_r, sens, projected, keep, to_x, to_y, to_xy, xs, ys
    ):
        planes, rows, depth = own.shape
        for lane in range(0, depth, 128):
            lanes = slice(lane, lane + 128)
            for group in range(rows // 8 + 2):
                if group == 0:
                    parts = ((corner_l, 0), (low, 0), (corner_r, 0))
                elif group == rows // 8 + 1:
                    parts = ((corner_l, 8), (high, 0), (corner_r, 8))
                else:
                    start = 8 * (group - 1)
                    parts = ((left, start), (own, start), (right, start))
                items = [ref[p, at : at + 8, lanes] for ref, at in parts for p in range(planes)]
                for p, item in enumerate(cone_list(items)):
                    xs[p, 8 * group : 8 * group + 8, lanes] = item
        for p in range(planes):
            ys[p * rows : (p + 1) * rows, :] = cone_rows(xs[p], 0)[:rows]
        filtered = z_pass(ys[...]) * WEIGHT
        tilted = jnp.tanh(SHARPNESS * (filtered - THRESHOLD))
        projected[...] = ((TANH_LOW + tilted) * (1.0 / SCALE_SUM)).reshape(planes, rows, depth)
        slope = (1.0 - tilted * tilted) * (SHARPNESS / SCALE_SUM)
        chain = sens[...] * slope.reshape(planes, rows, depth)
        upper_x = lax.axis_index("gx") >= hx
        upper_y = lax.axis_index("gy") >= hy
        near = jnp.where(upper_x, chain[:, :, 128:], chain[:, :, :128])
        far = jnp.where(upper_x, chain[:, :, :128], chain[:, :, 128:])
        for field, even_out, odd_out in ((near, keep, to_y), (far, to_x, to_xy)):
            top, bottom = field[:, : rows // 2], field[:, rows // 2 :]
            mask = first_lanes(top.shape)
            even = jnp.where(mask, top, swap_halves(bottom))
            odd = jnp.where(mask, swap_halves(top), bottom)
            even_out[...] = jnp.where(upper_y, odd, even)
            odd_out[...] = jnp.where(upper_y, even, odd)

    def sum_kernel(keep, from_x, from_y, from_xy, total, head, tail):
        other = flip_rows(from_y[...] + flip_planes(from_xy[...]))
        result = keep[...] + flip_planes(from_x[...]) + other
        total[...] = result
        head[...] = result[:, :8]
        tail[...] = result[:, -8:]

    def rows_kernel(field, from_low, from_high, out):
        own = field[...]
        rows = own.shape[1]
        head, tail = own[:, :8], own[:, -8:]
        mask = first_lanes(head.shape)
        place = lax.rem(lax.axis_index("gy"), hy)
        low = jnp.where(place == 0, reverse_eights(head, 1), swap_halves(from_low[...]))
        high = jnp.where(place == hy - 1, reverse_eights(tail, 1), swap_halves(from_high[...]))
        above = jnp.where(mask, low, swap_halves(tail))
        below = jnp.where(mask, swap_halves(head), high)
        padded = jnp.concatenate([above, own, below], axis=1)
        for p in range(own.shape[0]):
            out[p] = cone_rows(padded[p], 0)[:rows]

    def planes_kernel(own, left, right, out):
        planes, rows, _ = own.shape
        place = lax.rem(lax.axis_index("gx"), hx)
        first, last = place == 0, place == hx - 1
        for group in range(0, rows, 8):
            mine = [own[p, group : group + 8] for p in range(planes)]
            before = [jnp.where(first, mine[-1 - p], left[p, group : group + 8]) for p in range(planes)]
            after = [jnp.where(last, mine[-1 - p], right[p, group : group + 8]) for p in range(planes)]
            for p, item in enumerate(cone_list(before + mine + after)):
                out[p, group : group + 8] = item

    def finish_kernel(own, from_x, from_y, from_xy, gradient, flat):
        planes, rows, depth = gradient.shape
        upper_x = lax.axis_index("gx") >= hx
        upper_y = lax.axis_index("gy") >= hy
        near_own, near_y = own[...], flip_rows(from_y[...])
        far_x, far_xy = flip_planes(from_x[...]), flip_rows(flip_planes(from_xy[...]))
        sides = []
        for mine, other in ((near_own, near_y), (far_x, far_xy)):
            even, odd = jnp.where(upper_y, other, mine), jnp.where(upper_y, mine, other)
            mask = first_lanes(even.shape)
            top = jnp.where(mask, even, swap_halves(odd))
            bottom = jnp.where(mask, swap_halves(even), odd)
            sides.append(jnp.concatenate([top, bottom], axis=1).reshape(planes * rows, 128))
        near, far = sides
        flat[:, :128] = jnp.where(upper_x, far, near)
        flat[:, 128:] = jnp.where(upper_x, near, far)
        gradient[...] = (z_pass(flat[...]) * (0.25 * WEIGHT)).reshape(planes, rows, depth)

    both = [(i, j) for i in range(nx) for j in range(ny)]
    up_x = [(i, (i + 1) % nx) for i in range(nx)]
    down_x = [(b, a) for a, b in up_x]
    up_y = [(j, (j + 1) % ny) for j in range(ny)]
    down_y = [(b, a) for a, b in up_y]
    fold_up_x = [(a, b) for a, b in up_x if b % hx != 0]
    fold_down_x = [(b, a) for a, b in fold_up_x]
    fold_up_y = [(a, b) for a, b in up_y if b % hy != 0]
    fold_down_y = [(b, a) for a, b in fold_up_y]
    mirror_x = [(i, nx - 1 - i) for i in range(nx)]
    mirror_y = [(j, ny - 1 - j) for j in range(ny)]
    mirror_xy = [(i * ny + j, (nx - 1 - i) * ny + ny - 1 - j) for i, j in both]

    def mirrors(to_x, to_y, to_xy):
        return (
            lax.ppermute(to_x, "gx", mirror_x),
            lax.ppermute(to_y, "gy", mirror_y),
            lax.ppermute(to_xy, ("gx", "gy"), mirror_xy),
        )

    def local(density, sensitivity):
        block = density.shape
        planes, rows, depth = block
        packed = (planes, rows // 2, 128)
        edge = (planes, 8, 128)
        low = lax.ppermute(density[:, -8:], "gy", up_y)
        high = lax.ppermute(density[:, :8], "gy", down_y)
        left = lax.ppermute(density, "gx", up_x)
        right = lax.ppermute(density, "gx", down_x)
        edges = jnp.concatenate([low, high], axis=1)
        corner_l = lax.ppermute(edges, "gx", up_x)
        corner_r = lax.ppermute(edges, "gx", down_x)
        projected, keep, to_x, to_y, to_xy = run(
            project_kernel,
            [block, packed, packed, packed, packed],
            (density, left, right, low, high, corner_l, corner_r, sensitivity),
            (pltpu.VMEM((planes, rows + 16, depth), F32), pltpu.VMEM((planes * rows, depth), F32)),
        )
        total, head, tail = run(sum_kernel, [packed, edge, edge], (keep, *mirrors(to_x, to_y, to_xy)))
        from_low = lax.ppermute(tail, "gy", fold_up_y)
        from_high = lax.ppermute(head, "gy", fold_down_y)
        (smooth,) = run(rows_kernel, [packed], (total, from_low, from_high))
        before = lax.ppermute(smooth, "gx", fold_up_x)
        after = lax.ppermute(smooth, "gx", fold_down_x)
        (quarter,) = run(planes_kernel, [packed], (smooth, before, after))
        (gradient,) = run(
            finish_kernel,
            [block],
            (quarter, *mirrors(quarter, quarter, quarter)),
            (pltpu.VMEM((planes * rows, depth), F32),),
        )
        return projected, gradient

    return jax.shard_map(
        local,
        mesh=mesh,
        in_specs=(P("gx", "gy", None), P("gx", "gy", None)),
        out_specs=(P("gx", "gy", None), P("gx", "gy", None)),
        check_vma=False,
    )
```

time: 154 us -> 87.6 us (0.57)
  blocking collectives: 59.9 us -> 0 us
  starting transfers between devices: 16.2 us -> 43.2 us
  local copies, waits for them, and re-layouts: 18.3 us -> 1.94 us
  other arithmetic: 10 us -> 0 us
  waiting for transfers between devices: 46.9 us -> 37.4 us
  Pallas kernels: 0 us -> 3.86 us
    all_to_all x3 -> x0, blocking collectives: 59.9 us -> none  [the longest x1 25.9 us: flip_first(): lines = lax.all_to_all(field, 'gx', split_axis=1, concat_axis=0, tiled=True)]
    ppermute x8 -> x16, starting transfers between devices: 12.7 us -> 43.2 us  [the longest x2 9.33 us: mirrors(): lax.ppermute(to_x, 'gx', mirror_x)]
    add x5 -> x0, other arithmetic: 8.53 us -> none  [the longest x3 4.46 us: padded_pass(): total = piece if total is None else total + piece]
    unnamed x38 -> x5, local copies, waits for them, and re-layouts: 9.25 us -> 1.05 us
    all_to_all x1 -> x0, waiting for transfers between devices: 8.17 us -> none  [flip_second(): lax.all_to_all(averaged, 'gy', split_axis=1, concat_axis=0, tiled=True)]
    slice x34 -> x1, local copies, waits for them, and re-layouts: 6.56 us -> 0.88 us  [local(): high = lax.ppermute(density[:, :8], 'gy', down_y)]
    pallas_call x0 -> x5, Pallas kernels: none -> 3.86 us  [run(): pl.pallas_call(body, out_shape=[jax.ShapeDtypeStruct(shape, F32) for shap...]
    all_to_all x1 -> x0, starting transfers between devices: 3.49 us -> none  [flip_second(): lax.all_to_all(averaged, 'gy', split_axis=1, concat_axis=0, tiled=True)]
  transfers between devices with their start and end apart: 9 -> 16, of which waited for: 9 -> 10; matrix products, arithmetic and copies ran while one was open for 1% -> 1% of each run, Pallas kernels for 0% -> 0%
where the time goes in v1:
time: 87.6 us; the launch traced here: 87.1 us
  starting transfers between devices  43.2 us (49%)
  waiting for transfers between devices  37.4 us (43%)
  Pallas kernels  3.86 us (4%)
  local copies, waits for them, and re-layouts  1.94 us (2%)
    ppermute x1, waiting for transfers between devices, local(): low = lax.ppermute(density[:, -8:], 'gy', up_y)  13 us
    ppermute x2, starting transfers between devices, mirrors(): lax.ppermute(to_x, 'gx', mirror_x)  9.33 us
    ppermute x1, starting transfers between devices, local(): before = lax.ppermute(smooth, 'gx', fold_up_x)  8.21 us
    ppermute x2, starting transfers between devices, mirrors(): lax.ppermute(to_xy, ('gx', 'gy'), mirror_xy)  5.68 us
    ppermute x2, waiting for transfers between devices, mirrors(): lax.ppermute(to_x, 'gx', mirror_x)  5.39 us
    ppermute x2, waiting for transfers between devices, mirrors(): lax.ppermute(to_y, 'gy', mirror_y)  4.93 us
    ppermute x2, starting transfers between devices, mirrors(): lax.ppermute(to_y, 'gy', mirror_y)  4.92 us
    ppermute x1, waiting for transfers between devices, local(): from_high = lax.ppermute(head, 'gy', fold_down_y)  4.85 us
  transfers between devices with their start and end apart: 16, of which 10 were waited for; matrix products, arithmetic and copies ran while one was open for 1% of the time, Pallas kernels for 0%

profile of v1, /device:TPU:1, one launch (start us, length us, event | category | flops | bytes accessed | tf_op | source)
XLA Modules:
  0.0 87.1 jit_solution(13260814220002145083)
XLA Ops:
  0.6 0.0 copy-start
  0.6 3.3 %collective-permute-start.1 = (f32[8,64,256]{2,1,0:T(8,128)}, f32[8,64,256]{2,1,0:T(8,128)S(1)}, u32[]{:S(2)}, u32[]{:S(2)}) collective-permute-start(f32[8,64,256]{2,1,0:T(8,128)} %own.1), channel_id=1, source_target_pairs={{8,0},{16,8},{24,16},{32,24},{40,32},{48,40},{56,48},{64,56},{72,6... | collective-permute-start | bytes 1572872 | tf_op jit(solution)/shard_map/ppermute | solution.py:220
  4.0 0.0 collective-permute-start
  4.0 0.9 %fusion = (f32[8,8,256]{2,1,0:T(8,128)S(1)}, f32[8,8,256]{2,1,0:T(8,128)S(1)}) fusion(f32[8,64,256]{2,1,0:T(8,128)} %own.1), kind=kLoop, calls=%fused_computation.2 | loop fusion | bytes 262144 | tf_op jit(solution)/shard_map/slice | solution.py:218
  4.8 2.2 %collective-permute-start.2 = (f32[8,8,256]{2,1,0:T(8,128)S(1)}, f32[8,8,256]{2,1,0:T(8,128)S(1)}, u32[]{:S(2)}, u32[]{:S(2)}) collective-permute-start(f32[8,8,256]{2,1,0:T(8,128)S(1)} %get-tuple-element.19), channel_id=1, source_target_pairs={{0,1},{1,2},{2,3},{3,4},{4,5},{5,6},{6,7},{7,0},{8,9},{9,10},{10,1... | collective-permute-start | bytes 196616 | tf_op jit(solution)/shard_map/ppermute | solution.py:217
  7.0 3.0 %collective-permute-start.3 = (f32[8,8,256]{2,1,0:T(8,128)S(1)}, f32[8,8,256]{2,1,0:T(8,128)S(1)}, u32[]{:S(2)}, u32[]{:S(2)}) collective-permute-start(f32[8,8,256]{2,1,0:T(8,128)S(1)} %get-tuple-element.18), channel_id=1, source_target_pairs={{1,0},{2,1},{3,2},{4,3},{5,4},{6,5},{7,6},{0,7},{9,8},{10,9},{11,1... | collective-permute-start | bytes 196616 | tf_op jit(solution)/shard_map/ppermute | solution.py:218
  10.0 13.0 %collective-permute-done.2.low = f32[8,8,256]{2,1,0:T(8,128)S(1)} collective-permute-done((f32[8,8,256]{2,1,0:T(8,128)S(1)}, f32[8,8,256]{2,1,0:T(8,128)S(1)}, u32[]{:S(2)}, u32[]{:S(2)}) %collective-permute-start.2) | collective-permute-done | bytes 65568 | tf_op jit(solution)/shard_map/ppermute | solution.py:217
  23.0 0.0 collective-permute-done.3.high
  23.0 0.1 collective-permute-start.5
  23.1 1.7 %collective-permute-start.4 = (f32[8,16,256]{2,1,0:T(8,128)S(1)}, f32[8,16,256]{2,1,0:T(8,128)S(1)}, u32[]{:S(2)}, u32[]{:S(2)}) collective-permute-start(f32[8,16,256]{2,1,0:T(8,128)S(1)} %constant_dynamic-update-slice_fusion), channel_id=1, source_target_pairs={{0,8},{8,16},{16,24},{24,32},{32,40},{40,48},{48,56},{56,64},{64,7... | collective-permute-start | bytes 393224 | tf_op jit(solution)/shard_map/ppermute | solution.py:222
  24.8 2.6 %collective-permute-done.5.corner_r = f32[8,16,256]{2,1,0:T(8,128)S(1)} collective-permute-done((f32[8,16,256]{2,1,0:T(8,128)S(1)}, f32[8,16,256]{2,1,0:T(8,128)S(1)}, u32[]{:S(2)}, u32[]{:S(2)}) %collective-permute-start.5) | collective-permute-done | bytes 131104 | tf_op jit(solution)/shard_map/ppermute | solution.py:223
  27.5 0.0 collective-permute-done.4.corner_l
  27.5 0.0 collective-permute-done.1.right
  27.5 0.0 collective-permute-done.left
  27.5 0.0 copy-done
  27.5 0.0 copy-start.1
  27.5 1.0 %copy-done.1 = f32[8,64,256]{2,1,0:T(8,128)S(1)} copy-done((f32[8,64,256]{2,1,0:T(8,128)S(1)}, f32[8,64,256]{2,1,0:T(8,128)}, u32[]{:S(2)}) %copy-start.1) | copy-done | bytes 524312
  28.6 2.0 %shard_map.41 = (f32[8,64,256]{2,1,0:T(8,128)}, f32[8,32,128]{2,1,0:T(8,128)S(1)}, f32[8,32,128]{2,1,0:T(8,128)S(1)}, f32[8,32,128]{2,1,0:T(8,128)S(1)}, f32[8,32,128]{2,1,0:T(8,128)S(1)}) custom-call(f32[8,64,256]{2,1,0:T(8,128)S(1)} %copy-done, f32[8,64,256]{2,1,0:T(8,128)S(1)} %collective-permute-done.left, ...), custom_call_target="tpu_custom_call" | custom-call | tf_op jit(solution)/shard_map/pallas_call | solution.py:22
  30.6 7.0 %collective-permute-start.6 = (f32[8,32,128]{2,1,0:T(8,128)S(1)}, f32[8,32,128]{2,1,0:T(8,128)S(1)}, u32[]{:S(2)}, u32[]{:S(2)}) collective-permute-start(f32[8,32,128]{2,1,0:T(8,128)S(1)} %get-tuple-element.12), channel_id=1, source_target_pairs={{0,248},{8,240},{16,232},{24,224},{32,216},{40,208},{48,200},{56,1... | collective-permute-start | bytes 393224 | tf_op jit(solution)/shard_map/ppermute | solution.py:207
  37.6 0.6 collective-permute-start.7
  38.2 4.2 %collective-permute-start.8 = (f32[8,32,128]{2,1,0:T(8,128)S(1)}, f32[8,32,128]{2,1,0:T(8,128)S(1)}, u32[]{:S(2)}, u32[]{:S(2)}) collective-permute-start(f32[8,32,128]{2,1,0:T(8,128)S(1)} %get-tuple-element.14), channel_id=1, source_target_pairs={{0,255},{1,254},{2,253},{3,252},{4,251},{5,250},{6,249},{7,248},{8... | collective-permute-start | bytes 393224 | tf_op jit(solution)/shard_map/ppermute | solution.py:209
  42.4 0.6 collective-permute-done.6.from_x
  43.0 4.9 %collective-permute-done.7.from_y = f32[8,32,128]{2,1,0:T(8,128)S(1)} collective-permute-done((f32[8,32,128]{2,1,0:T(8,128)S(1)}, f32[8,32,128]{2,1,0:T(8,128)S(1)}, u32[]{:S(2)}, u32[]{:S(2)}) %collective-permute-start.7) | collective-permute-done | bytes 131104 | tf_op jit(solution)/shard_map/ppermute | solution.py:208
  47.9 2.5 %collective-permute-done.8.from_xy = f32[8,32,128]{2,1,0:T(8,128)S(1)} collective-permute-done((f32[8,32,128]{2,1,0:T(8,128)S(1)}, f32[8,32,128]{2,1,0:T(8,128)S(1)}, u32[]{:S(2)}, u32[]{:S(2)}) %collective-permute-start.8) | collective-permute-done | bytes 131104 | tf_op jit(solution)/shard_map/ppermute | solution.py:209
  50.4 0.1 shard_map.42
  50.5 1.5 %collective-permute-start.9 = (f32[8,8,128]{2,1,0:T(8,128)S(1)}, f32[8,8,128]{2,1,0:T(8,128)S(1)}, u32[]{:S(2)}, u32[]{:S(2)}) collective-permute-start(f32[8,8,128]{2,1,0:T(8,128)S(1)} %get-tuple-element.16), channel_id=1, source_target_pairs={{0,1},{1,2},{2,3},{4,5},{5,6},{6,7},{8,9},{9,10},{10,11},{12,13},{... | collective-permute-start | bytes 98312 | tf_op jit(solution)/shard_map/ppermute | solution.py:231
  52.0 1.3 %collective-permute-start.10 = (f32[8,8,128]{2,1,0:T(8,128)S(1)}, f32[8,8,128]{2,1,0:T(8,128)S(1)}, u32[]{:S(2)}, u32[]{:S(2)}) collective-permute-start(f32[8,8,128]{2,1,0:T(8,128)S(1)} %get-tuple-element.17), channel_id=1, source_target_pairs={{1,0},{2,1},{3,2},{5,4},{6,5},{7,6},{9,8},{10,9},{11,10},{13,12},{... | collective-permute-start | bytes 98312 | tf_op jit(solution)/shard_map/ppermute | solution.py:232
  53.3 0.0 collective-permute-done.9.from_low
  53.3 4.9 %collective-permute-done.10.from_high = f32[8,8,128]{2,1,0:T(8,128)S(1)} collective-permute-done((f32[8,8,128]{2,1,0:T(8,128)S(1)}, f32[8,8,128]{2,1,0:T(8,128)S(1)}, u32[]{:S(2)}, u32[]{:S(2)}) %collective-permute-start.10) | collective-permute-done | bytes 32800 | tf_op jit(solution)/shard_map/ppermute | solution.py:232
  58.2 0.2 shard_map.43.own
  58.4 1.9 %collective-permute-start.12 = (f32[8,32,128]{2,1,0:T(8,128)S(1)}, f32[8,32,128]{2,1,0:T(8,128)S(1)}, u32[]{:S(2)}, u32[]{:S(2)}) collective-permute-start(f32[8,32,128]{2,1,0:T(8,128)S(1)} %shard_map.43.own), channel_id=1, source_target_pairs={{8,0},{16,8},{24,16},{32,24},{40,32},{48,40},{56,48},{64,56},{72,6... | collective-permute-start | bytes 393224 | tf_op jit(solution)/shard_map/ppermute | solution.py:235
  60.3 8.2 %collective-permute-start.11 = (f32[8,32,128]{2,1,0:T(8,128)S(1)}, f32[8,32,128]{2,1,0:T(8,128)S(1)}, u32[]{:S(2)}, u32[]{:S(2)}) collective-permute-start(f32[8,32,128]{2,1,0:T(8,128)S(1)} %shard_map.43.own), channel_id=1, source_target_pairs={{0,8},{8,16},{16,24},{24,32},{32,40},{40,48},{48,56},{56,64},{64,7... | collective-permute-start | bytes 393224 | tf_op jit(solution)/shard_map/ppermute | solution.py:234
  68.6 0.7 collective-permute-done.12.right
  69.3 1.2 %collective-permute-done.11.left = f32[8,32,128]{2,1,0:T(8,128)S(1)} collective-permute-done((f32[8,32,128]{2,1,0:T(8,128)S(1)}, f32[8,32,128]{2,1,0:T(8,128)S(1)}, u32[]{:S(2)}, u32[]{:S(2)}) %collective-permute-start.11) | collective-permute-done | bytes 131104 | tf_op jit(solution)/shard_map/ppermute | solution.py:234
  70.5 0.1 shard_map.44.own
  70.6 1.5 %collective-permute-start.15 = (f32[8,32,128]{2,1,0:T(8,128)S(1)}, f32[8,32,128]{2,1,0:T(8,128)S(1)}, u32[]{:S(2)}, u32[]{:S(2)}) collective-permute-start(f32[8,32,128]{2,1,0:T(8,128)S(1)} %shard_map.44.own), channel_id=1, source_target_pairs={{0,255},{1,254},{2,253},{3,252},{4,251},{5,250},{6,249},{7,248},{8... | collective-permute-start | bytes 393224 | tf_op jit(solution)/shard_map/ppermute | solution.py:209
  72.1 4.3 %collective-permute-start.14 = (f32[8,32,128]{2,1,0:T(8,128)S(1)}, f32[8,32,128]{2,1,0:T(8,128)S(1)}, u32[]{:S(2)}, u32[]{:S(2)}) collective-permute-start(f32[8,32,128]{2,1,0:T(8,128)S(1)} %shard_map.44.own), channel_id=1, source_target_pairs={{0,7},{1,6},{2,5},{3,4},{4,3},{5,2},{6,1},{7,0},{8,15},{9,14},{10,... | collective-permute-start | bytes 393224 | tf_op jit(solution)/shard_map/ppermute | solution.py:208
  76.4 2.3 %collective-permute-start.13 = (f32[8,32,128]{2,1,0:T(8,128)S(1)}, f32[8,32,128]{2,1,0:T(8,128)S(1)}, u32[]{:S(2)}, u32[]{:S(2)}) collective-permute-start(f32[8,32,128]{2,1,0:T(8,128)S(1)} %shard_map.44.own), channel_id=1, source_target_pairs={{0,248},{8,240},{16,232},{24,224},{32,216},{40,208},{48,200},{56,1... | collective-permute-start | bytes 393224 | tf_op jit(solution)/shard_map/ppermute | solution.py:207
  78.7 2.2 %collective-permute-done.15.from_xy = f32[8,32,128]{2,1,0:T(8,128)S(1)} collective-permute-done((f32[8,32,128]{2,1,0:T(8,128)S(1)}, f32[8,32,128]{2,1,0:T(8,128)S(1)}, u32[]{:S(2)}, u32[]{:S(2)}) %collective-permute-start.15) | collective-permute-done | bytes 131104 | tf_op jit(solution)/shard_map/ppermute | solution.py:209
  80.9 0.0 collective-permute-done.14.from_y
  80.9 4.8 %collective-permute-done.13.from_x = f32[8,32,128]{2,1,0:T(8,128)S(1)} collective-permute-done((f32[8,32,128]{2,1,0:T(8,128)S(1)}, f32[8,32,128]{2,1,0:T(8,128)S(1)}, u32[]{:S(2)}, u32[]{:S(2)}) %collective-permute-start.13) | collective-permute-done | bytes 131104 | tf_op jit(solution)/shard_map/ppermute | solution.py:207
  85.7 1.4 %shard_map.45 = f32[8,64,256]{2,1,0:T(8,128)} custom-call(f32[8,32,128]{2,1,0:T(8,128)S(1)} %shard_map.44.own, f32[8,32,128]{2,1,0:T(8,128)S(1)} %collective-permute-done.13.from_x, f32[8,32,128]{2,1,0:T(8,128)S(1)} %collective-permute-done.14.from_y, f32[8,32,128]{2,1,0:T(8,128)S(1)} %collective-permute-done.15.from_xy), custom_call_target="tpu_custom_call" | custom-call | tf_op jit(solution)/shard_map/pallas_call | solution.py:22
  (2 shorter events, 0.0 us)
Async XLA Ops:
  0.6 26.9 %copy-start = (f32[8,64,256]{2,1,0:T(8,128)S(1)}, f32[8,64,256]{2,1,0:T(8,128)}, u32[]{:S(2)}) copy-start(f32[8,64,256]{2,1,0:T(8,128)} %own.1) | copy-start | bytes 1572868
  0.6 26.9 %collective-permute-start.1 = (f32[8,64,256]{2,1,0:T(8,128)}, f32[8,64,256]{2,1,0:T(8,128)S(1)}, u32[]{:S(2)}, u32[]{:S(2)}) collective-permute-start(f32[8,64,256]{2,1,0:T(8,128)} %own.1), channel_id=1, source_target_pairs={{8,0},{16,8},{24,16},{32,24},{40,32},{48,40},{56,48},{64,56},{72,6... | collective-permute-start | bytes 1572872 | tf_op jit(solution)/shard_map/ppermute | solution.py:220
  4.0 23.5 %collective-permute-start = (f32[8,64,256]{2,1,0:T(8,128)}, f32[8,64,256]{2,1,0:T(8,128)S(1)}, u32[]{:S(2)}, u32[]{:S(2)}) collective-permute-start(f32[8,64,256]{2,1,0:T(8,128)} %own.1), channel_id=1, source_target_pairs={{0,8},{8,16},{16,24},{24,32},{32,40},{40,48},{48,56},{56,64},{64,7... | collective-permute-start | bytes 1572872 | tf_op jit(solution)/shard_map/ppermute | solution.py:219
  4.8 18.1 %collective-permute-start.2 = (f32[8,8,256]{2,1,0:T(8,128)S(1)}, f32[8,8,256]{2,1,0:T(8,128)S(1)}, u32[]{:S(2)}, u32[]{:S(2)}) collective-permute-start(f32[8,8,256]{2,1,0:T(8,128)S(1)} %get-tuple-element.19), channel_id=1, source_target_pairs={{0,1},{1,2},{2,3},{3,4},{4,5},{5,6},{6,7},{7,0},{8,9},{9,10},{10,1... | collective-permute-start | bytes 196616 | tf_op jit(solution)/shard_map/ppermute | solution.py:217
  7.0 16.0 %collective-permute-start.3 = (f32[8,8,256]{2,1,0:T(8,128)S(1)}, f32[8,8,256]{2,1,0:T(8,128)S(1)}, u32[]{:S(2)}, u32[]{:S(2)}) collective-permute-start(f32[8,8,256]{2,1,0:T(8,128)S(1)} %get-tuple-element.18), channel_id=1, source_target_pairs={{1,0},{2,1},{3,2},{4,3},{5,4},{6,5},{7,6},{0,7},{9,8},{10,9},{11,1... | collective-permute-start | bytes 196616 | tf_op jit(solution)/shard_map/ppermute | solution.py:218
  23.0 4.5 %collective-permute-start.5 = (f32[8,16,256]{2,1,0:T(8,128)S(1)}, f32[8,16,256]{2,1,0:T(8,128)S(1)}, u32[]{:S(2)}, u32[]{:S(2)}) collective-permute-start(f32[8,16,256]{2,1,0:T(8,128)S(1)} %constant_dynamic-update-slice_fusion), channel_id=1, source_target_pairs={{8,0},{16,8},{24,16},{32,24},{40,32},{48,40},{56,48},{64,56},{72,6... | collective-permute-start | bytes 393224 | tf_op jit(solution)/shard_map/ppermute | solution.py:223
  23.1 4.4 %collective-permute-start.4 = (f32[8,16,256]{2,1,0:T(8,128)S(1)}, f32[8,16,256]{2,1,0:T(8,128)S(1)}, u32[]{:S(2)}, u32[]{:S(2)}) collective-permute-start(f32[8,16,256]{2,1,0:T(8,128)S(1)} %constant_dynamic-update-slice_fusion), channel_id=1, source_target_pairs={{0,8},{8,16},{16,24},{24,32},{32,40},{40,48},{48,56},{56,64},{64,7... | collective-permute-start | bytes 393224 | tf_op jit(solution)/shard_map/ppermute | solution.py:222
  27.5 1.0 %copy-start.1 = (f32[8,64,256]{2,1,0:T(8,128)S(1)}, f32[8,64,256]{2,1,0:T(8,128)}, u32[]{:S(2)}) copy-start(f32[8,64,256]{2,1,0:T(8,128)} %sens.1) | copy-start | bytes 1572868
  30.6 12.4 %collective-permute-start.6 = (f32[8,32,128]{2,1,0:T(8,128)S(1)}, f32[8,32,128]{2,1,0:T(8,128)S(1)}, u32[]{:S(2)}, u32[]{:S(2)}) collective-permute-start(f32[8,32,128]{2,1,0:T(8,128)S(1)} %get-tuple-element.12), channel_id=1, source_target_pairs={{0,248},{8,240},{16,232},{24,224},{32,216},{40,208},{48,200},{56,1... | collective-permute-start | bytes 393224 | tf_op jit(solution)/shard_map/ppermute | solution.py:207
  37.6 10.3 %collective-permute-start.7 = (f32[8,32,128]{2,1,0:T(8,128)S(1)}, f32[8,32,128]{2,1,0:T(8,128)S(1)}, u32[]{:S(2)}, u32[]{:S(2)}) collective-permute-start(f32[8,32,128]{2,1,0:T(8,128)S(1)} %get-tuple-element.13), channel_id=1, source_target_pairs={{0,7},{1,6},{2,5},{3,4},{4,3},{5,2},{6,1},{7,0},{8,15},{9,14},{10,... | collective-permute-start | bytes 393224 | tf_op jit(solution)/shard_map/ppermute | solution.py:208
  38.2 12.2 %collective-permute-start.8 = (f32[8,32,128]{2,1,0:T(8,128)S(1)}, f32[8,32,128]{2,1,0:T(8,128)S(1)}, u32[]{:S(2)}, u32[]{:S(2)}) collective-permute-start(f32[8,32,128]{2,1,0:T(8,128)S(1)} %get-tuple-element.14), channel_id=1, source_target_pairs={{0,255},{1,254},{2,253},{3,252},{4,251},{5,250},{6,249},{7,248},{8... | collective-permute-start | bytes 393224 | tf_op jit(solution)/shard_map/ppermute | solution.py:209
  50.5 2.8 %collective-permute-start.9 = (f32[8,8,128]{2,1,0:T(8,128)S(1)}, f32[8,8,128]{2,1,0:T(8,128)S(1)}, u32[]{:S(2)}, u32[]{:S(2)}) collective-permute-start(f32[8,8,128]{2,1,0:T(8,128)S(1)} %get-tuple-element.16), channel_id=1, source_target_pairs={{0,1},{1,2},{2,3},{4,5},{5,6},{6,7},{8,9},{9,10},{10,11},{12,13},{... | collective-permute-start | bytes 98312 | tf_op jit(solution)/shard_map/ppermute | solution.py:231
  52.0 6.2 %collective-permute-start.10 = (f32[8,8,128]{2,1,0:T(8,128)S(1)}, f32[8,8,128]{2,1,0:T(8,128)S(1)}, u32[]{:S(2)}, u32[]{:S(2)}) collective-permute-start(f32[8,8,128]{2,1,0:T(8,128)S(1)} %get-tuple-element.17), channel_id=1, source_target_pairs={{1,0},{2,1},{3,2},{5,4},{6,5},{7,6},{9,8},{10,9},{11,10},{13,12},{... | collective-permute-start | bytes 98312 | tf_op jit(solution)/shard_map/ppermute | solution.py:232
  58.4 10.9 %collective-permute-start.12 = (f32[8,32,128]{2,1,0:T(8,128)S(1)}, f32[8,32,128]{2,1,0:T(8,128)S(1)}, u32[]{:S(2)}, u32[]{:S(2)}) collective-permute-start(f32[8,32,128]{2,1,0:T(8,128)S(1)} %shard_map.43.own), channel_id=1, source_target_pairs={{8,0},{16,8},{24,16},{32,24},{40,32},{48,40},{56,48},{64,56},{72,6... | collective-permute-start | bytes 393224 | tf_op jit(solution)/shard_map/ppermute | solution.py:235
  60.3 10.1 %collective-permute-start.11 = (f32[8,32,128]{2,1,0:T(8,128)S(1)}, f32[8,32,128]{2,1,0:T(8,128)S(1)}, u32[]{:S(2)}, u32[]{:S(2)}) collective-permute-start(f32[8,32,128]{2,1,0:T(8,128)S(1)} %shard_map.43.own), channel_id=1, source_target_pairs={{0,8},{8,16},{16,24},{24,32},{32,40},{40,48},{48,56},{56,64},{64,7... | collective-permute-start | bytes 393224 | tf_op jit(solution)/shard_map/ppermute | solution.py:234
  70.6 10.3 %collective-permute-start.15 = (f32[8,32,128]{2,1,0:T(8,128)S(1)}, f32[8,32,128]{2,1,0:T(8,128)S(1)}, u32[]{:S(2)}, u32[]{:S(2)}) collective-permute-start(f32[8,32,128]{2,1,0:T(8,128)S(1)} %shard_map.44.own), channel_id=1, source_target_pairs={{0,255},{1,254},{2,253},{3,252},{4,251},{5,250},{6,249},{7,248},{8... | collective-permute-start | bytes 393224 | tf_op jit(solution)/shard_map/ppermute | solution.py:209
  72.1 8.8 %collective-permute-start.14 = (f32[8,32,128]{2,1,0:T(8,128)S(1)}, f32[8,32,128]{2,1,0:T(8,128)S(1)}, u32[]{:S(2)}, u32[]{:S(2)}) collective-permute-start(f32[8,32,128]{2,1,0:T(8,128)S(1)} %shard_map.44.own), channel_id=1, source_target_pairs={{0,7},{1,6},{2,5},{3,4},{4,3},{5,2},{6,1},{7,0},{8,15},{9,14},{10,... | collective-permute-start | bytes 393224 | tf_op jit(solution)/shard_map/ppermute | solution.py:208
  76.4 9.3 %collective-permute-start.13 = (f32[8,32,128]{2,1,0:T(8,128)S(1)}, f32[8,32,128]{2,1,0:T(8,128)S(1)}, u32[]{:S(2)}, u32[]{:S(2)}) collective-permute-start(f32[8,32,128]{2,1,0:T(8,128)S(1)} %shard_map.44.own), channel_id=1, source_target_pairs={{0,248},{8,240},{16,232},{24,224},{32,216},{40,208},{48,200},{56,1... | collective-permute-start | bytes 393224 | tf_op jit(solution)/shard_map/ppermute | solution.py:207

commit v2 on v1

v2 whole, which is shorter than its diff:
```python
import math

import jax
import jax.numpy as jnp
from jax import lax
from jax.experimental import pallas as pl
from jax.experimental.pallas import tpu as pltpu
from jax.sharding import PartitionSpec as P

RADIUS = 8
WIDTH = RADIUS + 1
EDGE = 2 * RADIUS
SHARPNESS = 8.0
THRESHOLD = 0.5
TANH_LOW = math.tanh(SHARPNESS * THRESHOLD)
SCALE_SUM = TANH_LOW + math.tanh(SHARPNESS * (1.0 - THRESHOLD))
WEIGHT = 1.0 / float(WIDTH**6)
HALF = 64
F32 = jnp.float32


def run(body, outs, args, scratch=()):
    return pl.pallas_call(
        body,
        out_shape=[jax.ShapeDtypeStruct(shape, F32) for shape in outs],
        in_specs=[pl.BlockSpec(memory_space=pltpu.VMEM)] * len(args),
        out_specs=[pl.BlockSpec(memory_space=pltpu.VMEM)] * len(outs),
        scratch_shapes=list(scratch),
        compiler_params=pltpu.CompilerParams(vmem_limit_bytes=24 * 1024 * 1024),
    )(*args)


def box_list(items):
    pairs = [a + b for a, b in zip(items, items[1:])]
    fours = [a + b for a, b in zip(pairs, pairs[2:])]
    eights = [a + b for a, b in zip(fours, fours[4:])]
    return [a + b for a, b in zip(eights, items[8:])]


def cone_list(items):
    return box_list(box_list(items))


def ahead(field, step, axis):
    return pltpu.roll(field, field.shape[axis] - step, axis)


def box_rows(field, axis):
    pairs = field + ahead(field, 1, axis)
    fours = pairs + ahead(pairs, 2, axis)
    eights = fours + ahead(fours, 4, axis)
    return eights + ahead(field, 8, axis)


def cone_rows(field, axis):
    return box_rows(box_rows(field, axis), axis)


def reverse_eights(field, axis):
    size = field.shape[axis]
    row = lax.broadcasted_iota(jnp.int32, field.shape, axis)
    for bit in (1, 2, 4):
        field = jnp.where(
            (row & bit) == 0, pltpu.roll(field, size - bit, axis), pltpu.roll(field, bit, axis)
        )
    return field


def swap_halves(field):
    return pltpu.roll(field, HALF, field.ndim - 1)


def flip_planes(field):
    return jnp.stack([field[p] for p in reversed(range(field.shape[0]))])


def flip_rows(field):
    field = reverse_eights(field, 1)
    rows = field.shape[1]
    groups = [field[:, r : r + 8] for r in range(0, rows, 8)]
    return swap_halves(jnp.concatenate(groups[::-1], axis=1))


def first_lanes(shape):
    return lax.broadcasted_iota(jnp.int32, shape, len(shape) - 1) < HALF


def z_pass(field, pieces):
    count = field.shape[-1]
    row = lax.broadcasted_iota(jnp.int32, (count, count), 0)
    col = lax.broadcasted_iota(jnp.int32, (count, count), 1)
    gap = jnp.abs(row - col)
    taps = jnp.maximum(WIDTH - jnp.minimum(gap, count - gap), 0).astype(F32).astype(jnp.bfloat16)
    total = None
    for _ in range(pieces):
        piece = field.astype(jnp.bfloat16)
        field = field - piece.astype(F32)
        part = jnp.dot(piece, taps, preferred_element_type=F32)
        total = part if total is None else total + part
    return total


def solution(mesh):
    nx, ny = mesh.shape["gx"], mesh.shape["gy"]
    hx, hy = nx // 2, ny // 2

    def ordered(odd, near, far):
        return jnp.where(odd, near, far), jnp.where(odd, far, near)

    def is_odd(axis):
        return lax.rem(lax.axis_index(axis), 2) == 1

    def across(own, near, far, odd, row, lanes, first=None, last=None):
        planes = own.shape[0]
        rows = slice(row, row + 8)
        mine = [own[p, rows, lanes] for p in range(planes)]
        before, after = [], []
        for p in range(planes):
            b, a = ordered(odd, near[p, rows, lanes], far[p, rows, lanes])
            before.append(b if first is None else jnp.where(first, mine[-1 - p], b))
            after.append(a if last is None else jnp.where(last, mine[-1 - p], a))
        return cone_list(before + mine + after)

    def hold_kernel(first, second, first_out, second_out):
        first_out[...] = first[...]
        second_out[...] = second[...]

    def cross_edges_kernel(own, near, far, sens, to_near, to_far):
        planes, rows, depth = own.shape
        odd_x, odd_y = is_odd("gx"), is_odd("gy")
        for lane in range(0, depth, 128):
            lanes = slice(lane, lane + 128)
            for row in range(0, EDGE, 8):
                heads = across(own, near, far, odd_x, row, lanes)
                tails = across(own, near, far, odd_x, rows - EDGE + row, lanes)
                for p, (head, tail) in enumerate(zip(heads, tails)):
                    to_near[p, row : row + 8, lanes] = jnp.where(odd_y, head, tail)
                    to_far[p, row : row + 8, lanes] = jnp.where(odd_y, tail, head)
        head, tail = sens[:, :RADIUS], sens[:, rows - RADIUS :]
        to_near[:, EDGE:] = jnp.where(odd_y, head, tail)
        to_far[:, EDGE:] = jnp.where(odd_y, tail, head)

    def cross_body_kernel(own, near, far, edge_near, edge_far, out, flat):
        planes, rows, depth = own.shape
        odd_x = is_odd("gx")
        head, tail = ordered(is_odd("gy"), edge_near[:, :EDGE], edge_far[:, :EDGE])
        for p in range(planes):
            flat[p * rows : p * rows + EDGE, :] = head[p]
            flat[(p + 1) * rows - EDGE : (p + 1) * rows, :] = tail[p]
        for lane in range(0, depth, 128):
            lanes = slice(lane, lane + 128)
            for row in range(EDGE, rows - EDGE, 8):
                for p, item in enumerate(across(own, near, far, odd_x, row, lanes)):
                    flat[p * rows + row : p * rows + row + 8, lanes] = item
        out[...] = z_pass(flat[...], 3).reshape(planes, rows, depth)

    def chain_kernel(own, near, far, sens, tilted_out, keep, to_x, to_y, to_xy, halo, ys):
        planes, rows, depth = own.shape
        wide = rows + 2 * RADIUS
        low, high = ordered(is_odd("gy"), near[...], far[...])
        for p in range(planes):
            halo[2 * EDGE * p : 2 * EDGE * p + EDGE, :] = low[p, :EDGE]
            halo[2 * EDGE * p + EDGE : 2 * EDGE * (p + 1), :] = high[p, :EDGE]
        outer = z_pass(halo[...], 3).reshape(planes, 2 * EDGE, depth)
        for p in range(planes):
            padded = jnp.concatenate([outer[p, :EDGE], own[p], outer[p, EDGE:]], axis=0)
            ys[p] = cone_rows(padded, 0)[:wide]
        filtered = ys[...] * WEIGHT
        tilted = jnp.tanh(SHARPNESS * (filtered - THRESHOLD))
        tilted_out[...] = tilted[:, RADIUS : RADIUS + rows]
        slope = (1.0 - tilted * tilted) * (SHARPNESS / SCALE_SUM)
        chain = jnp.concatenate([low[:, EDGE:], sens[...], high[:, EDGE:]], axis=1) * slope
        upper_x = lax.axis_index("gx") >= hx
        upper_y = lax.axis_index("gy") >= hy
        near = jnp.where(upper_x, chain[:, :, 128:], chain[:, :, :128])
        far = jnp.where(upper_x, chain[:, :, :128], chain[:, :, 128:])
        for field, even_out, odd_out in ((near, keep, to_y), (far, to_x, to_xy)):
            top, bottom = field[:, : wide // 2], field[:, wide // 2 :]
            mask = first_lanes(top.shape)
            even = jnp.where(mask, top, swap_halves(bottom))
            odd = jnp.where(mask, swap_halves(top), bottom)
            even_out[...] = jnp.where(upper_y, odd, even)
            odd_out[...] = jnp.where(upper_y, even, odd)

    def project_kernel(tilted, projected):
        projected[...] = (TANH_LOW + tilted[...]) * (1.0 / SCALE_SUM)

    def sum_kernel(keep, from_x, from_y, from_xy, out):
        other = flip_rows(from_y[...] + flip_planes(from_xy[...]))
        total = keep[...] + flip_planes(from_x[...]) + other
        rows = total.shape[1]
        swapped = swap_halves(total)
        upper = jnp.concatenate([total, swapped[:, :8]], axis=1)
        lower = jnp.concatenate([swapped[:, rows - 8 :], total], axis=1)
        padded = jnp.where(first_lanes(upper.shape), upper, lower)
        for p in range(total.shape[0]):
            out[p] = cone_rows(padded[p], 0)[: out.shape[1]]

    def cross_quarter_kernel(own, near, far, out):
        planes, rows, depth = own.shape
        place = lax.rem(lax.axis_index("gx"), hx)
        first, last = place == 0, place == hx - 1
        for row in range(0, rows, 8):
            items = across(own, near, far, is_odd("gx"), row, slice(0, depth), first, last)
            for p, item in enumerate(items):
                out[p, row : row + 8, :] = item

    def finish_kernel(own, from_x, from_y, from_xy, gradient, flat):
        planes, rows, depth = gradient.shape
        upper_x = lax.axis_index("gx") >= hx
        upper_y = lax.axis_index("gy") >= hy
        near_own, near_y = own[...], flip_rows(from_y[...])
        far_x, far_xy = flip_planes(from_x[...]), flip_rows(flip_planes(from_xy[...]))
        sides = []
        for mine, other in ((near_own, near_y), (far_x, far_xy)):
            even, odd = jnp.where(upper_y, other, mine), jnp.where(upper_y, mine, other)
            mask = first_lanes(even.shape)
            top = jnp.where(mask, even, swap_halves(odd))
            bottom = jnp.where(mask, swap_halves(even), odd)
            sides.append(jnp.concatenate([top, bottom], axis=1).reshape(planes * rows, 128))
        near, far = sides
        flat[:, :128] = jnp.where(upper_x, far, near)
        flat[:, 128:] = jnp.where(upper_x, near, far)
        gradient[...] = (z_pass(flat[...], 2) * (0.25 * WEIGHT)).reshape(planes, rows, depth)

    both = [(i, j) for i in range(nx) for j in range(ny)]
    near_x = [(i, i ^ 1) for i in range(nx)]
    near_y = [(j, j ^ 1) for j in range(ny)]
    far_x = [(i, (i + (1 if i % 2 else -1)) % nx) for i in range(nx)]
    far_y = [(j, (j + (1 if j % 2 else -1)) % ny) for j in range(ny)]
    fold_far_x = [(a, b) for a, b in far_x if a // hx == b // hx and abs(a - b) == 1]
    mirror_x = [(i, nx - 1 - i) for i in range(nx)]
    mirror_y = [(j, ny - 1 - j) for j in range(ny)]
    mirror_xy = [(i * ny + j, (nx - 1 - i) * ny + ny - 1 - j) for i, j in both]

    def mirrors(to_x, to_y, to_xy):
        from_xy = lax.ppermute(to_xy, ("gx", "gy"), mirror_xy)
        from_y = lax.ppermute(to_y, "gy", mirror_y)
        from_x = lax.ppermute(to_x, "gx", mirror_x)
        return from_x, from_y, from_xy

    def local(density, sensitivity):
        block = density.shape
        planes, rows, depth = block
        packed = (planes, rows // 2, 128)
        wide = (planes, rows // 2 + RADIUS, 128)
        flat = pltpu.VMEM((planes * rows, depth), F32)
        far = lax.ppermute(density, "gx", far_x)
        near = lax.ppermute(density, "gx", near_x)
        own, sens = run(hold_kernel, [block, block], (density, sensitivity))
        to_near, to_far = run(
            cross_edges_kernel, [(planes, EDGE + RADIUS, depth)] * 2, (own, near, far, sens)
        )
        from_far = lax.ppermute(to_far, "gy", far_y)
        from_near = lax.ppermute(to_near, "gy", near_y)
        (crossed,) = run(cross_body_kernel, [block], (own, near, far, to_near, to_far), (flat,))
        tilted, keep, to_x, to_y, to_xy = run(
            chain_kernel,
            [block, wide, wide, wide, wide],
            (crossed, from_near, from_far, sens),
            (
                pltpu.VMEM((planes * 2 * EDGE, depth), F32),
                pltpu.VMEM((planes, rows + 2 * RADIUS, depth), F32),
            ),
        )
        from_mirrors = mirrors(to_x, to_y, to_xy)
        (projected,) = run(project_kernel, [block], (tilted,))
        (smooth,) = run(sum_kernel, [packed], (keep, *from_mirrors))
        far = lax.ppermute(smooth, "gx", fold_far_x)
        near = lax.ppermute(smooth, "gx", near_x)
        (quarter,) = run(cross_quarter_kernel, [packed], (smooth, near, far))
        (gradient,) = run(
            finish_kernel,
            [block],
            (quarter, *mirrors(quarter, quarter, quarter)),
            (flat,),
        )
        return projected, gradient

    return jax.shard_map(
        local,
        mesh=mesh,
        in_specs=(P("gx", "gy", None), P("gx", "gy", None)),
        out_specs=(P("gx", "gy", None), P("gx", "gy", None)),
        check_vma=False,
    )
```

time: 87.6 us -> 76.2 us (0.87)
  starting transfers between devices: 43.2 us -> 34.2 us
  waiting for transfers between devices: 37.4 us -> 34.6 us
    ppermute x16 -> x12, starting transfers between devices: 43.2 us -> 34.2 us  [the longest x2 7.99 us: mirrors(): from_xy = lax.ppermute(to_xy, ('gx', 'gy'), mirror_xy)]
    ppermute x16 -> x12, waiting for transfers between devices: 37.4 us -> 34.6 us  [the longest x2 8.36 us: mirrors(): from_xy = lax.ppermute(to_xy, ('gx', 'gy'), mirror_xy)]
    unnamed x5 -> x4, local copies, waits for them, and re-layouts: 1.05 us -> 2.08 us
    slice x1 -> x0, local copies, waits for them, and re-layouts: 0.88 us -> none  [local(): high = lax.ppermute(density[:, :8], 'gy', down_y)]
    pallas_call x5 -> x8, Pallas kernels: 3.86 us -> 4.44 us  [run(): pl.pallas_call(body, out_shape=[jax.ShapeDtypeStruct(shape, F32) for shap...]
  transfers between devices with their start and end apart: 16 -> 12, of which waited for: 10 -> 10; matrix products, arithmetic and copies ran while one was open for 1% -> 0% of each run, Pallas kernels for 0% -> 2%
where the time goes in v2:
time: 76.2 us; the launch traced here: 76 us
  waiting for transfers between devices  34.6 us (45%)
  starting transfers between devices  34.2 us (45%)
  Pallas kernels  4.44 us (6%)
  local copies, waits for them, and re-layouts  2.08 us (3%)
    ppermute x2, waiting for transfers between devices, mirrors(): from_xy = lax.ppermute(to_xy, ('gx', 'gy'), mirror_xy)  8.36 us
    ppermute x2, starting transfers between devices, mirrors(): from_xy = lax.ppermute(to_xy, ('gx', 'gy'), mirror_xy)  7.99 us
    ppermute x2, waiting for transfers between devices, mirrors(): from_x = lax.ppermute(to_x, 'gx', mirror_x)  7.04 us
    ppermute x1, waiting for transfers between devices, local(): from_far = lax.ppermute(to_far, 'gy', far_y)  6.26 us
    ppermute x2, starting transfers between devices, mirrors(): from_x = lax.ppermute(to_x, 'gx', mirror_x)  6.16 us
    ppermute x1, waiting for transfers between devices, local(): far = lax.ppermute(density, 'gx', far_x)  5.7 us
    ppermute x1, starting transfers between devices, local(): near = lax.ppermute(density, 'gx', near_x)  5.13 us
    pallas_call x8, Pallas kernels, run(): pl.pallas_call(body, out_shape=[jax.ShapeDtypeStruct(shape, F32) for shap...  4.44 us
  transfers between devices with their start and end apart: 12, of which 10 were waited for; matrix products, arithmetic and copies ran while one was open for 0% of the time, Pallas kernels for 2%

profile of v2, /device:TPU:1, one launch (start us, length us, event | category | flops | bytes accessed | tf_op | source)
XLA Modules:
  0.0 76.0 jit_solution(13189176367619971246)
XLA Ops:
  0.6 2.7 %collective-permute-start.1 = (f32[8,64,256]{2,1,0:T(8,128)}, f32[8,64,256]{2,1,0:T(8,128)S(1)}, u32[]{:S(2)}, u32[]{:S(2)}) collective-permute-start(f32[8,64,256]{2,1,0:T(8,128)} %first.1), channel_id=1, source_target_pairs={{0,248},{8,16},{16,8},{24,32},{32,24},{40,48},{48,40},{56,64},{64,... | collective-permute-start | bytes 1572872 | tf_op jit(solution)/shard_map/ppermute | solution.py:248
  3.3 5.1 %collective-permute-start = (f32[8,64,256]{2,1,0:T(8,128)}, f32[8,64,256]{2,1,0:T(8,128)S(1)}, u32[]{:S(2)}, u32[]{:S(2)}) collective-permute-start(f32[8,64,256]{2,1,0:T(8,128)} %first.1), channel_id=1, source_target_pairs={{0,8},{8,0},{16,24},{24,16},{32,40},{40,32},{48,56},{56,48},{64,72... | collective-permute-start | bytes 1572872 | tf_op jit(solution)/shard_map/ppermute | solution.py:249
  8.4 0.0 copy-start
  8.4 1.0 %copy-done = f32[8,64,256]{2,1,0:T(8,128)S(1)} copy-done((f32[8,64,256]{2,1,0:T(8,128)S(1)}, f32[8,64,256]{2,1,0:T(8,128)}, u32[]{:S(2)}) %copy-start) | copy-done | bytes 524312
  9.5 0.0 copy-start.1
  9.5 1.0 %copy-done.1 = f32[8,64,256]{2,1,0:T(8,128)S(1)} copy-done((f32[8,64,256]{2,1,0:T(8,128)S(1)}, f32[8,64,256]{2,1,0:T(8,128)}, u32[]{:S(2)}) %copy-start.1) | copy-done | bytes 524312
  10.5 0.1 shard_map.41
  10.6 5.7 %collective-permute-done.1.far = f32[8,64,256]{2,1,0:T(8,128)S(1)} collective-permute-done((f32[8,64,256]{2,1,0:T(8,128)}, f32[8,64,256]{2,1,0:T(8,128)S(1)}, u32[]{:S(2)}, u32[]{:S(2)}) %collective-permute-start.1) | collective-permute-done | bytes 524320 | tf_op jit(solution)/shard_map/ppermute | solution.py:248
  16.3 0.0 collective-permute-done.near
  16.3 0.2 shard_map.42
  16.5 3.8 %collective-permute-start.2 = (f32[8,24,256]{2,1,0:T(8,128)S(1)}, f32[8,24,256]{2,1,0:T(8,128)S(1)}, u32[]{:S(2)}, u32[]{:S(2)}) collective-permute-start(f32[8,24,256]{2,1,0:T(8,128)S(1)} %get-tuple-element.13.edge_near), channel_id=1, source_target_pairs={{0,1},{1,0},{2,3},{3,2},{4,5},{5,4},{6,7},{7,6},{8,9},{9,8},{10,11... | collective-permute-start | bytes 589832 | tf_op jit(solution)/shard_map/ppermute | solution.py:255
  20.3 2.6 %collective-permute-start.3 = (f32[8,24,256]{2,1,0:T(8,128)S(1)}, f32[8,24,256]{2,1,0:T(8,128)S(1)}, u32[]{:S(2)}, u32[]{:S(2)}) collective-permute-start(f32[8,24,256]{2,1,0:T(8,128)S(1)} %get-tuple-element.14.edge_far), channel_id=1, source_target_pairs={{0,7},{1,2},{2,1},{3,4},{4,3},{5,6},{6,5},{7,0},{8,15},{9,10},{10,... | collective-permute-start | bytes 589832 | tf_op jit(solution)/shard_map/ppermute | solution.py:254
  22.8 0.6 shard_map.43.own
  23.4 1.5 %collective-permute-done.2.near = f32[8,24,256]{2,1,0:T(8,128)S(1)} collective-permute-done((f32[8,24,256]{2,1,0:T(8,128)S(1)}, f32[8,24,256]{2,1,0:T(8,128)S(1)}, u32[]{:S(2)}, u32[]{:S(2)}) %collective-permute-start.2) | collective-permute-done | bytes 196640 | tf_op jit(solution)/shard_map/ppermute | solution.py:255
  24.9 6.3 %collective-permute-done.3.far = f32[8,24,256]{2,1,0:T(8,128)S(1)} collective-permute-done((f32[8,24,256]{2,1,0:T(8,128)S(1)}, f32[8,24,256]{2,1,0:T(8,128)S(1)}, u32[]{:S(2)}, u32[]{:S(2)}) %collective-permute-start.3) | collective-permute-done | bytes 196640 | tf_op jit(solution)/shard_map/ppermute | solution.py:254
  31.2 1.0 %shard_map.44 = (f32[8,64,256]{2,1,0:T(8,128)S(1)}, f32[8,40,128]{2,1,0:T(8,128)S(1)}, f32[8,40,128]{2,1,0:T(8,128)S(1)}, f32[8,40,128]{2,1,0:T(8,128)S(1)}, f32[8,40,128]{2,1,0:T(8,128)S(1)}) custom-call(f32[8,64,256]{2,1,0:T(8,128)S(1)} %shard_map.43.own, f32[8,24,256]{2,1,0:T(8,128)S(1)} %collective-permute-done.2.near, ...), custom_call_target="tpu_custom_call" | custom-call | tf_op jit(solution)/shard_map/pallas_call | solution.py:23
  32.2 5.1 %collective-permute-start.4 = (f32[8,40,128]{2,1,0:T(8,128)S(1)}, f32[8,40,128]{2,1,0:T(8,128)S(1)}, u32[]{:S(2)}, u32[]{:S(2)}) collective-permute-start(f32[8,40,128]{2,1,0:T(8,128)S(1)} %get-tuple-element.17), channel_id=1, source_target_pairs={{0,248},{8,240},{16,232},{24,224},{32,216},{40,208},{48,200},{56,1... | collective-permute-start | bytes 491528 | tf_op jit(solution)/shard_map/ppermute | solution.py:239
  37.3 2.9 %collective-permute-start.5 = (f32[8,40,128]{2,1,0:T(8,128)S(1)}, f32[8,40,128]{2,1,0:T(8,128)S(1)}, u32[]{:S(2)}, u32[]{:S(2)}) collective-permute-start(f32[8,40,128]{2,1,0:T(8,128)S(1)} %get-tuple-element.18), channel_id=1, source_target_pairs={{0,7},{1,6},{2,5},{3,4},{4,3},{5,2},{6,1},{7,0},{8,15},{9,14},{10,... | collective-permute-start | bytes 491528 | tf_op jit(solution)/shard_map/ppermute | solution.py:238
  40.1 2.0 %collective-permute-start.6 = (f32[8,40,128]{2,1,0:T(8,128)S(1)}, f32[8,40,128]{2,1,0:T(8,128)S(1)}, u32[]{:S(2)}, u32[]{:S(2)}) collective-permute-start(f32[8,40,128]{2,1,0:T(8,128)S(1)} %get-tuple-element.19), channel_id=1, source_target_pairs={{0,255},{1,254},{2,253},{3,252},{4,251},{5,250},{6,249},{7,248},{8... | collective-permute-start | bytes 491528 | tf_op jit(solution)/shard_map/ppermute | solution.py:237
  42.2 3.1 %collective-permute-done.4.from_x = f32[8,40,128]{2,1,0:T(8,128)S(1)} collective-permute-done((f32[8,40,128]{2,1,0:T(8,128)S(1)}, f32[8,40,128]{2,1,0:T(8,128)S(1)}, u32[]{:S(2)}, u32[]{:S(2)}) %collective-permute-start.4) | collective-permute-done | bytes 163872 | tf_op jit(solution)/shard_map/ppermute | solution.py:239
  45.2 0.5 collective-permute-done.5.from_y
  45.7 4.6 %collective-permute-done.6.from_xy = f32[8,40,128]{2,1,0:T(8,128)S(1)} collective-permute-done((f32[8,40,128]{2,1,0:T(8,128)S(1)}, f32[8,40,128]{2,1,0:T(8,128)S(1)}, u32[]{:S(2)}, u32[]{:S(2)}) %collective-permute-start.6) | collective-permute-done | bytes 163872 | tf_op jit(solution)/shard_map/ppermute | solution.py:237
  50.3 0.3 shard_map.46.own
  50.6 1.9 %collective-permute-start.8 = (f32[8,32,128]{2,1,0:T(8,128)S(1)}, f32[8,32,128]{2,1,0:T(8,128)S(1)}, u32[]{:S(2)}, u32[]{:S(2)}) collective-permute-start(f32[8,32,128]{2,1,0:T(8,128)S(1)} %shard_map.46.own), channel_id=1, source_target_pairs={{8,16},{16,8},{24,32},{32,24},{40,48},{48,40},{56,64},{64,56},{72,... | collective-permute-start | bytes 393224 | tf_op jit(solution)/shard_map/ppermute | solution.py:269
  52.5 0.1 collective-permute-start.7
  52.6 4.3 %collective-permute-done.8.far = f32[8,32,128]{2,1,0:T(8,128)S(1)} collective-permute-done((f32[8,32,128]{2,1,0:T(8,128)S(1)}, f32[8,32,128]{2,1,0:T(8,128)S(1)}, u32[]{:S(2)}, u32[]{:S(2)}) %collective-permute-start.8) | collective-permute-done | bytes 131104 | tf_op jit(solution)/shard_map/ppermute | solution.py:269
  56.9 0.0 collective-permute-done.7.near
  56.9 0.1 shard_map.47.own
  57.0 6.0 %collective-permute-start.11 = (f32[8,32,128]{2,1,0:T(8,128)S(1)}, f32[8,32,128]{2,1,0:T(8,128)S(1)}, u32[]{:S(2)}, u32[]{:S(2)}) collective-permute-start(f32[8,32,128]{2,1,0:T(8,128)S(1)} %shard_map.47.own), channel_id=1, source_target_pairs={{0,255},{1,254},{2,253},{3,252},{4,251},{5,250},{6,249},{7,248},{8... | collective-permute-start | bytes 393224 | tf_op jit(solution)/shard_map/ppermute | solution.py:237
  63.0 1.0 %collective-permute-start.10 = (f32[8,32,128]{2,1,0:T(8,128)S(1)}, f32[8,32,128]{2,1,0:T(8,128)S(1)}, u32[]{:S(2)}, u32[]{:S(2)}) collective-permute-start(f32[8,32,128]{2,1,0:T(8,128)S(1)} %shard_map.47.own), channel_id=1, source_target_pairs={{0,7},{1,6},{2,5},{3,4},{4,3},{5,2},{6,1},{7,0},{8,15},{9,14},{10,... | collective-permute-start | bytes 393224 | tf_op jit(solution)/shard_map/ppermute | solution.py:238
  64.0 1.1 %collective-permute-start.9 = (f32[8,32,128]{2,1,0:T(8,128)S(1)}, f32[8,32,128]{2,1,0:T(8,128)S(1)}, u32[]{:S(2)}, u32[]{:S(2)}) collective-permute-start(f32[8,32,128]{2,1,0:T(8,128)S(1)} %shard_map.47.own), channel_id=1, source_target_pairs={{0,248},{8,240},{16,232},{24,224},{32,216},{40,208},{48,200},{56,1... | collective-permute-start | bytes 393224 | tf_op jit(solution)/shard_map/ppermute | solution.py:239
  65.1 0.9 %shard_map.45 = f32[8,64,256]{2,1,0:T(8,128)} custom-call(f32[8,64,256]{2,1,0:T(8,128)S(1)} %get-tuple-element.15.tilted), custom_call_target="tpu_custom_call" | custom-call | tf_op jit(solution)/shard_map/pallas_call | solution.py:23
  66.0 3.7 %collective-permute-done.11.from_xy = f32[8,32,128]{2,1,0:T(8,128)S(1)} collective-permute-done((f32[8,32,128]{2,1,0:T(8,128)S(1)}, f32[8,32,128]{2,1,0:T(8,128)S(1)}, u32[]{:S(2)}, u32[]{:S(2)}) %collective-permute-start.11) | collective-permute-done | bytes 131104 | tf_op jit(solution)/shard_map/ppermute | solution.py:237
  69.7 1.0 %collective-permute-done.10.from_y = f32[8,32,128]{2,1,0:T(8,128)S(1)} collective-permute-done((f32[8,32,128]{2,1,0:T(8,128)S(1)}, f32[8,32,128]{2,1,0:T(8,128)S(1)}, u32[]{:S(2)}, u32[]{:S(2)}) %collective-permute-start.10) | collective-permute-done | bytes 131104 | tf_op jit(solution)/shard_map/ppermute | solution.py:238
  70.7 4.0 %collective-permute-done.9.from_x = f32[8,32,128]{2,1,0:T(8,128)S(1)} collective-permute-done((f32[8,32,128]{2,1,0:T(8,128)S(1)}, f32[8,32,128]{2,1,0:T(8,128)S(1)}, u32[]{:S(2)}, u32[]{:S(2)}) %collective-permute-start.9) | collective-permute-done | bytes 131104 | tf_op jit(solution)/shard_map/ppermute | solution.py:239
  74.7 1.3 %shard_map.48 = f32[8,64,256]{2,1,0:T(8,128)} custom-call(f32[8,32,128]{2,1,0:T(8,128)S(1)} %shard_map.47.own, f32[8,32,128]{2,1,0:T(8,128)S(1)} %collective-permute-done.9.from_x, f32[8,32,128]{2,1,0:T(8,128)S(1)} %collective-permute-done.10.from_y, f32[8,32,128]{2,1,0:T(8,128)S(1)} %collective-permute-done.11.from_xy), custom_call_target="tpu_custom_call" | custom-call | tf_op jit(solution)/shard_map/pallas_call | solution.py:23
Async XLA Ops:
  0.6 15.7 %collective-permute-start.1 = (f32[8,64,256]{2,1,0:T(8,128)}, f32[8,64,256]{2,1,0:T(8,128)S(1)}, u32[]{:S(2)}, u32[]{:S(2)}) collective-permute-start(f32[8,64,256]{2,1,0:T(8,128)} %first.1), channel_id=1, source_target_pairs={{0,248},{8,16},{16,8},{24,32},{32,24},{40,48},{48,40},{56,64},{64,... | collective-permute-start | bytes 1572872 | tf_op jit(solution)/shard_map/ppermute | solution.py:248
  3.3 13.0 %collective-permute-start = (f32[8,64,256]{2,1,0:T(8,128)}, f32[8,64,256]{2,1,0:T(8,128)S(1)}, u32[]{:S(2)}, u32[]{:S(2)}) collective-permute-start(f32[8,64,256]{2,1,0:T(8,128)} %first.1), channel_id=1, source_target_pairs={{0,8},{8,0},{16,24},{24,16},{32,40},{40,32},{48,56},{56,48},{64,72... | collective-permute-start | bytes 1572872 | tf_op jit(solution)/shard_map/ppermute | solution.py:249
  8.4 1.0 %copy-start = (f32[8,64,256]{2,1,0:T(8,128)S(1)}, f32[8,64,256]{2,1,0:T(8,128)}, u32[]{:S(2)}) copy-start(f32[8,64,256]{2,1,0:T(8,128)} %second.1) | copy-start | bytes 1572868
  9.5 1.0 %copy-start.1 = (f32[8,64,256]{2,1,0:T(8,128)S(1)}, f32[8,64,256]{2,1,0:T(8,128)}, u32[]{:S(2)}) copy-start(f32[8,64,256]{2,1,0:T(8,128)} %first.1) | copy-start | bytes 1572868
  16.5 8.4 %collective-permute-start.2 = (f32[8,24,256]{2,1,0:T(8,128)S(1)}, f32[8,24,256]{2,1,0:T(8,128)S(1)}, u32[]{:S(2)}, u32[]{:S(2)}) collective-permute-start(f32[8,24,256]{2,1,0:T(8,128)S(1)} %get-tuple-element.13.edge_near), channel_id=1, source_target_pairs={{0,1},{1,0},{2,3},{3,2},{4,5},{5,4},{6,7},{7,6},{8,9},{9,8},{10,11... | collective-permute-start | bytes 589832 | tf_op jit(solution)/shard_map/ppermute | solution.py:255
  20.3 10.9 %collective-permute-start.3 = (f32[8,24,256]{2,1,0:T(8,128)S(1)}, f32[8,24,256]{2,1,0:T(8,128)S(1)}, u32[]{:S(2)}, u32[]{:S(2)}) collective-permute-start(f32[8,24,256]{2,1,0:T(8,128)S(1)} %get-tuple-element.14.edge_far), channel_id=1, source_target_pairs={{0,7},{1,2},{2,1},{3,4},{4,3},{5,6},{6,5},{7,0},{8,15},{9,10},{10,... | collective-permute-start | bytes 589832 | tf_op jit(solution)/shard_map/ppermute | solution.py:254
  32.2 13.0 %collective-permute-start.4 = (f32[8,40,128]{2,1,0:T(8,128)S(1)}, f32[8,40,128]{2,1,0:T(8,128)S(1)}, u32[]{:S(2)}, u32[]{:S(2)}) collective-permute-start(f32[8,40,128]{2,1,0:T(8,128)S(1)} %get-tuple-element.17), channel_id=1, source_target_pairs={{0,248},{8,240},{16,232},{24,224},{32,216},{40,208},{48,200},{56,1... | collective-permute-start | bytes 491528 | tf_op jit(solution)/shard_map/ppermute | solution.py:239
  37.3 8.4 %collective-permute-start.5 = (f32[8,40,128]{2,1,0:T(8,128)S(1)}, f32[8,40,128]{2,1,0:T(8,128)S(1)}, u32[]{:S(2)}, u32[]{:S(2)}) collective-permute-start(f32[8,40,128]{2,1,0:T(8,128)S(1)} %get-tuple-element.18), channel_id=1, source_target_pairs={{0,7},{1,6},{2,5},{3,4},{4,3},{5,2},{6,1},{7,0},{8,15},{9,14},{10,... | collective-permute-start | bytes 491528 | tf_op jit(solution)/shard_map/ppermute | solution.py:238
  40.1 10.2 %collective-permute-start.6 = (f32[8,40,128]{2,1,0:T(8,128)S(1)}, f32[8,40,128]{2,1,0:T(8,128)S(1)}, u32[]{:S(2)}, u32[]{:S(2)}) collective-permute-start(f32[8,40,128]{2,1,0:T(8,128)S(1)} %get-tuple-element.19), channel_id=1, source_target_pairs={{0,255},{1,254},{2,253},{3,252},{4,251},{5,250},{6,249},{7,248},{8... | collective-permute-start | bytes 491528 | tf_op jit(solution)/shard_map/ppermute | solution.py:237
  50.6 6.3 %collective-permute-start.8 = (f32[8,32,128]{2,1,0:T(8,128)S(1)}, f32[8,32,128]{2,1,0:T(8,128)S(1)}, u32[]{:S(2)}, u32[]{:S(2)}) collective-permute-start(f32[8,32,128]{2,1,0:T(8,128)S(1)} %shard_map.46.own), channel_id=1, source_target_pairs={{8,16},{16,8},{24,32},{32,24},{40,48},{48,40},{56,64},{64,56},{72,... | collective-permute-start | bytes 393224 | tf_op jit(solution)/shard_map/ppermute | solution.py:269
  52.5 4.4 %collective-permute-start.7 = (f32[8,32,128]{2,1,0:T(8,128)S(1)}, f32[8,32,128]{2,1,0:T(8,128)S(1)}, u32[]{:S(2)}, u32[]{:S(2)}) collective-permute-start(f32[8,32,128]{2,1,0:T(8,128)S(1)} %shard_map.46.own), channel_id=1, source_target_pairs={{0,8},{8,0},{16,24},{24,16},{32,40},{40,32},{48,56},{56,48},{64,72... | collective-permute-start | bytes 393224 | tf_op jit(solution)/shard_map/ppermute | solution.py:270
  57.0 12.7 %collective-permute-start.11 = (f32[8,32,128]{2,1,0:T(8,128)S(1)}, f32[8,32,128]{2,1,0:T(8,128)S(1)}, u32[]{:S(2)}, u32[]{:S(2)}) collective-permute-start(f32[8,32,128]{2,1,0:T(8,128)S(1)} %shard_map.47.own), channel_id=1, source_target_pairs={{0,255},{1,254},{2,253},{3,252},{4,251},{5,250},{6,249},{7,248},{8... | collective-permute-start | bytes 393224 | tf_op jit(solution)/shard_map/ppermute | solution.py:237
  63.0 7.7 %collective-permute-start.10 = (f32[8,32,128]{2,1,0:T(8,128)S(1)}, f32[8,32,128]{2,1,0:T(8,128)S(1)}, u32[]{:S(2)}, u32[]{:S(2)}) collective-permute-start(f32[8,32,128]{2,1,0:T(8,128)S(1)} %shard_map.47.own), channel_id=1, source_target_pairs={{0,7},{1,6},{2,5},{3,4},{4,3},{5,2},{6,1},{7,0},{8,15},{9,14},{10,... | collective-permute-start | bytes 393224 | tf_op jit(solution)/shard_map/ppermute | solution.py:238
  64.0 10.7 %collective-permute-start.9 = (f32[8,32,128]{2,1,0:T(8,128)S(1)}, f32[8,32,128]{2,1,0:T(8,128)S(1)}, u32[]{:S(2)}, u32[]{:S(2)}) collective-permute-start(f32[8,32,128]{2,1,0:T(8,128)S(1)} %shard_map.47.own), channel_id=1, source_target_pairs={{0,248},{8,240},{16,232},{24,224},{32,216},{40,208},{48,200},{56,1... | collective-permute-start | bytes 393224 | tf_op jit(solution)/shard_map/ppermute | solution.py:239

commit v3 on v2

--- a/solution.py
+++ b/solution.py
@@ -120,6 +120,10 @@
             before.append(b if first is None else jnp.where(first, mine[-1 - p], b))
             after.append(a if last is None else jnp.where(last, mine[-1 - p], a))
         return cone_list(before + mine + after)
+
+    def tilt(total):
+        tilted = jnp.tanh(SHARPNESS * (total * WEIGHT - THRESHOLD))
+        return tilted, (1.0 - tilted * tilted) * (SHARPNESS / SCALE_SUM)
 
     def hold_kernel(first, second, first_out, second_out):
         first_out[...] = first[...]
@@ -140,7 +144,7 @@
         to_near[:, EDGE:] = jnp.where(odd_y, head, tail)
         to_far[:, EDGE:] = jnp.where(odd_y, tail, head)
 
-    def cross_body_kernel(own, near, far, edge_near, edge_far, out, flat):
+    def cross_body_kernel(own, near, far, edge_near, edge_far, sens, outer, tilted_out, chain, middle, flat):
         planes, rows, depth = own.shape
         odd_x = is_odd("gx")
         head, tail = ordered(is_odd("gy"), edge_near[:, :EDGE], edge_far[:, :EDGE])
@@ -152,49 +156,60 @@
             for row in range(EDGE, rows - EDGE, 8):
                 for p, item in enumerate(across(own, near, far, odd_x, row, lanes)):
                     flat[p * rows + row : p * rows + row + 8, lanes] = item
-        out[...] = z_pass(flat[...], 3).reshape(planes, rows, depth)
-
-    def chain_kernel(own, near, far, sens, tilted_out, keep, to_x, to_y, to_xy, halo, ys):
-        planes, rows, depth = own.shape
-        wide = rows + 2 * RADIUS
+        crossed = z_pass(flat[...], 3).reshape(planes, rows, depth)
+        outer[:, :EDGE] = crossed[:, :EDGE]
+        outer[:, EDGE:] = crossed[:, rows - EDGE :]
+        inside = rows - 2 * RADIUS
+        for p in range(planes):
+            tilted, slope = tilt(cone_rows(crossed[p], 0)[:inside])
+            tilted_out[p] = tilted
+            part = sens[p, RADIUS : rows - RADIUS] * slope
+            chain[p] = part
+            middle[p] = cone_rows(part, 0)[: rows - 2 * EDGE]
+
+    def chain_kernel(
+        outer, chain_in, middle, near, far, sens, tilted_out, keep, to_x, to_y, to_xy, halo, ys
+    ):
+        planes, rows, depth = sens.shape
         low, high = ordered(is_odd("gy"), near[...], far[...])
         for p in range(planes):
             halo[2 * EDGE * p : 2 * EDGE * p + EDGE, :] = low[p, :EDGE]
             halo[2 * EDGE * p + EDGE : 2 * EDGE * (p + 1), :] = high[p, :EDGE]
-        outer = z_pass(halo[...], 3).reshape(planes, 2 * EDGE, depth)
-        for p in range(planes):
-            padded = jnp.concatenate([outer[p, :EDGE], own[p], outer[p, EDGE:]], axis=0)
-            ys[p] = cone_rows(padded, 0)[:wide]
-        filtered = ys[...] * WEIGHT
-        tilted = jnp.tanh(SHARPNESS * (filtered - THRESHOLD))
-        tilted_out[...] = tilted[:, RADIUS : RADIUS + rows]
-        slope = (1.0 - tilted * tilted) * (SHARPNESS / SCALE_SUM)
-        chain = jnp.concatenate([low[:, EDGE:], sens[...], high[:, EDGE:]], axis=1) * slope
+        beyond = z_pass(halo[...], 3).reshape(planes, 2 * EDGE, depth)
+        for p in range(planes):
+            top = jnp.concatenate([beyond[p, :EDGE], outer[p, :EDGE]], axis=0)
+            bottom = jnp.concatenate([outer[p, EDGE:], beyond[p, EDGE:]], axis=0)
+            tops, slope_top = tilt(cone_rows(top, 0)[:EDGE])
+            bottoms, slope_bottom = tilt(cone_rows(bottom, 0)[:EDGE])
+            tilted_out[p, :RADIUS] = tops[RADIUS:]
+            tilted_out[p, RADIUS:] = bottoms[:RADIUS]
+            above = jnp.concatenate([low[p, EDGE:], sens[p, :RADIUS]], axis=0) * slope_top
+            below = jnp.concatenate([sens[p, rows - RADIUS :], high[p, EDGE:]], axis=0) * slope_bottom
+            top = jnp.concatenate([above, chain_in[p, :EDGE]], axis=0)
+            bottom = jnp.concatenate([chain_in[p, rows - EDGE - 2 * RADIUS :], below], axis=0)
+            ys[p, :EDGE] = cone_rows(top, 0)[:EDGE]
+            ys[p, EDGE : rows - EDGE] = middle[p]
+            ys[p, rows - EDGE :] = cone_rows(bottom, 0)[:EDGE]
+        chain = ys[...]
         upper_x = lax.axis_index("gx") >= hx
         upper_y = lax.axis_index("gy") >= hy
         near = jnp.where(upper_x, chain[:, :, 128:], chain[:, :, :128])
         far = jnp.where(upper_x, chain[:, :, :128], chain[:, :, 128:])
         for field, even_out, odd_out in ((near, keep, to_y), (far, to_x, to_xy)):
-            top, bottom = field[:, : wide // 2], field[:, wide // 2 :]
+            top, bottom = field[:, : rows // 2], field[:, rows // 2 :]
             mask = first_lanes(top.shape)
             even = jnp.where(mask, top, swap_halves(bottom))
             odd = jnp.where(mask, swap_halves(top), bottom)
             even_out[...] = jnp.where(upper_y, odd, even)
             odd_out[...] = jnp.where(upper_y, even, odd)
 
-    def project_kernel(tilted, projected):
-        projected[...] = (TANH_LOW + tilted[...]) * (1.0 / SCALE_SUM)
-
-    def sum_kernel(keep, from_x, from_y, from_xy, out):
+    def project_kernel(inside, edges, projected):
+        tilted = jnp.concatenate([edges[:, :RADIUS], inside[...], edges[:, RADIUS:]], axis=1)
+        projected[...] = (TANH_LOW + tilted) * (1.0 / SCALE_SUM)
+
+    def sum_kernel(keep, from_x, from_xy, from_y, total):
         other = flip_rows(from_y[...] + flip_planes(from_xy[...]))
-        total = keep[...] + flip_planes(from_x[...]) + other
-        rows = total.shape[1]
-        swapped = swap_halves(total)
-        upper = jnp.concatenate([total, swapped[:, :8]], axis=1)
-        lower = jnp.concatenate([swapped[:, rows - 8 :], total], axis=1)
-        padded = jnp.where(first_lanes(upper.shape), upper, lower)
-        for p in range(total.shape[0]):
-            out[p] = cone_rows(padded[p], 0)[: out.shape[1]]
+        total[...] = keep[...] + flip_planes(from_x[...]) + other
 
     def cross_quarter_kernel(own, near, far, out):
         planes, rows, depth = own.shape
@@ -205,7 +220,7 @@
             for p, item in enumerate(items):
                 out[p, row : row + 8, :] = item
 
-    def finish_kernel(own, from_x, from_y, from_xy, gradient, flat):
+    def finish_kernel(own, from_y, from_xy, from_x, gradient, flat):
         planes, rows, depth = gradient.shape
         upper_x = lax.axis_index("gx") >= hx
         upper_y = lax.axis_index("gy") >= hy
@@ -234,16 +249,15 @@
     mirror_xy = [(i * ny + j, (nx - 1 - i) * ny + ny - 1 - j) for i, j in both]
 
     def mirrors(to_x, to_y, to_xy):
+        from_x = lax.ppermute(to_x, "gx", mirror_x)
         from_xy = lax.ppermute(to_xy, ("gx", "gy"), mirror_xy)
         from_y = lax.ppermute(to_y, "gy", mirror_y)
-        from_x = lax.ppermute(to_x, "gx", mirror_x)
         return from_x, from_y, from_xy
 
     def local(density, sensitivity):
         block = density.shape
         planes, rows, depth = block
         packed = (planes, rows // 2, 128)
-        wide = (planes, rows // 2 + RADIUS, 128)
         flat = pltpu.VMEM((planes * rows, depth), F32)
         far = lax.ppermute(density, "gx", far_x)
         near = lax.ppermute(density, "gx", near_x)
@@ -253,26 +267,34 @@
         )
         from_far = lax.ppermute(to_far, "gy", far_y)
         from_near = lax.ppermute(to_near, "gy", near_y)
-        (crossed,) = run(cross_body_kernel, [block], (own, near, far, to_near, to_far), (flat,))
-        tilted, keep, to_x, to_y, to_xy = run(
+        outer, inside, chain, middle = run(
+            cross_body_kernel,
+            [
+                (planes, 2 * EDGE, depth),
+                (planes, rows - 2 * RADIUS, depth),
+                (planes, rows - 2 * RADIUS, depth),
+                (planes, rows - 2 * EDGE, depth),
+            ],
+            (own, near, far, to_near, to_far, sens),
+            (flat,),
+        )
+        edges, keep, to_x, to_y, to_xy = run(
             chain_kernel,
-            [block, wide, wide, wide, wide],
-            (crossed, from_near, from_far, sens),
-            (
-                pltpu.VMEM((planes * 2 * EDGE, depth), F32),
-                pltpu.VMEM((planes, rows + 2 * RADIUS, depth), F32),
-            ),
-        )
-        from_mirrors = mirrors(to_x, to_y, to_xy)
-        (projected,) = run(project_kernel, [block], (tilted,))
-        (smooth,) = run(sum_kernel, [packed], (keep, *from_mirrors))
-        far = lax.ppermute(smooth, "gx", fold_far_x)
-        near = lax.ppermute(smooth, "gx", near_x)
-        (quarter,) = run(cross_quarter_kernel, [packed], (smooth, near, far))
+            [(planes, 2 * RADIUS, depth), packed, packed, packed, packed],
+            (outer, chain, middle, from_near, from_far, sens),
+            (pltpu.VMEM((planes * 2 * EDGE, depth), F32), pltpu.VMEM(block, F32)),
+        )
+        from_x, from_y, from_xy = mirrors(to_x, to_y, to_xy)
+        (projected,) = run(project_kernel, [block], (inside, edges))
+        (total,) = run(sum_kernel, [packed], (keep, from_x, from_xy, from_y))
+        far = lax.ppermute(total, "gx", fold_far_x)
+        near = lax.ppermute(total, "gx", near_x)
+        (quarter,) = run(cross_quarter_kernel, [packed], (total, near, far))
+        from_x, from_y, from_xy = mirrors(quarter, quarter, quarter)
         (gradient,) = run(
             finish_kernel,
             [block],
-            (quarter, *mirrors(quarter, quarter, quarter)),
+            (quarter, from_y, from_xy, from_x),
             (flat,),
         )
         return projected, gradient

time: 76.2 us -> 73.1 us (0.959)
  waiting for transfers between devices: 34.6 us -> 32.1 us
  starting transfers between devices: 34.2 us -> 33.2 us
    ppermute x2, starting transfers between devices: 7.99 us -> 4.15 us  [mirrors(): from_xy = lax.ppermute(to_xy, ('gx', 'gy'), mirror_xy)]
    ppermute x2, starting transfers between devices: 6.16 us -> 8.46 us  [mirrors(): from_x = lax.ppermute(to_x, 'gx', mirror_x)]
    ppermute x2, waiting for transfers between devices: 7.04 us -> 5.76 us  [mirrors(): from_x = lax.ppermute(to_x, 'gx', mirror_x)]
    ppermute x2, waiting for transfers between devices: 1.47 us -> 0.27 us  [mirrors(): from_y = lax.ppermute(to_y, 'gy', mirror_y)]
  transfers between devices with their start and end apart: 12 -> 12, of which waited for: 10 -> 9; matrix products, arithmetic and copies ran while one was open for 0% -> 0% of each run, Pallas kernels for 2% -> 3%
where the time goes in v3:
time: 73.1 us; the launch traced here: 72.9 us
  starting transfers between devices  33.2 us (45%)
  waiting for transfers between devices  32.1 us (44%)
  Pallas kernels  4.85 us (7%)
  local copies, waits for them, and re-layouts  2.08 us (3%)
    ppermute x2, waiting for transfers between devices, mirrors(): from_xy = lax.ppermute(to_xy, ('gx', 'gy'), mirror_xy)  9.06 us
    ppermute x2, starting transfers between devices, mirrors(): from_x = lax.ppermute(to_x, 'gx', mirror_x)  8.46 us
    ppermute x1, waiting for transfers between devices, local(): from_far = lax.ppermute(to_far, 'gy', far_y)  6.26 us
    ppermute x2, waiting for transfers between devices, mirrors(): from_x = lax.ppermute(to_x, 'gx', mirror_x)  5.76 us
    ppermute x1, waiting for transfers between devices, local(): far = lax.ppermute(density, 'gx', far_x)  5.7 us
    ppermute x1, starting transfers between devices, local(): near = lax.ppermute(density, 'gx', near_x)  5.13 us
    pallas_call x8, Pallas kernels, run(): pl.pallas_call(body, out_shape=[jax.ShapeDtypeStruct(shape, F32) for shap...  4.85 us
    ppermute x2, starting transfers between devices, mirrors(): from_y = lax.ppermute(to_y, 'gy', mirror_y)  4.26 us
  transfers between devices with their start and end apart: 12, of which 9 were waited for; matrix products, arithmetic and copies ran while one was open for 0% of the time, Pallas kernels for 3%

profile of v3, /device:TPU:1, one launch (start us, length us, event | category | flops | bytes accessed | tf_op | source)
XLA Modules:
  0.0 72.9 jit_solution(13479017005577741819)
XLA Ops:
  0.6 2.7 %collective-permute-start.1 = (f32[8,64,256]{2,1,0:T(8,128)}, f32[8,64,256]{2,1,0:T(8,128)S(1)}, u32[]{:S(2)}, u32[]{:S(2)}) collective-permute-start(f32[8,64,256]{2,1,0:T(8,128)} %first.1), channel_id=1, source_target_pairs={{0,248},{8,16},{16,8},{24,32},{32,24},{40,48},{48,40},{56,64},{64,... | collective-permute-start | bytes 1572872 | tf_op jit(solution)/shard_map/ppermute | solution.py:262
  3.3 5.1 %collective-permute-start = (f32[8,64,256]{2,1,0:T(8,128)}, f32[8,64,256]{2,1,0:T(8,128)S(1)}, u32[]{:S(2)}, u32[]{:S(2)}) collective-permute-start(f32[8,64,256]{2,1,0:T(8,128)} %first.1), channel_id=1, source_target_pairs={{0,8},{8,0},{16,24},{24,16},{32,40},{40,32},{48,56},{56,48},{64,72... | collective-permute-start | bytes 1572872 | tf_op jit(solution)/shard_map/ppermute | solution.py:263
  8.4 0.0 copy-start
  8.4 1.0 %copy-done = f32[8,64,256]{2,1,0:T(8,128)S(1)} copy-done((f32[8,64,256]{2,1,0:T(8,128)S(1)}, f32[8,64,256]{2,1,0:T(8,128)}, u32[]{:S(2)}) %copy-start) | copy-done | bytes 524312
  9.5 0.0 copy-start.1
  9.5 1.0 %copy-done.1 = f32[8,64,256]{2,1,0:T(8,128)S(1)} copy-done((f32[8,64,256]{2,1,0:T(8,128)S(1)}, f32[8,64,256]{2,1,0:T(8,128)}, u32[]{:S(2)}) %copy-start.1) | copy-done | bytes 524312
  10.5 0.1 shard_map.41
  10.6 5.7 %collective-permute-done.1.far = f32[8,64,256]{2,1,0:T(8,128)S(1)} collective-permute-done((f32[8,64,256]{2,1,0:T(8,128)}, f32[8,64,256]{2,1,0:T(8,128)S(1)}, u32[]{:S(2)}, u32[]{:S(2)}) %collective-permute-start.1) | collective-permute-done | bytes 524320 | tf_op jit(solution)/shard_map/ppermute | solution.py:262
  16.3 0.0 collective-permute-done.near
  16.3 0.2 shard_map.42
  16.5 3.8 %collective-permute-start.2 = (f32[8,24,256]{2,1,0:T(8,128)S(1)}, f32[8,24,256]{2,1,0:T(8,128)S(1)}, u32[]{:S(2)}, u32[]{:S(2)}) collective-permute-start(f32[8,24,256]{2,1,0:T(8,128)S(1)} %get-tuple-element.17.edge_near), channel_id=1, source_target_pairs={{0,1},{1,0},{2,3},{3,2},{4,5},{5,4},{6,7},{7,6},{8,9},{9,8},{10,11... | collective-permute-start | bytes 589832 | tf_op jit(solution)/shard_map/ppermute | solution.py:269
  20.3 2.6 %collective-permute-start.3 = (f32[8,24,256]{2,1,0:T(8,128)S(1)}, f32[8,24,256]{2,1,0:T(8,128)S(1)}, u32[]{:S(2)}, u32[]{:S(2)}) collective-permute-start(f32[8,24,256]{2,1,0:T(8,128)S(1)} %get-tuple-element.18.edge_far), channel_id=1, source_target_pairs={{0,7},{1,2},{2,1},{3,4},{4,3},{5,6},{6,5},{7,0},{8,15},{9,10},{10,... | collective-permute-start | bytes 589832 | tf_op jit(solution)/shard_map/ppermute | solution.py:268
  22.8 1.1 %shard_map.43 = (f32[8,32,256]{2,1,0:T(8,128)S(1)}, f32[8,48,256]{2,1,0:T(8,128)S(1)}, f32[8,48,256]{2,1,0:T(8,128)S(1)}, f32[8,32,256]{2,1,0:T(8,128)S(1)}) custom-call(f32[8,64,256]{2,1,0:T(8,128)S(1)} %get-tuple-element.15.own, f32[8,64,256]{2,1,0:T(8,128)S(1)} %collective-permute-done.near, f32[8,64,256]{2,1,0:T(8,128)S(1)} %collective-permute-done.1.far, ...), custom_call_target="tpu_custom_call" | custom-call | tf_op jit(solution)/shard_map/pallas_call | solution.py:23
  23.9 1.0 %collective-permute-done.2.near = f32[8,24,256]{2,1,0:T(8,128)S(1)} collective-permute-done((f32[8,24,256]{2,1,0:T(8,128)S(1)}, f32[8,24,256]{2,1,0:T(8,128)S(1)}, u32[]{:S(2)}, u32[]{:S(2)}) %collective-permute-start.2) | collective-permute-done | bytes 196640 | tf_op jit(solution)/shard_map/ppermute | solution.py:269
  24.9 6.3 %collective-permute-done.3.far = f32[8,24,256]{2,1,0:T(8,128)S(1)} collective-permute-done((f32[8,24,256]{2,1,0:T(8,128)S(1)}, f32[8,24,256]{2,1,0:T(8,128)S(1)}, u32[]{:S(2)}, u32[]{:S(2)}) %collective-permute-start.3) | collective-permute-done | bytes 196640 | tf_op jit(solution)/shard_map/ppermute | solution.py:268
  31.2 1.0 %shard_map.44 = (f32[8,16,256]{2,1,0:T(8,128)S(1)}, f32[8,32,128]{2,1,0:T(8,128)S(1)}, f32[8,32,128]{2,1,0:T(8,128)S(1)}, f32[8,32,128]{2,1,0:T(8,128)S(1)}, f32[8,32,128]{2,1,0:T(8,128)S(1)}) custom-call(f32[8,32,256]{2,1,0:T(8,128)S(1)} %get-tuple-element.20.outer, f32[8,48,256]{2,1,0:T(8,128)S(1)} %get-tuple-element.21.chain_in, ...), custom_call_target="tpu_custom_call" | custom-call | tf_op jit(solution)/shard_map/pallas_call | solution.py:23
  32.2 5.0 %collective-permute-start.4 = (f32[8,32,128]{2,1,0:T(8,128)S(1)}, f32[8,32,128]{2,1,0:T(8,128)S(1)}, u32[]{:S(2)}, u32[]{:S(2)}) collective-permute-start(f32[8,32,128]{2,1,0:T(8,128)S(1)} %get-tuple-element.25), channel_id=1, source_target_pairs={{0,248},{8,240},{16,232},{24,224},{32,216},{40,208},{48,200},{56,1... | collective-permute-start | bytes 393224 | tf_op jit(solution)/shard_map/ppermute | solution.py:252
  37.2 1.8 %collective-permute-start.5 = (f32[8,32,128]{2,1,0:T(8,128)S(1)}, f32[8,32,128]{2,1,0:T(8,128)S(1)}, u32[]{:S(2)}, u32[]{:S(2)}) collective-permute-start(f32[8,32,128]{2,1,0:T(8,128)S(1)} %get-tuple-element.26), channel_id=1, source_target_pairs={{0,255},{1,254},{2,253},{3,252},{4,251},{5,250},{6,249},{7,248},{8... | collective-permute-start | bytes 393224 | tf_op jit(solution)/shard_map/ppermute | solution.py:253
  39.0 2.2 %collective-permute-start.6 = (f32[8,32,128]{2,1,0:T(8,128)S(1)}, f32[8,32,128]{2,1,0:T(8,128)S(1)}, u32[]{:S(2)}, u32[]{:S(2)}) collective-permute-start(f32[8,32,128]{2,1,0:T(8,128)S(1)} %get-tuple-element.27), channel_id=1, source_target_pairs={{0,7},{1,6},{2,5},{3,4},{4,3},{5,2},{6,1},{7,0},{8,15},{9,14},{10,... | collective-permute-start | bytes 393224 | tf_op jit(solution)/shard_map/ppermute | solution.py:254
  41.2 2.5 %collective-permute-done.4.from_x = f32[8,32,128]{2,1,0:T(8,128)S(1)} collective-permute-done((f32[8,32,128]{2,1,0:T(8,128)S(1)}, f32[8,32,128]{2,1,0:T(8,128)S(1)}, u32[]{:S(2)}, u32[]{:S(2)}) %collective-permute-start.4) | collective-permute-done | bytes 131104 | tf_op jit(solution)/shard_map/ppermute | solution.py:252
  43.8 4.6 %collective-permute-done.5.from_xy = f32[8,32,128]{2,1,0:T(8,128)S(1)} collective-permute-done((f32[8,32,128]{2,1,0:T(8,128)S(1)}, f32[8,32,128]{2,1,0:T(8,128)S(1)}, u32[]{:S(2)}, u32[]{:S(2)}) %collective-permute-start.5) | collective-permute-done | bytes 131104 | tf_op jit(solution)/shard_map/ppermute | solution.py:253
  48.4 0.0 collective-permute-done.6.from_y
  48.4 0.1 shard_map.46.own
  48.5 2.1 %collective-permute-start.8 = (f32[8,32,128]{2,1,0:T(8,128)S(1)}, f32[8,32,128]{2,1,0:T(8,128)S(1)}, u32[]{:S(2)}, u32[]{:S(2)}) collective-permute-start(f32[8,32,128]{2,1,0:T(8,128)S(1)} %shard_map.46.own), channel_id=1, source_target_pairs={{8,16},{16,8},{24,32},{32,24},{40,48},{48,40},{56,64},{64,56},{72,... | collective-permute-start | bytes 393224 | tf_op jit(solution)/shard_map/ppermute | solution.py:290
  50.6 0.1 collective-permute-start.7
  50.7 4.1 %collective-permute-done.8.far = f32[8,32,128]{2,1,0:T(8,128)S(1)} collective-permute-done((f32[8,32,128]{2,1,0:T(8,128)S(1)}, f32[8,32,128]{2,1,0:T(8,128)S(1)}, u32[]{:S(2)}, u32[]{:S(2)}) %collective-permute-start.8) | collective-permute-done | bytes 131104 | tf_op jit(solution)/shard_map/ppermute | solution.py:290
  54.8 0.0 collective-permute-done.7.near
  54.8 0.1 shard_map.47.own
  54.9 3.4 %collective-permute-start.11 = (f32[8,32,128]{2,1,0:T(8,128)S(1)}, f32[8,32,128]{2,1,0:T(8,128)S(1)}, u32[]{:S(2)}, u32[]{:S(2)}) collective-permute-start(f32[8,32,128]{2,1,0:T(8,128)S(1)} %shard_map.47.own), channel_id=1, source_target_pairs={{0,248},{8,240},{16,232},{24,224},{32,216},{40,208},{48,200},{56,1... | collective-permute-start | bytes 393224 | tf_op jit(solution)/shard_map/ppermute | solution.py:252
  58.3 2.4 %collective-permute-start.10 = (f32[8,32,128]{2,1,0:T(8,128)S(1)}, f32[8,32,128]{2,1,0:T(8,128)S(1)}, u32[]{:S(2)}, u32[]{:S(2)}) collective-permute-start(f32[8,32,128]{2,1,0:T(8,128)S(1)} %shard_map.47.own), channel_id=1, source_target_pairs={{0,255},{1,254},{2,253},{3,252},{4,251},{5,250},{6,249},{7,248},{8... | collective-permute-start | bytes 393224 | tf_op jit(solution)/shard_map/ppermute | solution.py:253
  60.7 2.1 %collective-permute-start.9 = (f32[8,32,128]{2,1,0:T(8,128)S(1)}, f32[8,32,128]{2,1,0:T(8,128)S(1)}, u32[]{:S(2)}, u32[]{:S(2)}) collective-permute-start(f32[8,32,128]{2,1,0:T(8,128)S(1)} %shard_map.47.own), channel_id=1, source_target_pairs={{0,7},{1,6},{2,5},{3,4},{4,3},{5,2},{6,1},{7,0},{8,15},{9,14},{10,... | collective-permute-start | bytes 393224 | tf_op jit(solution)/shard_map/ppermute | solution.py:254
  62.7 0.9 %shard_map.45 = f32[8,64,256]{2,1,0:T(8,128)} custom-call(f32[8,48,256]{2,1,0:T(8,128)S(1)} %get-tuple-element.19.inside, f32[8,16,256]{2,1,0:T(8,128)S(1)} %get-tuple-element.23.edges), custom_call_target="tpu_custom_call" | custom-call | tf_op jit(solution)/shard_map/pallas_call | solution.py:23
  63.6 3.2 %collective-permute-done.11.from_x = f32[8,32,128]{2,1,0:T(8,128)S(1)} collective-permute-done((f32[8,32,128]{2,1,0:T(8,128)S(1)}, f32[8,32,128]{2,1,0:T(8,128)S(1)}, u32[]{:S(2)}, u32[]{:S(2)}) %collective-permute-start.11) | collective-permute-done | bytes 131104 | tf_op jit(solution)/shard_map/ppermute | solution.py:252
  66.8 4.5 %collective-permute-done.10.from_xy = f32[8,32,128]{2,1,0:T(8,128)S(1)} collective-permute-done((f32[8,32,128]{2,1,0:T(8,128)S(1)}, f32[8,32,128]{2,1,0:T(8,128)S(1)}, u32[]{:S(2)}, u32[]{:S(2)}) %collective-permute-start.10) | collective-permute-done | bytes 131104 | tf_op jit(solution)/shard_map/ppermute | solution.py:253
  71.3 0.3 collective-permute-done.9.from_y
  71.6 1.3 %shard_map.48 = f32[8,64,256]{2,1,0:T(8,128)} custom-call(f32[8,32,128]{2,1,0:T(8,128)S(1)} %shard_map.47.own, f32[8,32,128]{2,1,0:T(8,128)S(1)} %collective-permute-done.9.from_y, f32[8,32,128]{2,1,0:T(8,128)S(1)} %collective-permute-done.10.from_xy, f32[8,32,128]{2,1,0:T(8,128)S(1)} %collective-permute-done.11.from_x), custom_call_target="tpu_custom_call" | custom-call | tf_op jit(solution)/shard_map/pallas_call | solution.py:23
Async XLA Ops:
  0.6 15.7 %collective-permute-start.1 = (f32[8,64,256]{2,1,0:T(8,128)}, f32[8,64,256]{2,1,0:T(8,128)S(1)}, u32[]{:S(2)}, u32[]{:S(2)}) collective-permute-start(f32[8,64,256]{2,1,0:T(8,128)} %first.1), channel_id=1, source_target_pairs={{0,248},{8,16},{16,8},{24,32},{32,24},{40,48},{48,40},{56,64},{64,... | collective-permute-start | bytes 1572872 | tf_op jit(solution)/shard_map/ppermute | solution.py:262
  3.3 13.0 %collective-permute-start = (f32[8,64,256]{2,1,0:T(8,128)}, f32[8,64,256]{2,1,0:T(8,128)S(1)}, u32[]{:S(2)}, u32[]{:S(2)}) collective-permute-start(f32[8,64,256]{2,1,0:T(8,128)} %first.1), channel_id=1, source_target_pairs={{0,8},{8,0},{16,24},{24,16},{32,40},{40,32},{48,56},{56,48},{64,72... | collective-permute-start | bytes 1572872 | tf_op jit(solution)/shard_map/ppermute | solution.py:263
  8.4 1.0 %copy-start = (f32[8,64,256]{2,1,0:T(8,128)S(1)}, f32[8,64,256]{2,1,0:T(8,128)}, u32[]{:S(2)}) copy-start(f32[8,64,256]{2,1,0:T(8,128)} %second.1) | copy-start | bytes 1572868
  9.5 1.0 %copy-start.1 = (f32[8,64,256]{2,1,0:T(8,128)S(1)}, f32[8,64,256]{2,1,0:T(8,128)}, u32[]{:S(2)}) copy-start(f32[8,64,256]{2,1,0:T(8,128)} %first.1) | copy-start | bytes 1572868
  16.5 8.4 %collective-permute-start.2 = (f32[8,24,256]{2,1,0:T(8,128)S(1)}, f32[8,24,256]{2,1,0:T(8,128)S(1)}, u32[]{:S(2)}, u32[]{:S(2)}) collective-permute-start(f32[8,24,256]{2,1,0:T(8,128)S(1)} %get-tuple-element.17.edge_near), channel_id=1, source_target_pairs={{0,1},{1,0},{2,3},{3,2},{4,5},{5,4},{6,7},{7,6},{8,9},{9,8},{10,11... | collective-permute-start | bytes 589832 | tf_op jit(solution)/shard_map/ppermute | solution.py:269
  20.3 10.9 %collective-permute-start.3 = (f32[8,24,256]{2,1,0:T(8,128)S(1)}, f32[8,24,256]{2,1,0:T(8,128)S(1)}, u32[]{:S(2)}, u32[]{:S(2)}) collective-permute-start(f32[8,24,256]{2,1,0:T(8,128)S(1)} %get-tuple-element.18.edge_far), channel_id=1, source_target_pairs={{0,7},{1,2},{2,1},{3,4},{4,3},{5,6},{6,5},{7,0},{8,15},{9,10},{10,... | collective-permute-start | bytes 589832 | tf_op jit(solution)/shard_map/ppermute | solution.py:268
  32.2 11.6 %collective-permute-start.4 = (f32[8,32,128]{2,1,0:T(8,128)S(1)}, f32[8,32,128]{2,1,0:T(8,128)S(1)}, u32[]{:S(2)}, u32[]{:S(2)}) collective-permute-start(f32[8,32,128]{2,1,0:T(8,128)S(1)} %get-tuple-element.25), channel_id=1, source_target_pairs={{0,248},{8,240},{16,232},{24,224},{32,216},{40,208},{48,200},{56,1... | collective-permute-start | bytes 393224 | tf_op jit(solution)/shard_map/ppermute | solution.py:252
  37.2 11.1 %collective-permute-start.5 = (f32[8,32,128]{2,1,0:T(8,128)S(1)}, f32[8,32,128]{2,1,0:T(8,128)S(1)}, u32[]{:S(2)}, u32[]{:S(2)}) collective-permute-start(f32[8,32,128]{2,1,0:T(8,128)S(1)} %get-tuple-element.26), channel_id=1, source_target_pairs={{0,255},{1,254},{2,253},{3,252},{4,251},{5,250},{6,249},{7,248},{8... | collective-permute-start | bytes 393224 | tf_op jit(solution)/shard_map/ppermute | solution.py:253
  39.0 9.3 %collective-permute-start.6 = (f32[8,32,128]{2,1,0:T(8,128)S(1)}, f32[8,32,128]{2,1,0:T(8,128)S(1)}, u32[]{:S(2)}, u32[]{:S(2)}) collective-permute-start(f32[8,32,128]{2,1,0:T(8,128)S(1)} %get-tuple-element.27), channel_id=1, source_target_pairs={{0,7},{1,6},{2,5},{3,4},{4,3},{5,2},{6,1},{7,0},{8,15},{9,14},{10,... | collective-permute-start | bytes 393224 | tf_op jit(solution)/shard_map/ppermute | solution.py:254
  48.5 6.3 %collective-permute-start.8 = (f32[8,32,128]{2,1,0:T(8,128)S(1)}, f32[8,32,128]{2,1,0:T(8,128)S(1)}, u32[]{:S(2)}, u32[]{:S(2)}) collective-permute-start(f32[8,32,128]{2,1,0:T(8,128)S(1)} %shard_map.46.own), channel_id=1, source_target_pairs={{8,16},{16,8},{24,32},{32,24},{40,48},{48,40},{56,64},{64,56},{72,... | collective-permute-start | bytes 393224 | tf_op jit(solution)/shard_map/ppermute | solution.py:290
  50.6 4.2 %collective-permute-start.7 = (f32[8,32,128]{2,1,0:T(8,128)S(1)}, f32[8,32,128]{2,1,0:T(8,128)S(1)}, u32[]{:S(2)}, u32[]{:S(2)}) collective-permute-start(f32[8,32,128]{2,1,0:T(8,128)S(1)} %shard_map.46.own), channel_id=1, source_target_pairs={{0,8},{8,0},{16,24},{24,16},{32,40},{40,32},{48,56},{56,48},{64,72... | collective-permute-start | bytes 393224 | tf_op jit(solution)/shard_map/ppermute | solution.py:291
  54.9 11.9 %collective-permute-start.11 = (f32[8,32,128]{2,1,0:T(8,128)S(1)}, f32[8,32,128]{2,1,0:T(8,128)S(1)}, u32[]{:S(2)}, u32[]{:S(2)}) collective-permute-start(f32[8,32,128]{2,1,0:T(8,128)S(1)} %shard_map.47.own), channel_id=1, source_target_pairs={{0,248},{8,240},{16,232},{24,224},{32,216},{40,208},{48,200},{56,1... | collective-permute-start | bytes 393224 | tf_op jit(solution)/shard_map/ppermute | solution.py:252
  58.3 13.0 %collective-permute-start.10 = (f32[8,32,128]{2,1,0:T(8,128)S(1)}, f32[8,32,128]{2,1,0:T(8,128)S(1)}, u32[]{:S(2)}, u32[]{:S(2)}) collective-permute-start(f32[8,32,128]{2,1,0:T(8,128)S(1)} %shard_map.47.own), channel_id=1, source_target_pairs={{0,255},{1,254},{2,253},{3,252},{4,251},{5,250},{6,249},{7,248},{8... | collective-permute-start | bytes 393224 | tf_op jit(solution)/shard_map/ppermute | solution.py:253
  60.7 10.9 %collective-permute-start.9 = (f32[8,32,128]{2,1,0:T(8,128)S(1)}, f32[8,32,128]{2,1,0:T(8,128)S(1)}, u32[]{:S(2)}, u32[]{:S(2)}) collective-permute-start(f32[8,32,128]{2,1,0:T(8,128)S(1)} %shard_map.47.own), channel_id=1, source_target_pairs={{0,7},{1,6},{2,5},{3,4},{4,3},{5,2},{6,1},{7,0},{8,15},{9,14},{10,... | collective-permute-start | bytes 393224 | tf_op jit(solution)/shard_map/ppermute | solution.py:254

commit v4 on v3

--- a/solution.py
+++ b/solution.py
@@ -15,7 +15,6 @@
 TANH_LOW = math.tanh(SHARPNESS * THRESHOLD)
 SCALE_SUM = TANH_LOW + math.tanh(SHARPNESS * (1.0 - THRESHOLD))
 WEIGHT = 1.0 / float(WIDTH**6)
-HALF = 64
 F32 = jnp.float32
 
 
@@ -66,23 +65,14 @@
     return field
 
 
-def swap_halves(field):
-    return pltpu.roll(field, HALF, field.ndim - 1)
-
-
 def flip_planes(field):
     return jnp.stack([field[p] for p in reversed(range(field.shape[0]))])
 
 
 def flip_rows(field):
     field = reverse_eights(field, 1)
-    rows = field.shape[1]
-    groups = [field[:, r : r + 8] for r in range(0, rows, 8)]
-    return swap_halves(jnp.concatenate(groups[::-1], axis=1))
-
-
-def first_lanes(shape):
-    return lax.broadcasted_iota(jnp.int32, shape, len(shape) - 1) < HALF
+    groups = [field[:, r : r + 8] for r in range(0, field.shape[1], 8)]
+    return jnp.concatenate(groups[::-1], axis=1)
 
 
 def z_pass(field, pieces):
@@ -124,6 +114,12 @@
     def tilt(total):
         tilted = jnp.tanh(SHARPNESS * (total * WEIGHT - THRESHOLD))
         return tilted, (1.0 - tilted * tilted) * (SHARPNESS / SCALE_SUM)
+
+    def halves(field):
+        half = field.shape[-1] // 2
+        upper = lax.axis_index("gy") >= hy
+        low, high = field[..., :half], field[..., half:]
+        return jnp.where(upper, high, low), jnp.where(upper, low, high)
 
     def hold_kernel(first, second, first_out, second_out):
         first_out[...] = first[...]
@@ -144,7 +140,7 @@
         to_near[:, EDGE:] = jnp.where(odd_y, head, tail)
         to_far[:, EDGE:] = jnp.where(odd_y, tail, head)
 
-    def cross_body_kernel(own, near, far, edge_near, edge_far, sens, outer, tilted_out, chain, middle, flat):
+    def cross_body_kernel(own, near, far, edge_near, edge_far, sens, outer, tilted_out, chain, keep, send, flat, middle):
         planes, rows, depth = own.shape
         odd_x = is_odd("gx")
         head, tail = ordered(is_odd("gy"), edge_near[:, :EDGE], edge_far[:, :EDGE])
@@ -166,10 +162,9 @@
             part = sens[p, RADIUS : rows - RADIUS] * slope
             chain[p] = part
             middle[p] = cone_rows(part, 0)[: rows - 2 * EDGE]
-
-    def chain_kernel(
-        outer, chain_in, middle, near, far, sens, tilted_out, keep, to_x, to_y, to_xy, halo, ys
-    ):
+        keep[...], send[...] = halves(middle[...])
+
+    def chain_kernel(outer, chain_in, near, far, sens, tilted_out, keep, send, halo, ys):
         planes, rows, depth = sens.shape
         low, high = ordered(is_odd("gy"), near[...], far[...])
         for p in range(planes):
@@ -188,30 +183,20 @@
             top = jnp.concatenate([above, chain_in[p, :EDGE]], axis=0)
             bottom = jnp.concatenate([chain_in[p, rows - EDGE - 2 * RADIUS :], below], axis=0)
             ys[p, :EDGE] = cone_rows(top, 0)[:EDGE]
-            ys[p, EDGE : rows - EDGE] = middle[p]
-            ys[p, rows - EDGE :] = cone_rows(bottom, 0)[:EDGE]
-        chain = ys[...]
-        upper_x = lax.axis_index("gx") >= hx
-        upper_y = lax.axis_index("gy") >= hy
-        near = jnp.where(upper_x, chain[:, :, 128:], chain[:, :, :128])
-        far = jnp.where(upper_x, chain[:, :, :128], chain[:, :, 128:])
-        for field, even_out, odd_out in ((near, keep, to_y), (far, to_x, to_xy)):
-            top, bottom = field[:, : rows // 2], field[:, rows // 2 :]
-            mask = first_lanes(top.shape)
-            even = jnp.where(mask, top, swap_halves(bottom))
-            odd = jnp.where(mask, swap_halves(top), bottom)
-            even_out[...] = jnp.where(upper_y, odd, even)
-            odd_out[...] = jnp.where(upper_y, even, odd)
+            ys[p, EDGE:] = cone_rows(bottom, 0)[:EDGE]
+        keep[...], send[...] = halves(ys[...])
 
     def project_kernel(inside, edges, projected):
         tilted = jnp.concatenate([edges[:, :RADIUS], inside[...], edges[:, RADIUS:]], axis=1)
         projected[...] = (TANH_LOW + tilted) * (1.0 / SCALE_SUM)
 
-    def sum_kernel(keep, from_x, from_xy, from_y, total):
-        other = flip_rows(from_y[...] + flip_planes(from_xy[...]))
-        total[...] = keep[...] + flip_planes(from_x[...]) + other
-
-    def cross_quarter_kernel(own, near, far, out):
+    def sum_y_kernel(own, from_y, total):
+        total[...] = own[...] + flip_rows(from_y[...])
+
+    def sum_x_kernel(own, from_x, total):
+        total[...] = own[...] + flip_planes(from_x[...])
+
+    def cross_part_kernel(own, near, far, out):
         planes, rows, depth = own.shape
         place = lax.rem(lax.axis_index("gx"), hx)
         first, last = place == 0, place == hx - 1
@@ -220,25 +205,20 @@
             for p, item in enumerate(items):
                 out[p, row : row + 8, :] = item
 
-    def finish_kernel(own, from_y, from_xy, from_x, gradient, flat):
+    def finish_kernel(inner, outer, from_inner, from_outer, gradient, flat):
         planes, rows, depth = gradient.shape
-        upper_x = lax.axis_index("gx") >= hx
-        upper_y = lax.axis_index("gy") >= hy
-        near_own, near_y = own[...], flip_rows(from_y[...])
-        far_x, far_xy = flip_planes(from_x[...]), flip_rows(flip_planes(from_xy[...]))
-        sides = []
-        for mine, other in ((near_own, near_y), (far_x, far_xy)):
-            even, odd = jnp.where(upper_y, other, mine), jnp.where(upper_y, mine, other)
-            mask = first_lanes(even.shape)
-            top = jnp.where(mask, even, swap_halves(odd))
-            bottom = jnp.where(mask, swap_halves(even), odd)
-            sides.append(jnp.concatenate([top, bottom], axis=1).reshape(planes * rows, 128))
-        near, far = sides
-        flat[:, :128] = jnp.where(upper_x, far, near)
-        flat[:, 128:] = jnp.where(upper_x, near, far)
+        upper = lax.axis_index("gy") >= hy
+
+        def whole(inner, outer):
+            lines = jnp.concatenate([outer[:, :EDGE], inner, outer[:, EDGE:]], axis=1)
+            return lines.reshape(planes * rows, depth // 2)
+
+        mine = whole(inner[...], outer[...])
+        other = whole(flip_rows(from_inner[...]), flip_rows(from_outer[...]))
+        flat[:, : depth // 2] = jnp.where(upper, other, mine)
+        flat[:, depth // 2 :] = jnp.where(upper, mine, other)
         gradient[...] = (z_pass(flat[...], 2) * (0.25 * WEIGHT)).reshape(planes, rows, depth)
 
-    both = [(i, j) for i in range(nx) for j in range(ny)]
     near_x = [(i, i ^ 1) for i in range(nx)]
     near_y = [(j, j ^ 1) for j in range(ny)]
     far_x = [(i, (i + (1 if i % 2 else -1)) % nx) for i in range(nx)]
@@ -246,18 +226,20 @@
     fold_far_x = [(a, b) for a, b in far_x if a // hx == b // hx and abs(a - b) == 1]
     mirror_x = [(i, nx - 1 - i) for i in range(nx)]
     mirror_y = [(j, ny - 1 - j) for j in range(ny)]
-    mirror_xy = [(i * ny + j, (nx - 1 - i) * ny + ny - 1 - j) for i, j in both]
-
-    def mirrors(to_x, to_y, to_xy):
-        from_x = lax.ppermute(to_x, "gx", mirror_x)
-        from_xy = lax.ppermute(to_xy, ("gx", "gy"), mirror_xy)
-        from_y = lax.ppermute(to_y, "gy", mirror_y)
-        return from_x, from_y, from_xy
+
+    def symmetrized(keep, send):
+        part = keep.shape
+        (total,) = run(sum_y_kernel, [part], (keep, lax.ppermute(send, "gy", mirror_y)))
+        (total,) = run(sum_x_kernel, [part], (total, lax.ppermute(total, "gx", mirror_x)))
+        far = lax.ppermute(total, "gx", fold_far_x)
+        near = lax.ppermute(total, "gx", near_x)
+        (smooth,) = run(cross_part_kernel, [part], (total, near, far))
+        return smooth, lax.ppermute(smooth, "gy", mirror_y)
 
     def local(density, sensitivity):
         block = density.shape
         planes, rows, depth = block
-        packed = (planes, rows // 2, 128)
+        part = (planes, rows // 2, depth // 2)
         flat = pltpu.VMEM((planes * rows, depth), F32)
         far = lax.ppermute(density, "gx", far_x)
         near = lax.ppermute(density, "gx", near_x)
@@ -267,36 +249,28 @@
         )
         from_far = lax.ppermute(to_far, "gy", far_y)
         from_near = lax.ppermute(to_near, "gy", near_y)
-        outer, inside, chain, middle = run(
+        outer, inside, chain, *inner = run(
             cross_body_kernel,
             [
                 (planes, 2 * EDGE, depth),
                 (planes, rows - 2 * RADIUS, depth),
                 (planes, rows - 2 * RADIUS, depth),
-                (planes, rows - 2 * EDGE, depth),
+                part,
+                part,
             ],
             (own, near, far, to_near, to_far, sens),
-            (flat,),
-        )
-        edges, keep, to_x, to_y, to_xy = run(
+            (flat, pltpu.VMEM((planes, rows - 2 * EDGE, depth), F32)),
+        )
+        edges, *outer = run(
             chain_kernel,
-            [(planes, 2 * RADIUS, depth), packed, packed, packed, packed],
-            (outer, chain, middle, from_near, from_far, sens),
-            (pltpu.VMEM((planes * 2 * EDGE, depth), F32), pltpu.VMEM(block, F32)),
-        )
-        from_x, from_y, from_xy = mirrors(to_x, to_y, to_xy)
+            [(planes, 2 * RADIUS, depth), part, part],
+            (outer, chain, from_near, from_far, sens),
+            (pltpu.VMEM((planes * 2 * EDGE, depth), F32), pltpu.VMEM((planes, 2 * EDGE, depth), F32)),
+        )
         (projected,) = run(project_kernel, [block], (inside, edges))
-        (total,) = run(sum_kernel, [packed], (keep, from_x, from_xy, from_y))
-        far = lax.ppermute(total, "gx", fold_far_x)
-        near = lax.ppermute(total, "gx", near_x)
-        (quarter,) = run(cross_quarter_kernel, [packed], (total, near, far))
-        from_x, from_y, from_xy = mirrors(quarter, quarter, quarter)
-        (gradient,) = run(
-            finish_kernel,
-            [block],
-            (quarter, from_y, from_xy, from_x),
-            (flat,),
-        )
+        inner, from_inner = symmetrized(*inner)
+        outer, from_outer = symmetrized(*outer)
+        (gradient,) = run(finish_kernel, [block], (inner, outer, from_inner, from_outer), (flat,))
         return projected, gradient
 
     return jax.shard_map(

time: 73.1 us -> 67.8 us (0.927)
  waiting for transfers between devices: 32.1 us -> 19.6 us
  starting transfers between devices: 33.2 us -> 39.8 us
    ppermute x8 -> x10, waiting for transfers between devices: 19.2 us -> 8.07 us  [the longest x2 4.12 us: symmetrized(): return (smooth, lax.ppermute(smooth, 'gy', mirror_y))]
    ppermute x8 -> x10, starting transfers between devices: 19 us -> 25.7 us  [the longest x2 9.8 us: symmetrized(): lax.ppermute(total, 'gx', mirror_x)]
    ppermute x1, waiting for transfers between devices: 0.95 us -> 0.01 us  [local(): from_near = lax.ppermute(to_near, 'gy', near_y)]
    pallas_call x8 -> x12, Pallas kernels: 4.85 us -> 4.77 us  [run(): pl.pallas_call(body, out_shape=[jax.ShapeDtypeStruct(shape, F32) for shap...]
  transfers between devices with their start and end apart: 12 -> 14, of which waited for: 9 -> 8; matrix products, arithmetic and copies ran while one was open for 0% -> 0% of each run, Pallas kernels for 3% -> 5%
where the time goes in v4:
time: 67.8 us; the launch traced here: 67 us
  starting transfers between devices  39.8 us (59%)
  waiting for transfers between devices  19.6 us (29%)
  Pallas kernels  4.77 us (7%)
  local copies, waits for them, and re-layouts  2.08 us (3%)
  between operations  0.72 us (1%)
    ppermute x2, starting transfers between devices, symmetrized(): lax.ppermute(total, 'gx', mirror_x)  9.8 us
    ppermute x2, starting transfers between devices, symmetrized(): return (smooth, lax.ppermute(smooth, 'gy', mirror_y))  6.68 us
    ppermute x1, waiting for transfers between devices, local(): from_far = lax.ppermute(to_far, 'gy', far_y)  5.81 us
    ppermute x1, waiting for transfers between devices, local(): far = lax.ppermute(density, 'gx', far_x)  5.7 us
    ppermute x1, starting transfers between devices, local(): near = lax.ppermute(density, 'gx', near_x)  5.13 us
    ppermute x2, starting transfers between devices, symmetrized(): lax.ppermute(send, 'gy', mirror_y)  4.78 us
    pallas_call x12, Pallas kernels, run(): pl.pallas_call(body, out_shape=[jax.ShapeDtypeStruct(shape, F32) for shap...  4.77 us
    ppermute x2, starting transfers between devices, symmetrized(): far = lax.ppermute(total, 'gx', fold_far_x)  4.24 us
  transfers between devices with their start and end apart: 14, of which 8 were waited for; matrix products, arithmetic and copies ran while one was open for 0% of the time, Pallas kernels for 5%

profile of v4, /device:TPU:1, one launch (start us, length us, event | category | flops | bytes accessed | tf_op | source)
XLA Modules:
  0.0 67.0 jit_solution(11526923861399340994)
XLA Ops:
  0.6 2.7 %collective-permute-start.1 = (f32[8,64,256]{2,1,0:T(8,128)}, f32[8,64,256]{2,1,0:T(8,128)S(1)}, u32[]{:S(2)}, u32[]{:S(2)}) collective-permute-start(f32[8,64,256]{2,1,0:T(8,128)} %first.1), channel_id=1, source_target_pairs={{0,248},{8,16},{16,8},{24,32},{32,24},{40,48},{48,40},{56,64},{64,... | collective-permute-start | bytes 1572872 | tf_op jit(solution)/shard_map/ppermute | solution.py:244
  3.3 5.1 %collective-permute-start = (f32[8,64,256]{2,1,0:T(8,128)}, f32[8,64,256]{2,1,0:T(8,128)S(1)}, u32[]{:S(2)}, u32[]{:S(2)}) collective-permute-start(f32[8,64,256]{2,1,0:T(8,128)} %first.1), channel_id=1, source_target_pairs={{0,8},{8,0},{16,24},{24,16},{32,40},{40,32},{48,56},{56,48},{64,72... | collective-permute-start | bytes 1572872 | tf_op jit(solution)/shard_map/ppermute | solution.py:245
  8.4 0.0 copy-start
  8.4 1.0 %copy-done = f32[8,64,256]{2,1,0:T(8,128)S(1)} copy-done((f32[8,64,256]{2,1,0:T(8,128)S(1)}, f32[8,64,256]{2,1,0:T(8,128)}, u32[]{:S(2)}) %copy-start) | copy-done | bytes 524312
  9.5 0.0 copy-start.1
  9.5 1.0 %copy-done.1 = f32[8,64,256]{2,1,0:T(8,128)S(1)} copy-done((f32[8,64,256]{2,1,0:T(8,128)S(1)}, f32[8,64,256]{2,1,0:T(8,128)}, u32[]{:S(2)}) %copy-start.1) | copy-done | bytes 524312
  10.5 0.1 shard_map.41
  10.6 5.7 %collective-permute-done.1.far = f32[8,64,256]{2,1,0:T(8,128)S(1)} collective-permute-done((f32[8,64,256]{2,1,0:T(8,128)}, f32[8,64,256]{2,1,0:T(8,128)S(1)}, u32[]{:S(2)}, u32[]{:S(2)}) %collective-permute-start.1) | collective-permute-done | bytes 524320 | tf_op jit(solution)/shard_map/ppermute | solution.py:244
  16.3 0.0 collective-permute-done.near
  16.3 0.2 shard_map.42
  16.5 3.8 %collective-permute-start.2 = (f32[8,24,256]{2,1,0:T(8,128)S(1)}, f32[8,24,256]{2,1,0:T(8,128)S(1)}, u32[]{:S(2)}, u32[]{:S(2)}) collective-permute-start(f32[8,24,256]{2,1,0:T(8,128)S(1)} %get-tuple-element.16.edge_near), channel_id=1, source_target_pairs={{0,1},{1,0},{2,3},{3,2},{4,5},{5,4},{6,7},{7,6},{8,9},{9,8},{10,11... | collective-permute-start | bytes 589832 | tf_op jit(solution)/shard_map/ppermute | solution.py:251
  20.3 2.6 %collective-permute-start.3 = (f32[8,24,256]{2,1,0:T(8,128)S(1)}, f32[8,24,256]{2,1,0:T(8,128)S(1)}, u32[]{:S(2)}, u32[]{:S(2)}) collective-permute-start(f32[8,24,256]{2,1,0:T(8,128)S(1)} %get-tuple-element.17.edge_far), channel_id=1, source_target_pairs={{0,7},{1,2},{2,1},{3,4},{4,3},{5,6},{6,5},{7,0},{8,15},{9,10},{10,... | collective-permute-start | bytes 589832 | tf_op jit(solution)/shard_map/ppermute | solution.py:250
  22.8 1.1 %shard_map.43 = (f32[8,32,256]{2,1,0:T(8,128)S(1)}, f32[8,48,256]{2,1,0:T(8,128)S(1)}, f32[8,48,256]{2,1,0:T(8,128)S(1)}, f32[8,32,128]{2,1,0:T(8,128)S(1)}, f32[8,32,128]{2,1,0:T(8,128)S(1)}) custom-call(f32[8,64,256]{2,1,0:T(8,128)S(1)} %get-tuple-element.14.own, f32[8,64,256]{2,1,0:T(8,128)S(1)} %collective-permute-done.near, ...), custom_call_target="tpu_custom_call" | custom-call | tf_op jit(solution)/shard_map/pallas_call | solution.py:22
  24.0 2.6 %collective-permute-start.4 = (f32[8,32,128]{2,1,0:T(8,128)S(1)}, f32[8,32,128]{2,1,0:T(8,128)S(1)}, u32[]{:S(2)}, u32[]{:S(2)}) collective-permute-start(f32[8,32,128]{2,1,0:T(8,128)S(1)} %get-tuple-element.23), channel_id=1, source_target_pairs={{0,7},{1,6},{2,5},{3,4},{4,3},{5,2},{6,1},{7,0},{8,15},{9,14},{10,... | collective-permute-start | bytes 393224 | tf_op jit(solution)/shard_map/ppermute | solution.py:232
  26.6 0.0 collective-permute-done.2.near
  26.6 5.8 %collective-permute-done.3.far = f32[8,24,256]{2,1,0:T(8,128)S(1)} collective-permute-done((f32[8,24,256]{2,1,0:T(8,128)S(1)}, f32[8,24,256]{2,1,0:T(8,128)S(1)}, u32[]{:S(2)}, u32[]{:S(2)}) %collective-permute-start.3) | collective-permute-done | bytes 196640 | tf_op jit(solution)/shard_map/ppermute | solution.py:250
  32.4 1.0 %shard_map.44 = (f32[8,16,256]{2,1,0:T(8,128)S(1)}, f32[8,32,128]{2,1,0:T(8,128)S(1)}, f32[8,32,128]{2,1,0:T(8,128)S(1)}) custom-call(f32[8,32,256]{2,1,0:T(8,128)S(1)} %get-tuple-element.19.outer, f32[8,48,256]{2,1,0:T(8,128)S(1)} %get-tuple-element.20.chain_in, f32[8,24,256]{2,1,0:T(8,128)S(1)} %collective-permute-done.2.near, ...), custom_call_target="tpu_custom_call" | custom-call | tf_op jit(solution)/shard_map/pallas_call | solution.py:22
  33.4 2.2 %collective-permute-start.8 = (f32[8,32,128]{2,1,0:T(8,128)S(1)}, f32[8,32,128]{2,1,0:T(8,128)S(1)}, u32[]{:S(2)}, u32[]{:S(2)}) collective-permute-start(f32[8,32,128]{2,1,0:T(8,128)S(1)} %get-tuple-element.25), channel_id=1, source_target_pairs={{0,7},{1,6},{2,5},{3,4},{4,3},{5,2},{6,1},{7,0},{8,15},{9,14},{10,... | collective-permute-start | bytes 393224 | tf_op jit(solution)/shard_map/ppermute | solution.py:232
  35.5 0.0 collective-permute-done.4.from_y
  35.5 0.1 shard_map.46.own
  35.6 5.3 %collective-permute-start.5 = (f32[8,32,128]{2,1,0:T(8,128)S(1)}, f32[8,32,128]{2,1,0:T(8,128)S(1)}, u32[]{:S(2)}, u32[]{:S(2)}) collective-permute-start(f32[8,32,128]{2,1,0:T(8,128)S(1)} %shard_map.46.own), channel_id=1, source_target_pairs={{0,248},{8,240},{16,232},{24,224},{32,216},{40,208},{48,200},{56,1... | collective-permute-start | bytes 393224 | tf_op jit(solution)/shard_map/ppermute | solution.py:233
  40.8 1.8 %collective-permute-done.8.from_y = f32[8,32,128]{2,1,0:T(8,128)S(1)} collective-permute-done((f32[8,32,128]{2,1,0:T(8,128)S(1)}, f32[8,32,128]{2,1,0:T(8,128)S(1)}, u32[]{:S(2)}, u32[]{:S(2)}) %collective-permute-start.8) | collective-permute-done | bytes 131104 | tf_op jit(solution)/shard_map/ppermute | solution.py:232
  42.7 0.1 shard_map.49.own
  42.7 4.5 %collective-permute-start.9 = (f32[8,32,128]{2,1,0:T(8,128)S(1)}, f32[8,32,128]{2,1,0:T(8,128)S(1)}, u32[]{:S(2)}, u32[]{:S(2)}) collective-permute-start(f32[8,32,128]{2,1,0:T(8,128)S(1)} %shard_map.49.own), channel_id=1, source_target_pairs={{0,248},{8,240},{16,232},{24,224},{32,216},{40,208},{48,200},{56,1... | collective-permute-start | bytes 393224 | tf_op jit(solution)/shard_map/ppermute | solution.py:233
  47.3 0.0 collective-permute-done.5.from_x
  47.3 1.9 %collective-permute-start.7 = (f32[8,32,128]{2,1,0:T(8,128)S(1)}, f32[8,32,128]{2,1,0:T(8,128)S(1)}, u32[]{:S(2)}, u32[]{:S(2)}) collective-permute-start(f32[8,32,128]{2,1,0:T(8,128)S(1)} %shard_map.47.own), channel_id=1, source_target_pairs={{8,16},{16,8},{24,32},{32,24},{40,48},{48,40},{56,64},{64,56},{72,... | collective-permute-start | bytes 393224 | tf_op jit(solution)/shard_map/ppermute | solution.py:234
  49.3 0.1 collective-permute-start.6
  49.4 1.4 %collective-permute-done.9.from_x = f32[8,32,128]{2,1,0:T(8,128)S(1)} collective-permute-done((f32[8,32,128]{2,1,0:T(8,128)S(1)}, f32[8,32,128]{2,1,0:T(8,128)S(1)}, u32[]{:S(2)}, u32[]{:S(2)}) %collective-permute-start.9) | collective-permute-done | bytes 131104 | tf_op jit(solution)/shard_map/ppermute | solution.py:233
  50.8 2.3 %collective-permute-start.11 = (f32[8,32,128]{2,1,0:T(8,128)S(1)}, f32[8,32,128]{2,1,0:T(8,128)S(1)}, u32[]{:S(2)}, u32[]{:S(2)}) collective-permute-start(f32[8,32,128]{2,1,0:T(8,128)S(1)} %shard_map.50.own), channel_id=1, source_target_pairs={{8,16},{16,8},{24,32},{32,24},{40,48},{48,40},{56,64},{64,56},{72,... | collective-permute-start | bytes 393224 | tf_op jit(solution)/shard_map/ppermute | solution.py:234
  53.1 0.1 collective-permute-start.10
  53.2 0.4 collective-permute-done.7.far
  53.6 0.0 collective-permute-done.6.near
  53.6 0.1 shard_map.48.inner
  53.7 3.1 %collective-permute-start.12 = (f32[8,32,128]{2,1,0:T(8,128)S(1)}, f32[8,32,128]{2,1,0:T(8,128)S(1)}, u32[]{:S(2)}, u32[]{:S(2)}) collective-permute-start(f32[8,32,128]{2,1,0:T(8,128)S(1)} %shard_map.48.inner), channel_id=1, source_target_pairs={{0,7},{1,6},{2,5},{3,4},{4,3},{5,2},{6,1},{7,0},{8,15},{9,14},{10,... | collective-permute-start | bytes 393224 | tf_op jit(solution)/shard_map/ppermute | solution.py:237
  56.8 0.3 collective-permute-done.11.far
  57.1 0.0 collective-permute-done.10.near
  57.1 0.1 shard_map.51.outer
  57.2 3.6 %collective-permute-start.13 = (f32[8,32,128]{2,1,0:T(8,128)S(1)}, f32[8,32,128]{2,1,0:T(8,128)S(1)}, u32[]{:S(2)}, u32[]{:S(2)}) collective-permute-start(f32[8,32,128]{2,1,0:T(8,128)S(1)} %shard_map.51.outer), channel_id=1, source_target_pairs={{0,7},{1,6},{2,5},{3,4},{4,3},{5,2},{6,1},{7,0},{8,15},{9,14},{10,... | collective-permute-start | bytes 393224 | tf_op jit(solution)/shard_map/ppermute | solution.py:237
  60.8 0.9 %shard_map.45 = f32[8,64,256]{2,1,0:T(8,128)} custom-call(f32[8,48,256]{2,1,0:T(8,128)S(1)} %get-tuple-element.18.inside, f32[8,16,256]{2,1,0:T(8,128)S(1)} %get-tuple-element.21.edges), custom_call_target="tpu_custom_call" | custom-call | tf_op jit(solution)/shard_map/pallas_call | solution.py:22
  61.6 1.1 %collective-permute-done.12.from_inner = f32[8,32,128]{2,1,0:T(8,128)S(1)} collective-permute-done((f32[8,32,128]{2,1,0:T(8,128)S(1)}, f32[8,32,128]{2,1,0:T(8,128)S(1)}, u32[]{:S(2)}, u32[]{:S(2)}) %collective-permute-start.12) | collective-permute-done | bytes 131104 | tf_op jit(solution)/shard_map/ppermute | solution.py:237
  62.7 3.1 %collective-permute-done.13.from_outer = f32[8,32,128]{2,1,0:T(8,128)S(1)} collective-permute-done((f32[8,32,128]{2,1,0:T(8,128)S(1)}, f32[8,32,128]{2,1,0:T(8,128)S(1)}, u32[]{:S(2)}, u32[]{:S(2)}) %collective-permute-start.13) | collective-permute-done | bytes 131104 | tf_op jit(solution)/shard_map/ppermute | solution.py:237
  65.8 1.2 %shard_map.52 = f32[8,64,256]{2,1,0:T(8,128)} custom-call(f32[8,32,128]{2,1,0:T(8,128)S(1)} %shard_map.48.inner, f32[8,32,128]{2,1,0:T(8,128)S(1)} %shard_map.51.outer, f32[8,32,128]{2,1,0:T(8,128)S(1)} %collective-permute-done.12.from_inner, f32[8,32,128]{2,1,0:T(8,128)S(1)} %collective-permute-done.13.from_outer), custom_call_target="tpu_custom_call" | custom-call | tf_op jit(solution)/shard_map/pallas_call | solution.py:22
  (2 shorter events, 0.0 us)
Async XLA Ops:
  0.6 15.7 %collective-permute-start.1 = (f32[8,64,256]{2,1,0:T(8,128)}, f32[8,64,256]{2,1,0:T(8,128)S(1)}, u32[]{:S(2)}, u32[]{:S(2)}) collective-permute-start(f32[8,64,256]{2,1,0:T(8,128)} %first.1), channel_id=1, source_target_pairs={{0,248},{8,16},{16,8},{24,32},{32,24},{40,48},{48,40},{56,64},{64,... | collective-permute-start | bytes 1572872 | tf_op jit(solution)/shard_map/ppermute | solution.py:244
  3.3 13.0 %collective-permute-start = (f32[8,64,256]{2,1,0:T(8,128)}, f32[8,64,256]{2,1,0:T(8,128)S(1)}, u32[]{:S(2)}, u32[]{:S(2)}) collective-permute-start(f32[8,64,256]{2,1,0:T(8,128)} %first.1), channel_id=1, source_target_pairs={{0,8},{8,0},{16,24},{24,16},{32,40},{40,32},{48,56},{56,48},{64,72... | collective-permute-start | bytes 1572872 | tf_op jit(solution)/shard_map/ppermute | solution.py:245
  8.4 1.0 %copy-start = (f32[8,64,256]{2,1,0:T(8,128)S(1)}, f32[8,64,256]{2,1,0:T(8,128)}, u32[]{:S(2)}) copy-start(f32[8,64,256]{2,1,0:T(8,128)} %second.1) | copy-start | bytes 1572868
  9.5 1.0 %copy-start.1 = (f32[8,64,256]{2,1,0:T(8,128)S(1)}, f32[8,64,256]{2,1,0:T(8,128)}, u32[]{:S(2)}) copy-start(f32[8,64,256]{2,1,0:T(8,128)} %first.1) | copy-start | bytes 1572868
  16.5 10.1 %collective-permute-start.2 = (f32[8,24,256]{2,1,0:T(8,128)S(1)}, f32[8,24,256]{2,1,0:T(8,128)S(1)}, u32[]{:S(2)}, u32[]{:S(2)}) collective-permute-start(f32[8,24,256]{2,1,0:T(8,128)S(1)} %get-tuple-element.16.edge_near), channel_id=1, source_target_pairs={{0,1},{1,0},{2,3},{3,2},{4,5},{5,4},{6,7},{7,6},{8,9},{9,8},{10,11... | collective-permute-start | bytes 589832 | tf_op jit(solution)/shard_map/ppermute | solution.py:251
  20.3 12.1 %collective-permute-start.3 = (f32[8,24,256]{2,1,0:T(8,128)S(1)}, f32[8,24,256]{2,1,0:T(8,128)S(1)}, u32[]{:S(2)}, u32[]{:S(2)}) collective-permute-start(f32[8,24,256]{2,1,0:T(8,128)S(1)} %get-tuple-element.17.edge_far), channel_id=1, source_target_pairs={{0,7},{1,2},{2,1},{3,4},{4,3},{5,6},{6,5},{7,0},{8,15},{9,10},{10,... | collective-permute-start | bytes 589832 | tf_op jit(solution)/shard_map/ppermute | solution.py:250
  24.0 11.6 %collective-permute-start.4 = (f32[8,32,128]{2,1,0:T(8,128)S(1)}, f32[8,32,128]{2,1,0:T(8,128)S(1)}, u32[]{:S(2)}, u32[]{:S(2)}) collective-permute-start(f32[8,32,128]{2,1,0:T(8,128)S(1)} %get-tuple-element.23), channel_id=1, source_target_pairs={{0,7},{1,6},{2,5},{3,4},{4,3},{5,2},{6,1},{7,0},{8,15},{9,14},{10,... | collective-permute-start | bytes 393224 | tf_op jit(solution)/shard_map/ppermute | solution.py:232
  33.4 9.3 %collective-permute-start.8 = (f32[8,32,128]{2,1,0:T(8,128)S(1)}, f32[8,32,128]{2,1,0:T(8,128)S(1)}, u32[]{:S(2)}, u32[]{:S(2)}) collective-permute-start(f32[8,32,128]{2,1,0:T(8,128)S(1)} %get-tuple-element.25), channel_id=1, source_target_pairs={{0,7},{1,6},{2,5},{3,4},{4,3},{5,2},{6,1},{7,0},{8,15},{9,14},{10,... | collective-permute-start | bytes 393224 | tf_op jit(solution)/shard_map/ppermute | solution.py:232
  35.6 11.7 %collective-permute-start.5 = (f32[8,32,128]{2,1,0:T(8,128)S(1)}, f32[8,32,128]{2,1,0:T(8,128)S(1)}, u32[]{:S(2)}, u32[]{:S(2)}) collective-permute-start(f32[8,32,128]{2,1,0:T(8,128)S(1)} %shard_map.46.own), channel_id=1, source_target_pairs={{0,248},{8,240},{16,232},{24,224},{32,216},{40,208},{48,200},{56,1... | collective-permute-start | bytes 393224 | tf_op jit(solution)/shard_map/ppermute | solution.py:233
  42.7 8.0 %collective-permute-start.9 = (f32[8,32,128]{2,1,0:T(8,128)S(1)}, f32[8,32,128]{2,1,0:T(8,128)S(1)}, u32[]{:S(2)}, u32[]{:S(2)}) collective-permute-start(f32[8,32,128]{2,1,0:T(8,128)S(1)} %shard_map.49.own), channel_id=1, source_target_pairs={{0,248},{8,240},{16,232},{24,224},{32,216},{40,208},{48,200},{56,1... | collective-permute-start | bytes 393224 | tf_op jit(solution)/shard_map/ppermute | solution.py:233
  47.3 6.3 %collective-permute-start.7 = (f32[8,32,128]{2,1,0:T(8,128)S(1)}, f32[8,32,128]{2,1,0:T(8,128)S(1)}, u32[]{:S(2)}, u32[]{:S(2)}) collective-permute-start(f32[8,32,128]{2,1,0:T(8,128)S(1)} %shard_map.47.own), channel_id=1, source_target_pairs={{8,16},{16,8},{24,32},{32,24},{40,48},{48,40},{56,64},{64,56},{72,... | collective-permute-start | bytes 393224 | tf_op jit(solution)/shard_map/ppermute | solution.py:234
  49.3 4.4 %collective-permute-start.6 = (f32[8,32,128]{2,1,0:T(8,128)S(1)}, f32[8,32,128]{2,1,0:T(8,128)S(1)}, u32[]{:S(2)}, u32[]{:S(2)}) collective-permute-start(f32[8,32,128]{2,1,0:T(8,128)S(1)} %shard_map.47.own), channel_id=1, source_target_pairs={{0,8},{8,0},{16,24},{24,16},{32,40},{40,32},{48,56},{56,48},{64,72... | collective-permute-start | bytes 393224 | tf_op jit(solution)/shard_map/ppermute | solution.py:235
  50.8 6.3 %collective-permute-start.11 = (f32[8,32,128]{2,1,0:T(8,128)S(1)}, f32[8,32,128]{2,1,0:T(8,128)S(1)}, u32[]{:S(2)}, u32[]{:S(2)}) collective-permute-start(f32[8,32,128]{2,1,0:T(8,128)S(1)} %shard_map.50.own), channel_id=1, source_target_pairs={{8,16},{16,8},{24,32},{32,24},{40,48},{48,40},{56,64},{64,56},{72,... | collective-permute-start | bytes 393224 | tf_op jit(solution)/shard_map/ppermute | solution.py:234
  53.1 4.0 %collective-permute-start.10 = (f32[8,32,128]{2,1,0:T(8,128)S(1)}, f32[8,32,128]{2,1,0:T(8,128)S(1)}, u32[]{:S(2)}, u32[]{:S(2)}) collective-permute-start(f32[8,32,128]{2,1,0:T(8,128)S(1)} %shard_map.50.own), channel_id=1, source_target_pairs={{0,8},{8,0},{16,24},{24,16},{32,40},{40,32},{48,56},{56,48},{64,72... | collective-permute-start | bytes 393224 | tf_op jit(solution)/shard_map/ppermute | solution.py:235
  53.7 9.0 %collective-permute-start.12 = (f32[8,32,128]{2,1,0:T(8,128)S(1)}, f32[8,32,128]{2,1,0:T(8,128)S(1)}, u32[]{:S(2)}, u32[]{:S(2)}) collective-permute-start(f32[8,32,128]{2,1,0:T(8,128)S(1)} %shard_map.48.inner), channel_id=1, source_target_pairs={{0,7},{1,6},{2,5},{3,4},{4,3},{5,2},{6,1},{7,0},{8,15},{9,14},{10,... | collective-permute-start | bytes 393224 | tf_op jit(solution)/shard_map/ppermute | solution.py:237
  57.2 8.6 %collective-permute-start.13 = (f32[8,32,128]{2,1,0:T(8,128)S(1)}, f32[8,32,128]{2,1,0:T(8,128)S(1)}, u32[]{:S(2)}, u32[]{:S(2)}) collective-permute-start(f32[8,32,128]{2,1,0:T(8,128)S(1)} %shard_map.51.outer), channel_id=1, source_target_pairs={{0,7},{1,6},{2,5},{3,4},{4,3},{5,2},{6,1},{7,0},{8,15},{9,14},{10,... | collective-permute-start | bytes 393224 | tf_op jit(solution)/shard_map/ppermute | solution.py:237

commit v5 on v4

--- a/solution.py
+++ b/solution.py
@@ -18,13 +18,16 @@
 F32 = jnp.float32
 
 
-def run(body, outs, args, scratch=()):
+def run(body, outs, args, scratch=(), passed=None):
+    vmem, far = pl.BlockSpec(memory_space=pltpu.VMEM), pl.BlockSpec(memory_space=pl.ANY)
+    last = len(args) - 1
     return pl.pallas_call(
         body,
         out_shape=[jax.ShapeDtypeStruct(shape, F32) for shape in outs],
-        in_specs=[pl.BlockSpec(memory_space=pltpu.VMEM)] * len(args),
-        out_specs=[pl.BlockSpec(memory_space=pltpu.VMEM)] * len(outs),
+        in_specs=[far if passed and k == last else vmem for k in range(len(args))],
+        out_specs=[vmem if passed is None else far] * len(outs),
         scratch_shapes=list(scratch),
+        input_output_aliases={last: 0} if passed else {},
         compiler_params=pltpu.CompilerParams(vmem_limit_bytes=24 * 1024 * 1024),
     )(*args)
 
@@ -205,19 +208,32 @@
             for p, item in enumerate(items):
                 out[p, row : row + 8, :] = item
 
-    def finish_kernel(inner, outer, from_inner, from_outer, gradient, flat):
-        planes, rows, depth = gradient.shape
+    def smooth_z(own, from_y, held, flat):
+        planes, rows, depth = held.shape
         upper = lax.axis_index("gy") >= hy
-
-        def whole(inner, outer):
-            lines = jnp.concatenate([outer[:, :EDGE], inner, outer[:, EDGE:]], axis=1)
-            return lines.reshape(planes * rows, depth // 2)
-
-        mine = whole(inner[...], outer[...])
-        other = whole(flip_rows(from_inner[...]), flip_rows(from_outer[...]))
+        mine = own[...].reshape(planes * rows, depth // 2)
+        other = flip_rows(from_y[...]).reshape(planes * rows, depth // 2)
         flat[:, : depth // 2] = jnp.where(upper, other, mine)
         flat[:, depth // 2 :] = jnp.where(upper, mine, other)
-        gradient[...] = (z_pass(flat[...], 2) * (0.25 * WEIGHT)).reshape(planes, rows, depth)
+        held[...] = (z_pass(flat[...], 2) * (0.25 * WEIGHT)).reshape(planes, rows, depth)
+
+    def finish_inner_kernel(own, from_y, gradient, held, flat, sems):
+        smooth_z(own, from_y, held, flat)
+        inside = pl.ds(EDGE, held.shape[1])
+        copy = pltpu.make_async_copy(held, gradient.at[:, inside], sems.at[0])
+        copy.start()
+        copy.wait()
+
+    def finish_outer_kernel(own, from_y, _, gradient, held, flat, sems):
+        smooth_z(own, from_y, held, flat)
+        copies = [
+            pltpu.make_async_copy(held.at[:, pl.ds(row, EDGE)], gradient.at[:, pl.ds(at, EDGE)], sems.at[k])
+            for k, (row, at) in enumerate(((0, 0), (EDGE, gradient.shape[1] - EDGE)))
+        ]
+        for copy in copies:
+            copy.start()
+        for copy in copies:
+            copy.wait()
 
     near_x = [(i, i ^ 1) for i in range(nx)]
     near_y = [(j, j ^ 1) for j in range(ny)]
@@ -270,7 +286,13 @@
         (projected,) = run(project_kernel, [block], (inside, edges))
         inner, from_inner = symmetrized(*inner)
         outer, from_outer = symmetrized(*outer)
-        (gradient,) = run(finish_kernel, [block], (inner, outer, from_inner, from_outer), (flat,))
+        scratch = (
+            pltpu.VMEM((planes, rows // 2, depth), F32),
+            pltpu.VMEM((planes * rows // 2, depth), F32),
+            pltpu.SemaphoreType.DMA((2,)),
+        )
+        (gradient,) = run(finish_inner_kernel, [block], (inner, from_inner), scratch, 0)
+        (gradient,) = run(finish_outer_kernel, [block], (outer, from_outer, gradient), scratch, 1)
         return projected, gradient
 
     return jax.shard_map(

time: 67.8 us -> 67.7 us (level)
  waiting for transfers between devices: 19.6 us -> 18.5 us
  Pallas kernels: 4.77 us -> 5.62 us
    ppermute x2, waiting for transfers between devices: 4.12 us -> 3.08 us  [symmetrized(): return (smooth, lax.ppermute(smooth, 'gy', mirror_y))]
    pallas_call x12 -> x13, Pallas kernels: 4.77 us -> 5.62 us  [run(): pl.pallas_call(body, out_shape=[jax.ShapeDtypeStruct(shape, F32) for shap...]
  transfers between devices with their start and end apart: 14 -> 14, of which waited for: 8 -> 8; matrix products, arithmetic and copies ran while one was open for 0% -> 0% of each run, Pallas kernels for 5% -> 7%
where the time goes in v5:
time: 67.7 us; the launch traced here: 66.8 us
  starting transfers between devices  39.8 us (59%)
  waiting for transfers between devices  18.5 us (27%)
  Pallas kernels  5.62 us (8%)
  local copies, waits for them, and re-layouts  2.08 us (3%)
  between operations  0.73 us (1%)
    ppermute x2, starting transfers between devices, symmetrized(): lax.ppermute(total, 'gx', mirror_x)  9.8 us
    ppermute x2, starting transfers between devices, symmetrized(): return (smooth, lax.ppermute(smooth, 'gy', mirror_y))  6.68 us
    ppermute x1, waiting for transfers between devices, local(): from_far = lax.ppermute(to_far, 'gy', far_y)  5.81 us
    ppermute x1, waiting for transfers between devices, local(): far = lax.ppermute(density, 'gx', far_x)  5.7 us
    pallas_call x13, Pallas kernels, run(): pl.pallas_call(body, out_shape=[jax.ShapeDtypeStruct(shape, F32) for shap...  5.62 us
    ppermute x1, starting transfers between devices, local(): near = lax.ppermute(density, 'gx', near_x)  5.13 us
    ppermute x2, starting transfers between devices, symmetrized(): lax.ppermute(send, 'gy', mirror_y)  4.78 us
    ppermute x2, starting transfers between devices, symmetrized(): far = lax.ppermute(total, 'gx', fold_far_x)  4.24 us
  transfers between devices with their start and end apart: 14, of which 8 were waited for; matrix products, arithmetic and copies ran while one was open for 0% of the time, Pallas kernels for 7%

profile of v5, /device:TPU:1, one launch (start us, length us, event | category | flops | bytes accessed | tf_op | source)
XLA Modules:
  0.0 66.8 jit_solution(9117500108826791172)
XLA Ops:
  0.6 2.7 %collective-permute-start.1 = (f32[8,64,256]{2,1,0:T(8,128)}, f32[8,64,256]{2,1,0:T(8,128)S(1)}, u32[]{:S(2)}, u32[]{:S(2)}) collective-permute-start(f32[8,64,256]{2,1,0:T(8,128)} %first.1), channel_id=1, source_target_pairs={{0,248},{8,16},{16,8},{24,32},{32,24},{40,48},{48,40},{56,64},{64,... | collective-permute-start | bytes 1572872 | tf_op jit(solution)/shard_map/ppermute | solution.py:260
  3.3 5.1 %collective-permute-start = (f32[8,64,256]{2,1,0:T(8,128)}, f32[8,64,256]{2,1,0:T(8,128)S(1)}, u32[]{:S(2)}, u32[]{:S(2)}) collective-permute-start(f32[8,64,256]{2,1,0:T(8,128)} %first.1), channel_id=1, source_target_pairs={{0,8},{8,0},{16,24},{24,16},{32,40},{40,32},{48,56},{56,48},{64,72... | collective-permute-start | bytes 1572872 | tf_op jit(solution)/shard_map/ppermute | solution.py:261
  8.4 0.0 copy-start
  8.4 1.0 %copy-done = f32[8,64,256]{2,1,0:T(8,128)S(1)} copy-done((f32[8,64,256]{2,1,0:T(8,128)S(1)}, f32[8,64,256]{2,1,0:T(8,128)}, u32[]{:S(2)}) %copy-start) | copy-done | bytes 524312
  9.5 0.0 copy-start.1
  9.5 1.0 %copy-done.1 = f32[8,64,256]{2,1,0:T(8,128)S(1)} copy-done((f32[8,64,256]{2,1,0:T(8,128)S(1)}, f32[8,64,256]{2,1,0:T(8,128)}, u32[]{:S(2)}) %copy-start.1) | copy-done | bytes 524312
  10.5 0.1 shard_map.41
  10.6 5.7 %collective-permute-done.1.far = f32[8,64,256]{2,1,0:T(8,128)S(1)} collective-permute-done((f32[8,64,256]{2,1,0:T(8,128)}, f32[8,64,256]{2,1,0:T(8,128)S(1)}, u32[]{:S(2)}, u32[]{:S(2)}) %collective-permute-start.1) | collective-permute-done | bytes 524320 | tf_op jit(solution)/shard_map/ppermute | solution.py:260
  16.3 0.0 collective-permute-done.near
  16.3 0.2 shard_map.42
  16.5 3.8 %collective-permute-start.2 = (f32[8,24,256]{2,1,0:T(8,128)S(1)}, f32[8,24,256]{2,1,0:T(8,128)S(1)}, u32[]{:S(2)}, u32[]{:S(2)}) collective-permute-start(f32[8,24,256]{2,1,0:T(8,128)S(1)} %get-tuple-element.16.edge_near), channel_id=1, source_target_pairs={{0,1},{1,0},{2,3},{3,2},{4,5},{5,4},{6,7},{7,6},{8,9},{9,8},{10,11... | collective-permute-start | bytes 589832 | tf_op jit(solution)/shard_map/ppermute | solution.py:267
  20.3 2.6 %collective-permute-start.3 = (f32[8,24,256]{2,1,0:T(8,128)S(1)}, f32[8,24,256]{2,1,0:T(8,128)S(1)}, u32[]{:S(2)}, u32[]{:S(2)}) collective-permute-start(f32[8,24,256]{2,1,0:T(8,128)S(1)} %get-tuple-element.17.edge_far), channel_id=1, source_target_pairs={{0,7},{1,2},{2,1},{3,4},{4,3},{5,6},{6,5},{7,0},{8,15},{9,10},{10,... | collective-permute-start | bytes 589832 | tf_op jit(solution)/shard_map/ppermute | solution.py:266
  22.8 1.1 %shard_map.43 = (f32[8,32,256]{2,1,0:T(8,128)S(1)}, f32[8,48,256]{2,1,0:T(8,128)S(1)}, f32[8,48,256]{2,1,0:T(8,128)S(1)}, f32[8,32,128]{2,1,0:T(8,128)S(1)}, f32[8,32,128]{2,1,0:T(8,128)S(1)}) custom-call(f32[8,64,256]{2,1,0:T(8,128)S(1)} %get-tuple-element.14.own, f32[8,64,256]{2,1,0:T(8,128)S(1)} %collective-permute-done.near, ...), custom_call_target="tpu_custom_call" | custom-call | tf_op jit(solution)/shard_map/pallas_call | solution.py:24
  24.0 2.6 %collective-permute-start.9 = (f32[8,32,128]{2,1,0:T(8,128)S(1)}, f32[8,32,128]{2,1,0:T(8,128)S(1)}, u32[]{:S(2)}, u32[]{:S(2)}) collective-permute-start(f32[8,32,128]{2,1,0:T(8,128)S(1)} %get-tuple-element.25), channel_id=1, source_target_pairs={{0,7},{1,6},{2,5},{3,4},{4,3},{5,2},{6,1},{7,0},{8,15},{9,14},{10,... | collective-permute-start | bytes 393224 | tf_op jit(solution)/shard_map/ppermute | solution.py:248
  26.6 0.0 collective-permute-done.2.near
  26.6 5.8 %collective-permute-done.3.far = f32[8,24,256]{2,1,0:T(8,128)S(1)} collective-permute-done((f32[8,24,256]{2,1,0:T(8,128)S(1)}, f32[8,24,256]{2,1,0:T(8,128)S(1)}, u32[]{:S(2)}, u32[]{:S(2)}) %collective-permute-start.3) | collective-permute-done | bytes 196640 | tf_op jit(solution)/shard_map/ppermute | solution.py:266
  32.4 1.0 %shard_map.44 = (f32[8,16,256]{2,1,0:T(8,128)S(1)}, f32[8,32,128]{2,1,0:T(8,128)S(1)}, f32[8,32,128]{2,1,0:T(8,128)S(1)}) custom-call(f32[8,32,256]{2,1,0:T(8,128)S(1)} %get-tuple-element.19.outer, f32[8,48,256]{2,1,0:T(8,128)S(1)} %get-tuple-element.20.chain_in, f32[8,24,256]{2,1,0:T(8,128)S(1)} %collective-permute-done.2.near, ...), custom_call_target="tpu_custom_call" | custom-call | tf_op jit(solution)/shard_map/pallas_call | solution.py:24
  33.4 2.2 %collective-permute-start.4 = (f32[8,32,128]{2,1,0:T(8,128)S(1)}, f32[8,32,128]{2,1,0:T(8,128)S(1)}, u32[]{:S(2)}, u32[]{:S(2)}) collective-permute-start(f32[8,32,128]{2,1,0:T(8,128)S(1)} %get-tuple-element.23), channel_id=1, source_target_pairs={{0,7},{1,6},{2,5},{3,4},{4,3},{5,2},{6,1},{7,0},{8,15},{9,14},{10,... | collective-permute-start | bytes 393224 | tf_op jit(solution)/shard_map/ppermute | solution.py:248
  35.5 0.0 collective-permute-done.9.from_y
  35.5 0.1 shard_map.49.own
  35.6 5.3 %collective-permute-start.10 = (f32[8,32,128]{2,1,0:T(8,128)S(1)}, f32[8,32,128]{2,1,0:T(8,128)S(1)}, u32[]{:S(2)}, u32[]{:S(2)}) collective-permute-start(f32[8,32,128]{2,1,0:T(8,128)S(1)} %shard_map.49.own), channel_id=1, source_target_pairs={{0,248},{8,240},{16,232},{24,224},{32,216},{40,208},{48,200},{56,1... | collective-permute-start | bytes 393224 | tf_op jit(solution)/shard_map/ppermute | solution.py:249
  40.8 1.8 %collective-permute-done.4.from_y = f32[8,32,128]{2,1,0:T(8,128)S(1)} collective-permute-done((f32[8,32,128]{2,1,0:T(8,128)S(1)}, f32[8,32,128]{2,1,0:T(8,128)S(1)}, u32[]{:S(2)}, u32[]{:S(2)}) %collective-permute-start.4) | collective-permute-done | bytes 131104 | tf_op jit(solution)/shard_map/ppermute | solution.py:248
  42.7 0.1 shard_map.46.own
  42.7 4.5 %collective-permute-start.5 = (f32[8,32,128]{2,1,0:T(8,128)S(1)}, f32[8,32,128]{2,1,0:T(8,128)S(1)}, u32[]{:S(2)}, u32[]{:S(2)}) collective-permute-start(f32[8,32,128]{2,1,0:T(8,128)S(1)} %shard_map.46.own), channel_id=1, source_target_pairs={{0,248},{8,240},{16,232},{24,224},{32,216},{40,208},{48,200},{56,1... | collective-permute-start | bytes 393224 | tf_op jit(solution)/shard_map/ppermute | solution.py:249
  47.3 0.0 collective-permute-done.10.from_x
  47.3 1.9 %collective-permute-start.12 = (f32[8,32,128]{2,1,0:T(8,128)S(1)}, f32[8,32,128]{2,1,0:T(8,128)S(1)}, u32[]{:S(2)}, u32[]{:S(2)}) collective-permute-start(f32[8,32,128]{2,1,0:T(8,128)S(1)} %shard_map.50.own), channel_id=1, source_target_pairs={{8,16},{16,8},{24,32},{32,24},{40,48},{48,40},{56,64},{64,56},{72,... | collective-permute-start | bytes 393224 | tf_op jit(solution)/shard_map/ppermute | solution.py:250
  49.3 0.1 collective-permute-start.11
  49.4 1.4 %collective-permute-done.5.from_x = f32[8,32,128]{2,1,0:T(8,128)S(1)} collective-permute-done((f32[8,32,128]{2,1,0:T(8,128)S(1)}, f32[8,32,128]{2,1,0:T(8,128)S(1)}, u32[]{:S(2)}, u32[]{:S(2)}) %collective-permute-start.5) | collective-permute-done | bytes 131104 | tf_op jit(solution)/shard_map/ppermute | solution.py:249
  50.8 2.3 %collective-permute-start.7 = (f32[8,32,128]{2,1,0:T(8,128)S(1)}, f32[8,32,128]{2,1,0:T(8,128)S(1)}, u32[]{:S(2)}, u32[]{:S(2)}) collective-permute-start(f32[8,32,128]{2,1,0:T(8,128)S(1)} %shard_map.47.own), channel_id=1, source_target_pairs={{8,16},{16,8},{24,32},{32,24},{40,48},{48,40},{56,64},{64,56},{72,... | collective-permute-start | bytes 393224 | tf_op jit(solution)/shard_map/ppermute | solution.py:250
  53.1 0.1 collective-permute-start.6
  53.2 0.4 collective-permute-done.12.far
  53.6 0.0 collective-permute-done.11.near
  53.6 0.1 shard_map.51.own
  53.7 3.1 %collective-permute-start.13 = (f32[8,32,128]{2,1,0:T(8,128)S(1)}, f32[8,32,128]{2,1,0:T(8,128)S(1)}, u32[]{:S(2)}, u32[]{:S(2)}) collective-permute-start(f32[8,32,128]{2,1,0:T(8,128)S(1)} %shard_map.51.own), channel_id=1, source_target_pairs={{0,7},{1,6},{2,5},{3,4},{4,3},{5,2},{6,1},{7,0},{8,15},{9,14},{10,... | collective-permute-start | bytes 393224 | tf_op jit(solution)/shard_map/ppermute | solution.py:253
  56.8 0.3 collective-permute-done.7.far
  57.1 0.0 collective-permute-done.6.near
  57.1 0.1 shard_map.48.own
  57.2 3.6 %collective-permute-start.8 = (f32[8,32,128]{2,1,0:T(8,128)S(1)}, f32[8,32,128]{2,1,0:T(8,128)S(1)}, u32[]{:S(2)}, u32[]{:S(2)}) collective-permute-start(f32[8,32,128]{2,1,0:T(8,128)S(1)} %shard_map.48.own), channel_id=1, source_target_pairs={{0,7},{1,6},{2,5},{3,4},{4,3},{5,2},{6,1},{7,0},{8,15},{9,14},{10,... | collective-permute-start | bytes 393224 | tf_op jit(solution)/shard_map/ppermute | solution.py:253
  60.8 0.9 %shard_map.45 = f32[8,64,256]{2,1,0:T(8,128)} custom-call(f32[8,48,256]{2,1,0:T(8,128)S(1)} %get-tuple-element.18.inside, f32[8,16,256]{2,1,0:T(8,128)S(1)} %get-tuple-element.21.edges), custom_call_target="tpu_custom_call" | custom-call | tf_op jit(solution)/shard_map/pallas_call | solution.py:24
  61.6 1.1 %collective-permute-done.13.from_y = f32[8,32,128]{2,1,0:T(8,128)S(1)} collective-permute-done((f32[8,32,128]{2,1,0:T(8,128)S(1)}, f32[8,32,128]{2,1,0:T(8,128)S(1)}, u32[]{:S(2)}, u32[]{:S(2)}) %collective-permute-start.13) | collective-permute-done | bytes 131104 | tf_op jit(solution)/shard_map/ppermute | solution.py:253
  62.7 1.0 %shard_map.52._ = f32[8,64,256]{2,1,0:T(8,128)} custom-call(f32[8,32,128]{2,1,0:T(8,128)S(1)} %shard_map.51.own, f32[8,32,128]{2,1,0:T(8,128)S(1)} %collective-permute-done.13.from_y), custom_call_target="tpu_custom_call" | custom-call | tf_op jit(solution)/shard_map/pallas_call | solution.py:24
  63.7 2.0 %collective-permute-done.8.from_y = f32[8,32,128]{2,1,0:T(8,128)S(1)} collective-permute-done((f32[8,32,128]{2,1,0:T(8,128)S(1)}, f32[8,32,128]{2,1,0:T(8,128)S(1)}, u32[]{:S(2)}, u32[]{:S(2)}) %collective-permute-start.8) | collective-permute-done | bytes 131104 | tf_op jit(solution)/shard_map/ppermute | solution.py:253
  65.8 1.0 %shard_map.53 = f32[8,64,256]{2,1,0:T(8,128)} custom-call(f32[8,32,128]{2,1,0:T(8,128)S(1)} %shard_map.48.own, f32[8,32,128]{2,1,0:T(8,128)S(1)} %collective-permute-done.8.from_y, f32[8,64,256]{2,1,0:T(8,128)} %shard_map.52._), custom_call_target="tpu_custom_call", output_to_operand_aliasing={{}: (2, {})} | custom-call | tf_op jit(solution)/shard_map/pallas_call | solution.py:24
  (2 shorter events, 0.0 us)
Async XLA Ops:
  0.6 15.7 %collective-permute-start.1 = (f32[8,64,256]{2,1,0:T(8,128)}, f32[8,64,256]{2,1,0:T(8,128)S(1)}, u32[]{:S(2)}, u32[]{:S(2)}) collective-permute-start(f32[8,64,256]{2,1,0:T(8,128)} %first.1), channel_id=1, source_target_pairs={{0,248},{8,16},{16,8},{24,32},{32,24},{40,48},{48,40},{56,64},{64,... | collective-permute-start | bytes 1572872 | tf_op jit(solution)/shard_map/ppermute | solution.py:260
  3.3 13.0 %collective-permute-start = (f32[8,64,256]{2,1,0:T(8,128)}, f32[8,64,256]{2,1,0:T(8,128)S(1)}, u32[]{:S(2)}, u32[]{:S(2)}) collective-permute-start(f32[8,64,256]{2,1,0:T(8,128)} %first.1), channel_id=1, source_target_pairs={{0,8},{8,0},{16,24},{24,16},{32,40},{40,32},{48,56},{56,48},{64,72... | collective-permute-start | bytes 1572872 | tf_op jit(solution)/shard_map/ppermute | solution.py:261
  8.4 1.0 %copy-start = (f32[8,64,256]{2,1,0:T(8,128)S(1)}, f32[8,64,256]{2,1,0:T(8,128)}, u32[]{:S(2)}) copy-start(f32[8,64,256]{2,1,0:T(8,128)} %second.1) | copy-start | bytes 1572868
  9.5 1.0 %copy-start.1 = (f32[8,64,256]{2,1,0:T(8,128)S(1)}, f32[8,64,256]{2,1,0:T(8,128)}, u32[]{:S(2)}) copy-start(f32[8,64,256]{2,1,0:T(8,128)} %first.1) | copy-start | bytes 1572868
  16.5 10.1 %collective-permute-start.2 = (f32[8,24,256]{2,1,0:T(8,128)S(1)}, f32[8,24,256]{2,1,0:T(8,128)S(1)}, u32[]{:S(2)}, u32[]{:S(2)}) collective-permute-start(f32[8,24,256]{2,1,0:T(8,128)S(1)} %get-tuple-element.16.edge_near), channel_id=1, source_target_pairs={{0,1},{1,0},{2,3},{3,2},{4,5},{5,4},{6,7},{7,6},{8,9},{9,8},{10,11... | collective-permute-start | bytes 589832 | tf_op jit(solution)/shard_map/ppermute | solution.py:267
  20.3 12.1 %collective-permute-start.3 = (f32[8,24,256]{2,1,0:T(8,128)S(1)}, f32[8,24,256]{2,1,0:T(8,128)S(1)}, u32[]{:S(2)}, u32[]{:S(2)}) collective-permute-start(f32[8,24,256]{2,1,0:T(8,128)S(1)} %get-tuple-element.17.edge_far), channel_id=1, source_target_pairs={{0,7},{1,2},{2,1},{3,4},{4,3},{5,6},{6,5},{7,0},{8,15},{9,10},{10,... | collective-permute-start | bytes 589832 | tf_op jit(solution)/shard_map/ppermute | solution.py:266
  24.0 11.6 %collective-permute-start.9 = (f32[8,32,128]{2,1,0:T(8,128)S(1)}, f32[8,32,128]{2,1,0:T(8,128)S(1)}, u32[]{:S(2)}, u32[]{:S(2)}) collective-permute-start(f32[8,32,128]{2,1,0:T(8,128)S(1)} %get-tuple-element.25), channel_id=1, source_target_pairs={{0,7},{1,6},{2,5},{3,4},{4,3},{5,2},{6,1},{7,0},{8,15},{9,14},{10,... | collective-permute-start | bytes 393224 | tf_op jit(solution)/shard_map/ppermute | solution.py:248
  33.4 9.3 %collective-permute-start.4 = (f32[8,32,128]{2,1,0:T(8,128)S(1)}, f32[8,32,128]{2,1,0:T(8,128)S(1)}, u32[]{:S(2)}, u32[]{:S(2)}) collective-permute-start(f32[8,32,128]{2,1,0:T(8,128)S(1)} %get-tuple-element.23), channel_id=1, source_target_pairs={{0,7},{1,6},{2,5},{3,4},{4,3},{5,2},{6,1},{7,0},{8,15},{9,14},{10,... | collective-permute-start | bytes 393224 | tf_op jit(solution)/shard_map/ppermute | solution.py:248
  35.6 11.7 %collective-permute-start.10 = (f32[8,32,128]{2,1,0:T(8,128)S(1)}, f32[8,32,128]{2,1,0:T(8,128)S(1)}, u32[]{:S(2)}, u32[]{:S(2)}) collective-permute-start(f32[8,32,128]{2,1,0:T(8,128)S(1)} %shard_map.49.own), channel_id=1, source_target_pairs={{0,248},{8,240},{16,232},{24,224},{32,216},{40,208},{48,200},{56,1... | collective-permute-start | bytes 393224 | tf_op jit(solution)/shard_map/ppermute | solution.py:249
  42.7 8.0 %collective-permute-start.5 = (f32[8,32,128]{2,1,0:T(8,128)S(1)}, f32[8,32,128]{2,1,0:T(8,128)S(1)}, u32[]{:S(2)}, u32[]{:S(2)}) collective-permute-start(f32[8,32,128]{2,1,0:T(8,128)S(1)} %shard_map.46.own), channel_id=1, source_target_pairs={{0,248},{8,240},{16,232},{24,224},{32,216},{40,208},{48,200},{56,1... | collective-permute-start | bytes 393224 | tf_op jit(solution)/shard_map/ppermute | solution.py:249
  47.3 6.3 %collective-permute-start.12 = (f32[8,32,128]{2,1,0:T(8,128)S(1)}, f32[8,32,128]{2,1,0:T(8,128)S(1)}, u32[]{:S(2)}, u32[]{:S(2)}) collective-permute-start(f32[8,32,128]{2,1,0:T(8,128)S(1)} %shard_map.50.own), channel_id=1, source_target_pairs={{8,16},{16,8},{24,32},{32,24},{40,48},{48,40},{56,64},{64,56},{72,... | collective-permute-start | bytes 393224 | tf_op jit(solution)/shard_map/ppermute | solution.py:250
  49.3 4.4 %collective-permute-start.11 = (f32[8,32,128]{2,1,0:T(8,128)S(1)}, f32[8,32,128]{2,1,0:T(8,128)S(1)}, u32[]{:S(2)}, u32[]{:S(2)}) collective-permute-start(f32[8,32,128]{2,1,0:T(8,128)S(1)} %shard_map.50.own), channel_id=1, source_target_pairs={{0,8},{8,0},{16,24},{24,16},{32,40},{40,32},{48,56},{56,48},{64,72... | collective-permute-start | bytes 393224 | tf_op jit(solution)/shard_map/ppermute | solution.py:251
  50.8 6.3 %collective-permute-start.7 = (f32[8,32,128]{2,1,0:T(8,128)S(1)}, f32[8,32,128]{2,1,0:T(8,128)S(1)}, u32[]{:S(2)}, u32[]{:S(2)}) collective-permute-start(f32[8,32,128]{2,1,0:T(8,128)S(1)} %shard_map.47.own), channel_id=1, source_target_pairs={{8,16},{16,8},{24,32},{32,24},{40,48},{48,40},{56,64},{64,56},{72,... | collective-permute-start | bytes 393224 | tf_op jit(solution)/shard_map/ppermute | solution.py:250
  53.1 4.0 %collective-permute-start.6 = (f32[8,32,128]{2,1,0:T(8,128)S(1)}, f32[8,32,128]{2,1,0:T(8,128)S(1)}, u32[]{:S(2)}, u32[]{:S(2)}) collective-permute-start(f32[8,32,128]{2,1,0:T(8,128)S(1)} %shard_map.47.own), channel_id=1, source_target_pairs={{0,8},{8,0},{16,24},{24,16},{32,40},{40,32},{48,56},{56,48},{64,72... | collective-permute-start | bytes 393224 | tf_op jit(solution)/shard_map/ppermute | solution.py:251
  53.7 9.0 %collective-permute-start.13 = (f32[8,32,128]{2,1,0:T(8,128)S(1)}, f32[8,32,128]{2,1,0:T(8,128)S(1)}, u32[]{:S(2)}, u32[]{:S(2)}) collective-permute-start(f32[8,32,128]{2,1,0:T(8,128)S(1)} %shard_map.51.own), channel_id=1, source_target_pairs={{0,7},{1,6},{2,5},{3,4},{4,3},{5,2},{6,1},{7,0},{8,15},{9,14},{10,... | collective-permute-start | bytes 393224 | tf_op jit(solution)/shard_map/ppermute | solution.py:253
  57.2 8.6 %collective-permute-start.8 = (f32[8,32,128]{2,1,0:T(8,128)S(1)}, f32[8,32,128]{2,1,0:T(8,128)S(1)}, u32[]{:S(2)}, u32[]{:S(2)}) collective-permute-start(f32[8,32,128]{2,1,0:T(8,128)S(1)} %shard_map.48.own), channel_id=1, source_target_pairs={{0,7},{1,6},{2,5},{3,4},{4,3},{5,2},{6,1},{7,0},{8,15},{9,14},{10,... | collective-permute-start | bytes 393224 | tf_op jit(solution)/shard_map/ppermute | solution.py:253

commit v6 on v5

--- a/solution.py
+++ b/solution.py
@@ -167,26 +167,43 @@
             middle[p] = cone_rows(part, 0)[: rows - 2 * EDGE]
         keep[...], send[...] = halves(middle[...])
 
-    def chain_kernel(outer, chain_in, near, far, sens, tilted_out, keep, send, halo, ys):
+    def one_side(low, outer, chain, message, sens, put):
         planes, rows, depth = sens.shape
-        low, high = ordered(is_odd("gy"), near[...], far[...])
+        halo = message[:, :EDGE].reshape(planes * EDGE, depth)
+        beyond = z_pass(halo, 3).reshape(planes, EDGE, depth)
+
+        def join(outside, inside):
+            first, second = jnp.where(low, outside, inside), jnp.where(low, inside, outside)
+            return jnp.concatenate([first, second], axis=0)
+
         for p in range(planes):
-            halo[2 * EDGE * p : 2 * EDGE * p + EDGE, :] = low[p, :EDGE]
-            halo[2 * EDGE * p + EDGE : 2 * EDGE * (p + 1), :] = high[p, :EDGE]
-        beyond = z_pass(halo[...], 3).reshape(planes, 2 * EDGE, depth)
-        for p in range(planes):
-            top = jnp.concatenate([beyond[p, :EDGE], outer[p, :EDGE]], axis=0)
-            bottom = jnp.concatenate([outer[p, EDGE:], beyond[p, EDGE:]], axis=0)
-            tops, slope_top = tilt(cone_rows(top, 0)[:EDGE])
-            bottoms, slope_bottom = tilt(cone_rows(bottom, 0)[:EDGE])
-            tilted_out[p, :RADIUS] = tops[RADIUS:]
-            tilted_out[p, RADIUS:] = bottoms[:RADIUS]
-            above = jnp.concatenate([low[p, EDGE:], sens[p, :RADIUS]], axis=0) * slope_top
-            below = jnp.concatenate([sens[p, rows - RADIUS :], high[p, EDGE:]], axis=0) * slope_bottom
-            top = jnp.concatenate([above, chain_in[p, :EDGE]], axis=0)
-            bottom = jnp.concatenate([chain_in[p, rows - EDGE - 2 * RADIUS :], below], axis=0)
-            ys[p, :EDGE] = cone_rows(top, 0)[:EDGE]
-            ys[p, EDGE:] = cone_rows(bottom, 0)[:EDGE]
+            inside = jnp.where(low, outer[p, :EDGE], outer[p, EDGE:])
+            tilted, slope = tilt(cone_rows(join(beyond[p], inside), 0)[:EDGE])
+            inside = jnp.where(low, sens[p, :RADIUS], sens[p, rows - RADIUS :])
+            part = join(message[p, EDGE:], inside) * slope
+            inside = jnp.where(low, chain[p, :EDGE], chain[p, rows - 2 * RADIUS - EDGE :])
+            at_edge = jnp.where(low, tilted[RADIUS:], tilted[:RADIUS])
+            put(p, at_edge, cone_rows(join(part, inside), 0)[:EDGE])
+
+    def near_kernel(outer, chain, message, sens, tilted_out, ys):
+        def put(p, tilted, part):
+            tilted_out[p] = tilted
+            ys[p] = part
+
+        one_side(is_odd("gy"), outer, chain, message, sens, put)
+
+    def chain_kernel(outer, chain, message, sens, near_tilted, near_ys, tilted_out, keep, send, ys):
+        odd = is_odd("gy")
+
+        def put(p, tilted, part):
+            low, high = ordered(odd, near_tilted[p], tilted)
+            tilted_out[p, :RADIUS] = low
+            tilted_out[p, RADIUS:] = high
+            low, high = ordered(odd, near_ys[p], part)
+            ys[p, :EDGE] = low
+            ys[p, EDGE:] = high
+
+        one_side(jnp.logical_not(odd), outer, chain, message, sens, put)
         keep[...], send[...] = halves(ys[...])
 
     def project_kernel(inside, edges, projected):
@@ -277,11 +294,16 @@
             (own, near, far, to_near, to_far, sens),
             (flat, pltpu.VMEM((planes, rows - 2 * EDGE, depth), F32)),
         )
+        near_edge = run(
+            near_kernel,
+            [(planes, RADIUS, depth), (planes, EDGE, depth)],
+            (outer, chain, from_near, sens),
+        )
         edges, *outer = run(
             chain_kernel,
             [(planes, 2 * RADIUS, depth), part, part],
-            (outer, chain, from_near, from_far, sens),
-            (pltpu.VMEM((planes * 2 * EDGE, depth), F32), pltpu.VMEM((planes, 2 * EDGE, depth), F32)),
+            (outer, chain, from_far, sens, *near_edge),
+            (pltpu.VMEM((planes, 2 * EDGE, depth), F32),),
         )
         (projected,) = run(project_kernel, [block], (inside, edges))
         inner, from_inner = symmetrized(*inner)

time: 67.7 us -> 67.7 us (level)
    pallas_call x13 -> x14, Pallas kernels: 5.62 us -> 5.96 us  [run(): pl.pallas_call(body, out_shape=[jax.ShapeDtypeStruct(shape, F32) for shap...]
where the time goes in v6:
time: 67.7 us; the launch traced here: 66.5 us
  starting transfers between devices  39.8 us (59%)
  waiting for transfers between devices  17.9 us (26%)
  Pallas kernels  5.96 us (9%)
  local copies, waits for them, and re-layouts  2.08 us (3%)
  between operations  0.73 us (1%)
    ppermute x2, starting transfers between devices, symmetrized(): lax.ppermute(total, 'gx', mirror_x)  9.8 us
    ppermute x2, starting transfers between devices, symmetrized(): return (smooth, lax.ppermute(smooth, 'gy', mirror_y))  6.69 us
    pallas_call x14, Pallas kernels, run(): pl.pallas_call(body, out_shape=[jax.ShapeDtypeStruct(shape, F32) for shap...  5.96 us
    ppermute x1, waiting for transfers between devices, local(): far = lax.ppermute(density, 'gx', far_x)  5.7 us
    ppermute x1, waiting for transfers between devices, local(): from_far = lax.ppermute(to_far, 'gy', far_y)  5.17 us
    ppermute x1, starting transfers between devices, local(): near = lax.ppermute(density, 'gx', near_x)  5.13 us
    ppermute x2, starting transfers between devices, symmetrized(): lax.ppermute(send, 'gy', mirror_y)  4.78 us
    ppermute x2, starting transfers between devices, symmetrized(): far = lax.ppermute(total, 'gx', fold_far_x)  4.18 us
  transfers between devices with their start and end apart: 14, of which 8 were waited for; matrix products, arithmetic and copies ran while one was open for 0% of the time, Pallas kernels for 7%

profile of v6, /device:TPU:1, one launch (start us, length us, event | category | flops | bytes accessed | tf_op | source)
XLA Modules:
  0.0 66.5 jit_solution(16579406955109433688)
XLA Ops:
  0.6 2.7 %collective-permute-start.1 = (f32[8,64,256]{2,1,0:T(8,128)}, f32[8,64,256]{2,1,0:T(8,128)S(1)}, u32[]{:S(2)}, u32[]{:S(2)}) collective-permute-start(f32[8,64,256]{2,1,0:T(8,128)} %first.1), channel_id=1, source_target_pairs={{0,248},{8,16},{16,8},{24,32},{32,24},{40,48},{48,40},{56,64},{64,... | collective-permute-start | bytes 1572872 | tf_op jit(solution)/shard_map/ppermute | solution.py:277
  3.3 5.1 %collective-permute-start = (f32[8,64,256]{2,1,0:T(8,128)}, f32[8,64,256]{2,1,0:T(8,128)S(1)}, u32[]{:S(2)}, u32[]{:S(2)}) collective-permute-start(f32[8,64,256]{2,1,0:T(8,128)} %first.1), channel_id=1, source_target_pairs={{0,8},{8,0},{16,24},{24,16},{32,40},{40,32},{48,56},{56,48},{64,72... | collective-permute-start | bytes 1572872 | tf_op jit(solution)/shard_map/ppermute | solution.py:278
  8.4 0.0 copy-start
  8.4 1.0 %copy-done = f32[8,64,256]{2,1,0:T(8,128)S(1)} copy-done((f32[8,64,256]{2,1,0:T(8,128)S(1)}, f32[8,64,256]{2,1,0:T(8,128)}, u32[]{:S(2)}) %copy-start) | copy-done | bytes 524312
  9.5 0.0 copy-start.1
  9.5 1.0 %copy-done.1 = f32[8,64,256]{2,1,0:T(8,128)S(1)} copy-done((f32[8,64,256]{2,1,0:T(8,128)S(1)}, f32[8,64,256]{2,1,0:T(8,128)}, u32[]{:S(2)}) %copy-start.1) | copy-done | bytes 524312
  10.5 0.1 shard_map.41
  10.6 5.7 %collective-permute-done.1.far = f32[8,64,256]{2,1,0:T(8,128)S(1)} collective-permute-done((f32[8,64,256]{2,1,0:T(8,128)}, f32[8,64,256]{2,1,0:T(8,128)S(1)}, u32[]{:S(2)}, u32[]{:S(2)}) %collective-permute-start.1) | collective-permute-done | bytes 524320 | tf_op jit(solution)/shard_map/ppermute | solution.py:277
  16.3 0.0 collective-permute-done.near
  16.3 0.2 shard_map.42
  16.5 3.8 %collective-permute-start.3 = (f32[8,24,256]{2,1,0:T(8,128)S(1)}, f32[8,24,256]{2,1,0:T(8,128)S(1)}, u32[]{:S(2)}, u32[]{:S(2)}) collective-permute-start(f32[8,24,256]{2,1,0:T(8,128)S(1)} %get-tuple-element.18.edge_near), channel_id=1, source_target_pairs={{0,1},{1,0},{2,3},{3,2},{4,5},{5,4},{6,7},{7,6},{8,9},{9,8},{10,11... | collective-permute-start | bytes 589832 | tf_op jit(solution)/shard_map/ppermute | solution.py:284
  20.3 2.6 %collective-permute-start.2 = (f32[8,24,256]{2,1,0:T(8,128)S(1)}, f32[8,24,256]{2,1,0:T(8,128)S(1)}, u32[]{:S(2)}, u32[]{:S(2)}) collective-permute-start(f32[8,24,256]{2,1,0:T(8,128)S(1)} %get-tuple-element.19.edge_far), channel_id=1, source_target_pairs={{0,7},{1,2},{2,1},{3,4},{4,3},{5,6},{6,5},{7,0},{8,15},{9,10},{10,... | collective-permute-start | bytes 589832 | tf_op jit(solution)/shard_map/ppermute | solution.py:283
  22.8 1.1 %shard_map.43 = (f32[8,32,256]{2,1,0:T(8,128)S(1)}, f32[8,48,256]{2,1,0:T(8,128)S(1)}, f32[8,48,256]{2,1,0:T(8,128)S(1)}, f32[8,32,128]{2,1,0:T(8,128)S(1)}, f32[8,32,128]{2,1,0:T(8,128)S(1)}) custom-call(f32[8,64,256]{2,1,0:T(8,128)S(1)} %get-tuple-element.16.own, f32[8,64,256]{2,1,0:T(8,128)S(1)} %collective-permute-done.near, ...), custom_call_target="tpu_custom_call" | custom-call | tf_op jit(solution)/shard_map/pallas_call | solution.py:24
  24.0 2.6 %collective-permute-start.9 = (f32[8,32,128]{2,1,0:T(8,128)S(1)}, f32[8,32,128]{2,1,0:T(8,128)S(1)}, u32[]{:S(2)}, u32[]{:S(2)}) collective-permute-start(f32[8,32,128]{2,1,0:T(8,128)S(1)} %get-tuple-element.29), channel_id=1, source_target_pairs={{0,7},{1,6},{2,5},{3,4},{4,3},{5,2},{6,1},{7,0},{8,15},{9,14},{10,... | collective-permute-start | bytes 393224 | tf_op jit(solution)/shard_map/ppermute | solution.py:265
  26.6 0.0 collective-permute-done.3.message
  26.6 0.6 shard_map.44
  27.2 5.2 %collective-permute-done.2.message = f32[8,24,256]{2,1,0:T(8,128)S(1)} collective-permute-done((f32[8,24,256]{2,1,0:T(8,128)S(1)}, f32[8,24,256]{2,1,0:T(8,128)S(1)}, u32[]{:S(2)}, u32[]{:S(2)}) %collective-permute-start.2) | collective-permute-done | bytes 196640 | tf_op jit(solution)/shard_map/ppermute | solution.py:283
  32.4 0.7 shard_map.45
  33.0 2.2 %collective-permute-start.4 = (f32[8,32,128]{2,1,0:T(8,128)S(1)}, f32[8,32,128]{2,1,0:T(8,128)S(1)}, u32[]{:S(2)}, u32[]{:S(2)}) collective-permute-start(f32[8,32,128]{2,1,0:T(8,128)S(1)} %get-tuple-element.27), channel_id=1, source_target_pairs={{0,7},{1,6},{2,5},{3,4},{4,3},{5,2},{6,1},{7,0},{8,15},{9,14},{10,... | collective-permute-start | bytes 393224 | tf_op jit(solution)/shard_map/ppermute | solution.py:265
  35.2 0.0 collective-permute-done.9.from_y
  35.2 0.1 shard_map.50.own
  35.3 5.3 %collective-permute-start.10 = (f32[8,32,128]{2,1,0:T(8,128)S(1)}, f32[8,32,128]{2,1,0:T(8,128)S(1)}, u32[]{:S(2)}, u32[]{:S(2)}) collective-permute-start(f32[8,32,128]{2,1,0:T(8,128)S(1)} %shard_map.50.own), channel_id=1, source_target_pairs={{0,248},{8,240},{16,232},{24,224},{32,216},{40,208},{48,200},{56,1... | collective-permute-start | bytes 393224 | tf_op jit(solution)/shard_map/ppermute | solution.py:266
  40.5 1.8 %collective-permute-done.4.from_y = f32[8,32,128]{2,1,0:T(8,128)S(1)} collective-permute-done((f32[8,32,128]{2,1,0:T(8,128)S(1)}, f32[8,32,128]{2,1,0:T(8,128)S(1)}, u32[]{:S(2)}, u32[]{:S(2)}) %collective-permute-start.4) | collective-permute-done | bytes 131104 | tf_op jit(solution)/shard_map/ppermute | solution.py:265
  42.4 0.1 shard_map.47.own
  42.4 4.5 %collective-permute-start.5 = (f32[8,32,128]{2,1,0:T(8,128)S(1)}, f32[8,32,128]{2,1,0:T(8,128)S(1)}, u32[]{:S(2)}, u32[]{:S(2)}) collective-permute-start(f32[8,32,128]{2,1,0:T(8,128)S(1)} %shard_map.47.own), channel_id=1, source_target_pairs={{0,248},{8,240},{16,232},{24,224},{32,216},{40,208},{48,200},{56,1... | collective-permute-start | bytes 393224 | tf_op jit(solution)/shard_map/ppermute | solution.py:266
  47.0 0.0 collective-permute-done.10.from_x
  47.0 1.9 %collective-permute-start.12 = (f32[8,32,128]{2,1,0:T(8,128)S(1)}, f32[8,32,128]{2,1,0:T(8,128)S(1)}, u32[]{:S(2)}, u32[]{:S(2)}) collective-permute-start(f32[8,32,128]{2,1,0:T(8,128)S(1)} %shard_map.51.own), channel_id=1, source_target_pairs={{8,16},{16,8},{24,32},{32,24},{40,48},{48,40},{56,64},{64,56},{72,... | collective-permute-start | bytes 393224 | tf_op jit(solution)/shard_map/ppermute | solution.py:267
  49.0 0.1 collective-permute-start.11
  49.1 1.4 %collective-permute-done.5.from_x = f32[8,32,128]{2,1,0:T(8,128)S(1)} collective-permute-done((f32[8,32,128]{2,1,0:T(8,128)S(1)}, f32[8,32,128]{2,1,0:T(8,128)S(1)}, u32[]{:S(2)}, u32[]{:S(2)}) %collective-permute-start.5) | collective-permute-done | bytes 131104 | tf_op jit(solution)/shard_map/ppermute | solution.py:266
  50.5 2.3 %collective-permute-start.7 = (f32[8,32,128]{2,1,0:T(8,128)S(1)}, f32[8,32,128]{2,1,0:T(8,128)S(1)}, u32[]{:S(2)}, u32[]{:S(2)}) collective-permute-start(f32[8,32,128]{2,1,0:T(8,128)S(1)} %shard_map.48.own), channel_id=1, source_target_pairs={{8,16},{16,8},{24,32},{32,24},{40,48},{48,40},{56,64},{64,56},{72,... | collective-permute-start | bytes 393224 | tf_op jit(solution)/shard_map/ppermute | solution.py:267
  52.8 0.1 collective-permute-start.6
  52.9 0.5 collective-permute-done.12.far
  53.3 0.0 collective-permute-done.11.near
  53.3 0.1 shard_map.52.own
  53.4 3.1 %collective-permute-start.13 = (f32[8,32,128]{2,1,0:T(8,128)S(1)}, f32[8,32,128]{2,1,0:T(8,128)S(1)}, u32[]{:S(2)}, u32[]{:S(2)}) collective-permute-start(f32[8,32,128]{2,1,0:T(8,128)S(1)} %shard_map.52.own), channel_id=1, source_target_pairs={{0,7},{1,6},{2,5},{3,4},{4,3},{5,2},{6,1},{7,0},{8,15},{9,14},{10,... | collective-permute-start | bytes 393224 | tf_op jit(solution)/shard_map/ppermute | solution.py:270
  56.5 0.3 collective-permute-done.7.far
  56.8 0.0 collective-permute-done.6.near
  56.8 0.1 shard_map.49.own
  56.9 3.6 %collective-permute-start.8 = (f32[8,32,128]{2,1,0:T(8,128)S(1)}, f32[8,32,128]{2,1,0:T(8,128)S(1)}, u32[]{:S(2)}, u32[]{:S(2)}) collective-permute-start(f32[8,32,128]{2,1,0:T(8,128)S(1)} %shard_map.49.own), channel_id=1, source_target_pairs={{0,7},{1,6},{2,5},{3,4},{4,3},{5,2},{6,1},{7,0},{8,15},{9,14},{10,... | collective-permute-start | bytes 393224 | tf_op jit(solution)/shard_map/ppermute | solution.py:270
  60.5 0.9 %shard_map.46 = f32[8,64,256]{2,1,0:T(8,128)} custom-call(f32[8,48,256]{2,1,0:T(8,128)S(1)} %get-tuple-element.20.inside, f32[8,16,256]{2,1,0:T(8,128)S(1)} %get-tuple-element.25.edges), custom_call_target="tpu_custom_call" | custom-call | tf_op jit(solution)/shard_map/pallas_call | solution.py:24
  61.3 1.1 %collective-permute-done.13.from_y = f32[8,32,128]{2,1,0:T(8,128)S(1)} collective-permute-done((f32[8,32,128]{2,1,0:T(8,128)S(1)}, f32[8,32,128]{2,1,0:T(8,128)S(1)}, u32[]{:S(2)}, u32[]{:S(2)}) %collective-permute-start.13) | collective-permute-done | bytes 131104 | tf_op jit(solution)/shard_map/ppermute | solution.py:270
  62.5 1.0 %shard_map.53._ = f32[8,64,256]{2,1,0:T(8,128)} custom-call(f32[8,32,128]{2,1,0:T(8,128)S(1)} %shard_map.52.own, f32[8,32,128]{2,1,0:T(8,128)S(1)} %collective-permute-done.13.from_y), custom_call_target="tpu_custom_call" | custom-call | tf_op jit(solution)/shard_map/pallas_call | solution.py:24
  63.5 1.9 %collective-permute-done.8.from_y = f32[8,32,128]{2,1,0:T(8,128)S(1)} collective-permute-done((f32[8,32,128]{2,1,0:T(8,128)S(1)}, f32[8,32,128]{2,1,0:T(8,128)S(1)}, u32[]{:S(2)}, u32[]{:S(2)}) %collective-permute-start.8) | collective-permute-done | bytes 131104 | tf_op jit(solution)/shard_map/ppermute | solution.py:270
  65.4 1.0 %shard_map.54 = f32[8,64,256]{2,1,0:T(8,128)} custom-call(f32[8,32,128]{2,1,0:T(8,128)S(1)} %shard_map.49.own, f32[8,32,128]{2,1,0:T(8,128)S(1)} %collective-permute-done.8.from_y, f32[8,64,256]{2,1,0:T(8,128)} %shard_map.53._), custom_call_target="tpu_custom_call", output_to_operand_aliasing={{}: (2, {})} | custom-call | tf_op jit(solution)/shard_map/pallas_call | solution.py:24
  (2 shorter events, 0.0 us)
Async XLA Ops:
  0.6 15.7 %collective-permute-start.1 = (f32[8,64,256]{2,1,0:T(8,128)}, f32[8,64,256]{2,1,0:T(8,128)S(1)}, u32[]{:S(2)}, u32[]{:S(2)}) collective-permute-start(f32[8,64,256]{2,1,0:T(8,128)} %first.1), channel_id=1, source_target_pairs={{0,248},{8,16},{16,8},{24,32},{32,24},{40,48},{48,40},{56,64},{64,... | collective-permute-start | bytes 1572872 | tf_op jit(solution)/shard_map/ppermute | solution.py:277
  3.3 13.0 %collective-permute-start = (f32[8,64,256]{2,1,0:T(8,128)}, f32[8,64,256]{2,1,0:T(8,128)S(1)}, u32[]{:S(2)}, u32[]{:S(2)}) collective-permute-start(f32[8,64,256]{2,1,0:T(8,128)} %first.1), channel_id=1, source_target_pairs={{0,8},{8,0},{16,24},{24,16},{32,40},{40,32},{48,56},{56,48},{64,72... | collective-permute-start | bytes 1572872 | tf_op jit(solution)/shard_map/ppermute | solution.py:278
  8.4 1.0 %copy-start = (f32[8,64,256]{2,1,0:T(8,128)S(1)}, f32[8,64,256]{2,1,0:T(8,128)}, u32[]{:S(2)}) copy-start(f32[8,64,256]{2,1,0:T(8,128)} %second.1) | copy-start | bytes 1572868
  9.5 1.0 %copy-start.1 = (f32[8,64,256]{2,1,0:T(8,128)S(1)}, f32[8,64,256]{2,1,0:T(8,128)}, u32[]{:S(2)}) copy-start(f32[8,64,256]{2,1,0:T(8,128)} %first.1) | copy-start | bytes 1572868
  16.5 10.1 %collective-permute-start.3 = (f32[8,24,256]{2,1,0:T(8,128)S(1)}, f32[8,24,256]{2,1,0:T(8,128)S(1)}, u32[]{:S(2)}, u32[]{:S(2)}) collective-permute-start(f32[8,24,256]{2,1,0:T(8,128)S(1)} %get-tuple-element.18.edge_near), channel_id=1, source_target_pairs={{0,1},{1,0},{2,3},{3,2},{4,5},{5,4},{6,7},{7,6},{8,9},{9,8},{10,11... | collective-permute-start | bytes 589832 | tf_op jit(solution)/shard_map/ppermute | solution.py:284
  20.3 12.1 %collective-permute-start.2 = (f32[8,24,256]{2,1,0:T(8,128)S(1)}, f32[8,24,256]{2,1,0:T(8,128)S(1)}, u32[]{:S(2)}, u32[]{:S(2)}) collective-permute-start(f32[8,24,256]{2,1,0:T(8,128)S(1)} %get-tuple-element.19.edge_far), channel_id=1, source_target_pairs={{0,7},{1,2},{2,1},{3,4},{4,3},{5,6},{6,5},{7,0},{8,15},{9,10},{10,... | collective-permute-start | bytes 589832 | tf_op jit(solution)/shard_map/ppermute | solution.py:283
  24.0 11.3 %collective-permute-start.9 = (f32[8,32,128]{2,1,0:T(8,128)S(1)}, f32[8,32,128]{2,1,0:T(8,128)S(1)}, u32[]{:S(2)}, u32[]{:S(2)}) collective-permute-start(f32[8,32,128]{2,1,0:T(8,128)S(1)} %get-tuple-element.29), channel_id=1, source_target_pairs={{0,7},{1,6},{2,5},{3,4},{4,3},{5,2},{6,1},{7,0},{8,15},{9,14},{10,... | collective-permute-start | bytes 393224 | tf_op jit(solution)/shard_map/ppermute | solution.py:265
  33.0 9.3 %collective-permute-start.4 = (f32[8,32,128]{2,1,0:T(8,128)S(1)}, f32[8,32,128]{2,1,0:T(8,128)S(1)}, u32[]{:S(2)}, u32[]{:S(2)}) collective-permute-start(f32[8,32,128]{2,1,0:T(8,128)S(1)} %get-tuple-element.27), channel_id=1, source_target_pairs={{0,7},{1,6},{2,5},{3,4},{4,3},{5,2},{6,1},{7,0},{8,15},{9,14},{10,... | collective-permute-start | bytes 393224 | tf_op jit(solution)/shard_map/ppermute | solution.py:265
  35.3 11.7 %collective-permute-start.10 = (f32[8,32,128]{2,1,0:T(8,128)S(1)}, f32[8,32,128]{2,1,0:T(8,128)S(1)}, u32[]{:S(2)}, u32[]{:S(2)}) collective-permute-start(f32[8,32,128]{2,1,0:T(8,128)S(1)} %shard_map.50.own), channel_id=1, source_target_pairs={{0,248},{8,240},{16,232},{24,224},{32,216},{40,208},{48,200},{56,1... | collective-permute-start | bytes 393224 | tf_op jit(solution)/shard_map/ppermute | solution.py:266
  42.4 8.0 %collective-permute-start.5 = (f32[8,32,128]{2,1,0:T(8,128)S(1)}, f32[8,32,128]{2,1,0:T(8,128)S(1)}, u32[]{:S(2)}, u32[]{:S(2)}) collective-permute-start(f32[8,32,128]{2,1,0:T(8,128)S(1)} %shard_map.47.own), channel_id=1, source_target_pairs={{0,248},{8,240},{16,232},{24,224},{32,216},{40,208},{48,200},{56,1... | collective-permute-start | bytes 393224 | tf_op jit(solution)/shard_map/ppermute | solution.py:266
  47.0 6.3 %collective-permute-start.12 = (f32[8,32,128]{2,1,0:T(8,128)S(1)}, f32[8,32,128]{2,1,0:T(8,128)S(1)}, u32[]{:S(2)}, u32[]{:S(2)}) collective-permute-start(f32[8,32,128]{2,1,0:T(8,128)S(1)} %shard_map.51.own), channel_id=1, source_target_pairs={{8,16},{16,8},{24,32},{32,24},{40,48},{48,40},{56,64},{64,56},{72,... | collective-permute-start | bytes 393224 | tf_op jit(solution)/shard_map/ppermute | solution.py:267
  49.0 4.4 %collective-permute-start.11 = (f32[8,32,128]{2,1,0:T(8,128)S(1)}, f32[8,32,128]{2,1,0:T(8,128)S(1)}, u32[]{:S(2)}, u32[]{:S(2)}) collective-permute-start(f32[8,32,128]{2,1,0:T(8,128)S(1)} %shard_map.51.own), channel_id=1, source_target_pairs={{0,8},{8,0},{16,24},{24,16},{32,40},{40,32},{48,56},{56,48},{64,72... | collective-permute-start | bytes 393224 | tf_op jit(solution)/shard_map/ppermute | solution.py:268
  50.5 6.3 %collective-permute-start.7 = (f32[8,32,128]{2,1,0:T(8,128)S(1)}, f32[8,32,128]{2,1,0:T(8,128)S(1)}, u32[]{:S(2)}, u32[]{:S(2)}) collective-permute-start(f32[8,32,128]{2,1,0:T(8,128)S(1)} %shard_map.48.own), channel_id=1, source_target_pairs={{8,16},{16,8},{24,32},{32,24},{40,48},{48,40},{56,64},{64,56},{72,... | collective-permute-start | bytes 393224 | tf_op jit(solution)/shard_map/ppermute | solution.py:267
  52.8 4.0 %collective-permute-start.6 = (f32[8,32,128]{2,1,0:T(8,128)S(1)}, f32[8,32,128]{2,1,0:T(8,128)S(1)}, u32[]{:S(2)}, u32[]{:S(2)}) collective-permute-start(f32[8,32,128]{2,1,0:T(8,128)S(1)} %shard_map.48.own), channel_id=1, source_target_pairs={{0,8},{8,0},{16,24},{24,16},{32,40},{40,32},{48,56},{56,48},{64,72... | collective-permute-start | bytes 393224 | tf_op jit(solution)/shard_map/ppermute | solution.py:268
  53.4 9.0 %collective-permute-start.13 = (f32[8,32,128]{2,1,0:T(8,128)S(1)}, f32[8,32,128]{2,1,0:T(8,128)S(1)}, u32[]{:S(2)}, u32[]{:S(2)}) collective-permute-start(f32[8,32,128]{2,1,0:T(8,128)S(1)} %shard_map.52.own), channel_id=1, source_target_pairs={{0,7},{1,6},{2,5},{3,4},{4,3},{5,2},{6,1},{7,0},{8,15},{9,14},{10,... | collective-permute-start | bytes 393224 | tf_op jit(solution)/shard_map/ppermute | solution.py:270
  56.9 8.6 %collective-permute-start.8 = (f32[8,32,128]{2,1,0:T(8,128)S(1)}, f32[8,32,128]{2,1,0:T(8,128)S(1)}, u32[]{:S(2)}, u32[]{:S(2)}) collective-permute-start(f32[8,32,128]{2,1,0:T(8,128)S(1)} %shard_map.49.own), channel_id=1, source_target_pairs={{0,7},{1,6},{2,5},{3,4},{4,3},{5,2},{6,1},{7,0},{8,15},{9,14},{10,... | collective-permute-start | bytes 393224 | tf_op jit(solution)/shard_map/ppermute | solution.py:270
